TPU v7x, 32 devices: a whole 2x2x4 slice. The times are simulated.
32 devices in a mesh: groups: 2 (over y), rows: 4 (over z), cols: 4 (over x, core).
Axes of the slice: x: 2, y: 2, z: 4, core: 2. Of those that a mesh axis runs over, the one named last changes fastest.
Arguments:
- query: bfloat16 [128, 24, 1024], P(('groups', 'rows'), None, 'cols'), parts along dimension 0, may hold values from -8 to 8, as said below
- keys: bfloat16 [128, 24, 1024], P(('groups', 'rows'), None, 'cols'), parts along dimension 0, may hold values from -4 to 4, as said below
- values: bfloat16 [128, 24, 1024], P(('groups', 'rows'), None, 'cols'), parts along dimension 0, may hold values from -6 to 6
- registers: bfloat16 [2, 64, 1024], P(None, 'rows', 'cols'), may hold values from -6 to 6
- cotangent: bfloat16 [128, 24, 1024], P(('groups', 'rows'), None, 'cols'), parts along dimension 0, may hold values from -6 to 6
Outputs:
- attended: bfloat16 [128, 24, 1024], P(('groups', 'rows'), None, 'cols'), parts along dimension 0
- grad_query: bfloat16 [128, 24, 1024], P(('groups', 'rows'), None, 'cols'), parts along dimension 0
- grad_keys: bfloat16 [128, 24, 1024], P(('groups', 'rows'), None, 'cols'), parts along dimension 0
- grad_values: bfloat16 [128, 24, 1024], P(('groups', 'rows'), None, 'cols'), parts along dimension 0
- grad_registers: float32 [4, 64, 1024], P('groups', 'rows', 'cols'), parts along dimension 0
There are 2 independent parts, one for each index of `groups`. A program takes and returns all parts, laid end to end along the dimension named above; an argument that names none is the same for every part. Nothing has to cross between parts.
Inputs may be any that keep to these rules, and one draw needn't show every extreme that they name: `query`: queries of order one; a few reach larger magnitudes. keys of order one.
All inputs are finite; a program needn't handle non-finite values.
Results may differ from a plain program's by a relative error of at most 0.0073.
Values may be sent and summed in bfloat16 or wider, within the bound.
No kernel may reach another device: no remote copies, remote signals or barrier semaphores. Data moves between devices by JAX's collectives and lax.ppermute only.
A program may use at most 128 MiB of HBM per device.

v0:
```python
import jax
import jax.numpy as jnp
from jax import lax
from jax.sharding import PartitionSpec as P

HEAD = 64
TILE = 8


def padded(array, sides, width):
    for axis, dim in sides:
        count, length = (lax.axis_size(axis), array.shape[dim])
        up = [(i, (i + 1) % count) for i in range(count - 1)]
        down = [(j, i) for i, j in up]
        last = lax.slice_in_dim(array, length - width, length, axis=dim)
        initial = lax.slice_in_dim(array, 0, width, axis=dim)
        before = lax.ppermute(last, axis, up)
        after = lax.ppermute(initial, axis, down)
        array = jnp.concatenate([before, array, after], axis=dim)
    return array


def passed_along(array, axis, by):
    count = lax.axis_size(axis)
    pairs = [(i, i + by) for i in range(count) if 0 <= i + by < count]
    return lax.ppermute(array, axis, pairs)


def to_tiles(field, head_count):
    row_count = field.shape[0] // TILE
    tile_cols = field.shape[1] // TILE
    shaped = field.reshape(row_count, TILE, tile_cols, TILE, head_count, HEAD)
    return jnp.transpose(shaped, (4, 0, 2, 1, 3, 5)).reshape(
        head_count, row_count, tile_cols, TILE * TILE, HEAD
    )


def from_tiles(tiled):
    head_count, row_count, tile_cols = (tiled.shape[0], tiled.shape[1], tiled.shape[2])
    shaped = tiled.reshape(head_count, row_count, tile_cols, TILE, TILE, HEAD)
    return jnp.transpose(shaped, (1, 3, 2, 4, 0, 5)).reshape(
        row_count * TILE, tile_cols * TILE, head_count * HEAD
    )


def sweep(
    query_rows,
    grad_rows,
    key_rows,
    value_rows,
    reg_keys,
    reg_values,
    first_row,
    total_rows,
    own_low,
    own_high,
):
    feature = query_rows.shape[2]
    head_count = feature // HEAD
    tile_cols = query_rows.shape[1] // TILE
    query_count = query_rows.shape[0] // TILE
    patch_count = TILE * TILE
    local_count = 9 * patch_count
    factor = HEAD ** (-0.5)
    flat = jnp.float32
    col_margin = ((0, 0), (0, 0), (1, 1), (0, 0), (0, 0))
    q_tiles = to_tiles(query_rows, head_count)
    g_tiles = to_tiles(grad_rows, head_count)
    k_tiles = jnp.pad(to_tiles(key_rows, head_count), col_margin)
    v_tiles = jnp.pad(to_tiles(value_rows, head_count), col_margin)
    reg_k = jnp.transpose(reg_keys.reshape(-1, head_count, HEAD), (1, 0, 2))
    reg_v = jnp.transpose(reg_values.reshape(-1, head_count, HEAD), (1, 0, 2))
    col_at = (
        jnp.arange(tile_cols, dtype=jnp.int32)[:, None]
        + jnp.arange(3, dtype=jnp.int32)[None, :]
        - 1
    )
    col_valid = (col_at >= 0) & (col_at < tile_cols)
    start_state = (
        jnp.zeros(k_tiles.shape, flat),
        jnp.zeros(k_tiles.shape, flat),
        jnp.zeros(reg_k.shape, flat),
        jnp.zeros(reg_k.shape, flat),
    )

    def gather_near(window):
        return jnp.concatenate(
            [
                window[:, above, across : across + tile_cols]
                for above in range(3)
                for across in range(3)
            ],
            axis=2,
        )

    def spread_near(near):
        rows_out = []
        for above in range(3):
            total = jnp.zeros((head_count, tile_cols + 2, patch_count, HEAD), flat)
            for across in range(3):
                block = (above * 3 + across) * patch_count
                piece = near[:, :, block : block + patch_count]
                total = total + jnp.pad(piece, ((0, 0), (across, 2 - across), (0, 0), (0, 0)))
            rows_out.append(total)
        return jnp.stack(rows_out, axis=1)

    def advance(state_in, row_idx):
        acc_keys, acc_values, acc_reg_k, acc_reg_v = state_in
        queries = lax.dynamic_index_in_dim(q_tiles, row_idx, 1, keepdims=False)
        grads_in = lax.dynamic_index_in_dim(g_tiles, row_idx, 1, keepdims=False)
        near_keys = gather_near(lax.dynamic_slice_in_dim(k_tiles, row_idx, 3, 1))
        near_values = gather_near(lax.dynamic_slice_in_dim(v_tiles, row_idx, 3, 1))
        tile_at = first_row + row_idx - 1 + jnp.arange(3, dtype=jnp.int32)
        row_valid = (tile_at >= 0) & (tile_at < total_rows)
        valid_nine = (row_valid[None, :, None] & col_valid[:, None, :]).reshape(tile_cols, 9)
        allowed = jnp.repeat(valid_nine, patch_count, axis=1)[None, :, None, :]
        scores = (
            jnp.einsum("hcqd,hckd->hcqk", queries, near_keys, preferred_element_type=flat) * factor
        )
        scores = jnp.where(allowed, scores, -1e30)
        reg_scores = (
            jnp.einsum("hcqd,hgd->hcqg", queries, reg_k, preferred_element_type=flat) * factor
        )
        all_scores = jnp.concatenate([scores, reg_scores], axis=-1)
        row_max = jnp.max(all_scores, axis=-1, keepdims=True)
        exp_scores = jnp.exp(all_scores - row_max)
        probs = exp_scores / jnp.sum(exp_scores, axis=-1, keepdims=True)
        weights = probs.astype(jnp.bfloat16)
        local_weights = weights[..., :local_count]
        reg_weights = weights[..., local_count:]
        mixed = jnp.einsum(
            "hcqk,hckd->hcqd", local_weights, near_values, preferred_element_type=flat
        )
        mixed = mixed + jnp.einsum(
            "hcqg,hgd->hcqd", reg_weights, reg_v, preferred_element_type=flat
        )
        result = mixed.astype(jnp.bfloat16)
        d_local = jnp.einsum("hcqd,hckd->hcqk", grads_in, near_values, preferred_element_type=flat)
        d_reg = jnp.einsum("hcqd,hgd->hcqg", grads_in, reg_v, preferred_element_type=flat)
        d_weights = jnp.concatenate([d_local, d_reg], axis=-1).astype(jnp.bfloat16)
        d_wide = lax.optimization_barrier(d_weights).astype(flat)
        row_dot = jnp.sum(probs * d_wide, axis=-1, keepdims=True)
        d_scores = (probs * (d_wide - row_dot)).astype(jnp.bfloat16)
        ds_local = d_scores[..., :local_count]
        ds_reg = d_scores[..., local_count:]
        grad_q = jnp.einsum("hcqk,hckd->hcqd", ds_local, near_keys, preferred_element_type=flat)
        grad_q = (
            grad_q + jnp.einsum("hcqg,hgd->hcqd", ds_reg, reg_k, preferred_element_type=flat)
        ) * factor
        grad_near_k = (
            jnp.einsum("hcqk,hcqd->hckd", ds_local, queries, preferred_element_type=flat) * factor
        )
        grad_near_v = jnp.einsum(
            "hcqk,hcqd->hckd", local_weights, grads_in, preferred_element_type=flat
        )
        grad_rk = (
            jnp.einsum("hcqg,hcqd->hgd", ds_reg, queries, preferred_element_type=flat) * factor
        )
        grad_rv = jnp.einsum("hcqg,hcqd->hgd", reg_weights, grads_in, preferred_element_type=flat)
        acc_keys = lax.dynamic_update_slice_in_dim(
            acc_keys,
            lax.dynamic_slice_in_dim(acc_keys, row_idx, 3, 1) + spread_near(grad_near_k),
            row_idx,
            1,
        )
        acc_values = lax.dynamic_update_slice_in_dim(
            acc_values,
            lax.dynamic_slice_in_dim(acc_values, row_idx, 3, 1) + spread_near(grad_near_v),
            row_idx,
            1,
        )
        inside = ((row_idx >= own_low) & (row_idx < own_high)).astype(flat)
        acc_reg_k = acc_reg_k + inside * grad_rk
        acc_reg_v = acc_reg_v + inside * grad_rv
        return ((acc_keys, acc_values, acc_reg_k, acc_reg_v), (result, grad_q))

    final_state, outputs = lax.scan(advance, start_state, jnp.arange(query_count, dtype=jnp.int32))
    results, grads_q = outputs
    acc_keys, acc_values, acc_reg_k, acc_reg_v = final_state
    results = from_tiles(jnp.moveaxis(results, 0, 1))
    grads_q = from_tiles(jnp.moveaxis(grads_q, 0, 1))
    keys_out = from_tiles(acc_keys[:, :, 1:-1])
    values_out = from_tiles(acc_values[:, :, 1:-1])
    reg_k_out = jnp.transpose(acc_reg_k, (1, 0, 2)).reshape(-1, feature)
    reg_v_out = jnp.transpose(acc_reg_v, (1, 0, 2)).reshape(-1, feature)
    return (results, grads_q, keys_out, values_out, reg_k_out, reg_v_out)


def shards(query, keys, values, registers, cotangent):
    tile_rows = query.shape[0] // TILE
    total_rows = tile_rows * lax.axis_size("rows")
    first_row = lax.axis_index("rows") * tile_rows
    reg_both = lax.all_gather(registers, "rows", axis=1, tiled=True)
    reg_keys = reg_both[0]
    reg_values = reg_both[1]
    both_sides = padded(jnp.stack([keys, values]), (("rows", 1),), TILE)
    attended, grad_query, acc_keys, acc_values, grad_rk, grad_rv = sweep(
        query,
        cotangent,
        both_sides[0],
        both_sides[1],
        reg_keys,
        reg_values,
        first_row,
        total_rows,
        0,
        tile_rows,
    )
    from_below = passed_along(
        jnp.stack([acc_keys[:TILE], acc_values[:TILE]]).astype(jnp.bfloat16), "rows", -1
    ).astype(jnp.float32)
    from_above = passed_along(jnp.stack([acc_keys[-TILE:], acc_values[-TILE:]]), "rows", 1)
    grad_keys = acc_keys[TILE:-TILE].at[:TILE].add(from_above[0]).at[-TILE:].add(from_below[0])
    grad_values = acc_values[TILE:-TILE].at[:TILE].add(from_above[1]).at[-TILE:].add(from_below[1])
    grad_registers = lax.psum_scatter(
        jnp.stack([grad_rk, grad_rv]), "rows", scatter_dimension=1, tiled=True
    )
    return (
        attended,
        grad_query.astype(jnp.bfloat16),
        grad_keys.astype(jnp.bfloat16),
        grad_values.astype(jnp.bfloat16),
        grad_registers,
    )


def solution(mesh):
    in_specs = (
        P(("groups", "rows"), None, "cols"),
        P(("groups", "rows"), None, "cols"),
        P(("groups", "rows"), None, "cols"),
        P(None, "rows", "cols"),
        P(("groups", "rows"), None, "cols"),
    )
    out_specs = (
        P(("groups", "rows"), None, "cols"),
        P(("groups", "rows"), None, "cols"),
        P(("groups", "rows"), None, "cols"),
        P(("groups", "rows"), None, "cols"),
        P("groups", "rows", "cols"),
    )
    return jax.shard_map(shards, mesh=mesh, in_specs=in_specs, out_specs=out_specs, check_vma=False)
```

profile of v0, /device:TPU:0, one launch (start us, length us, event | category | flops | bytes accessed | tf_op | source)
XLA Modules:
  0.0 241.9 jit_solution(16138694085985145654)
XLA Ops:
  8.4 4.9 %collective-permute-start = (bf16[2,8,24,256]{3,2,1,0:T(8,128)(2,1)S(1)}, bf16[2,8,24,256]{3,2,1,0:T(8,128)(2,1)S(1)}, u32[]{:S(2)}, u32[]{:S(2)}) collective-permute-start(bf16[2,8,24,256]{3,2,1,0:T(8,128)(2,1)S(1)} %get-tuple-element.424), channel_id=1, source_target_pairs={{0,4},{4,8},{8,12},{1,5},{5,9},{9,13},{2,6},{6,10},{10,14},{3,7},{... | collective-permute-start | bytes 589832 | tf_op jit(solution)/shard_map/ppermute | solution.py:17
  14.7 16.3 %all_gather.3 = bf16[2,64,256]{2,1,0:T(8,128)(2,1)S(1)} all-gather(bf16[2,16,256]{2,1,0:T(8,128)(2,1)} %param.18), channel_id=1, replica_groups=mesh['groups'=2,'rows'=4,'cols'=4] {'rows'}, dimensions={1}, use_global_device_ids=true | all-gather | bytes 81920 | tf_op jit(solution)/shard_map/all_gather | solution.py:193
  36.3 1.4 pad.126
  37.7 1.8 broadcast.182.clone2
  39.6 1.8 broadcast.182.clone
  41.4 153.6 %while.27 = (s32[]{:T(128)}, f32[4,4,5,64,64]{4,3,2,1,0:T(8,128)}, f32[4,4,5,64,64]{4,3,2,1,0:T(8,128)}, f32[4,64,64]{2,1,0:T(8,128)}, f32[4,64,64]{2,1,0:T(8,12...) while((s32[]{:T(128)}, f32[4,4,5,64,64]{4,3,2,1,0:T(8,128)}, ...), condition=%wide.region_5.6_spmd.clone, body=%wide.region_0.5_spmd.clone.sunk | while | flops 393904096 | bytes 103458672 | solution.py:177
  50.3 1.7 copy.145
  52.0 1.7 copy.146
  53.8 1.7 copy.147
  55.5 1.7 copy.148
  58.5 2.3 concatenate.44
  63.3 1.7 copy.133
  65.0 1.7 copy.134
  72.4 2.5 %concatenate.43 = bf16[4,3,576,64]{2,3,1,0:T(8,128)(2,1)S(1)} concatenate(bf16[4,3,64,64]{2,3,1,0:T(8,128)(2,1)S(1)} %bitcast.258, bf16[4,3,64,64]{2,3,1,0:T(8,128)(2,1)S(1)} %bitcast.260, bf16[4,3,64,64]{2,3,1,0:T(8,128)(2,1)} %bitcast.262, bf16[4,3,64,64]{2,3,1,0:T(8,128)(2,1)} %bitcast.264, bf16[4,3,64,64]{2,3,1,0:T(8,128)(2,1)} %bitcast.266, ...), dimensions={2} | concatenate | bytes 1769472 | tf_op jit(solution)/shard_map/while/body/eval_jaxpr/concatenate | solution.py:87
  74.8 3.1 %constant_dynamic-slice_fusion.26 = f32[4,3,5,64,64]{4,3,2,1,0:T(8,128)} fusion(f32[4,4,5,64,64]{4,3,2,1,0:T(8,128)} %get-tuple-element.630, s32[]{:T(128)S(6)} %select_n.32), kind=kLoop, calls=%fused_computation.99.clone.1 | loop fusion | bytes 1966084 | tf_op jit(solution)/shard_map/while/body/eval_jaxpr/dynamic_slice | solution.py:162
  78.0 2.8 %copy.143 = f32[4,3,5,64,64]{3,4,2,0,1:T(8,128)} copy(f32[4,3,5,64,64]{4,3,2,1,0:T(8,128)} %constant_dynamic-slice_fusion.26) | data formatting | bytes 1966080 | tf_op jit(solution)/shard_map/while/body/eval_jaxpr/dynamic_slice | solution.py:162
  80.8 3.0 %constant_dynamic-slice_fusion.24 = f32[4,3,5,64,64]{4,3,2,1,0:T(8,128)} fusion(f32[4,4,5,64,64]{4,3,2,1,0:T(8,128)} %get-tuple-element.631, s32[]{:T(128)S(6)} %select_n.32), kind=kLoop, calls=%fused_computation.93.clone.1 | loop fusion | bytes 1966084 | tf_op jit(solution)/shard_map/while/body/eval_jaxpr/dynamic_slice | solution.py:168
  83.8 2.9 %copy.132 = f32[4,3,5,64,64]{3,4,2,0,1:T(8,128)} copy(f32[4,3,5,64,64]{4,3,2,1,0:T(8,128)} %constant_dynamic-slice_fusion.24) | data formatting | bytes 1966080 | tf_op jit(solution)/shard_map/while/body/eval_jaxpr/dynamic_slice | solution.py:168
  88.4 8.1 %fusion.148 = bf16[4,3,64,640]{3,2,1,0:T(8,128)(2,1)S(1)} fusion(bf16[4,3,64,640]{3,2,1,0:T(8,128)(2,1)S(1)} %copy-done.6, f32[4,3,64]{2,1,0:T(4,128)S(1)} %fusion.144, f32[4,3,64]{2,1,0:T(4,128)S(1)} %reduce_max.33, f32[4,3,64,64]{3,2,1,0:T(8,128)S(1)} %get-tuple-element.563, f32[4,3,64,576]{3,2,1,0:T(8,128)S(1)} %get-tuple-element.573), kind=kOutput, calls=%fused_computation.5.clone.1 | output fusion | flops 5899647 | bytes 3938304 | tf_op jit(solution)/shard_map/while/body/eval_jaxpr/sub | solution.py:143
  103.0 1.3 copy-done.1
  104.4 1.7 maximum_add_fusion.4
  106.0 2.9 %copy.142 = f32[4,3,5,64,64]{4,3,2,1,0:T(8,128)} copy(f32[4,3,5,64,64]{3,4,2,0,1:T(8,128)} %maximum_add_fusion.4) | data formatting | bytes 1966080 | tf_op jit(solution)/shard_map/while/body/eval_jaxpr/dynamic_update_slice | solution.py:166
  109.8 1.3 copy-done
  111.6 1.7 copy.153
  113.3 4.7 %constant_dynamic-update-slice_fusion.3 = (f32[4,4,5,64,64]{4,3,2,1,0:T(8,128)}, f32[4,4,5,64,64]{4,3,2,1,0:T(8,128)}) fusion(f32[4,4,5,64,64]{4,3,2,1,0:T(8,128)} %get-tuple-element.631, f32[4,3,5,64,64]{4,3,2,1,0:T(8,128)} %copy.142, s32[]{:T(128)S(6)} %select_n.32, f32[4,4,5,64,64]{4,3,2,1,0:T(8,128)} %get-tuple-element.630, ...), kind=kLoop, calls=%fused_computation.92.clone.1 | loop fusion | bytes 7864324 | tf_op jit(solution)/shard_map/while/body/eval_jaxpr/dynamic_update_slice | solution.py:166
  127.0 1.7 copy.145
  128.8 1.7 copy.146
  130.5 1.7 copy.147
  132.2 1.7 copy.148
  135.2 2.3 concatenate.44
  140.0 1.7 copy.133
  141.7 1.7 copy.134
  149.1 2.5 %concatenate.43 = bf16[4,3,576,64]{2,3,1,0:T(8,128)(2,1)S(1)} concatenate(bf16[4,3,64,64]{2,3,1,0:T(8,128)(2,1)S(1)} %bitcast.258, bf16[4,3,64,64]{2,3,1,0:T(8,128)(2,1)S(1)} %bitcast.260, bf16[4,3,64,64]{2,3,1,0:T(8,128)(2,1)} %bitcast.262, bf16[4,3,64,64]{2,3,1,0:T(8,128)(2,1)} %bitcast.264, bf16[4,3,64,64]{2,3,1,0:T(8,128)(2,1)} %bitcast.266, ...), dimensions={2} | concatenate | bytes 1769472 | tf_op jit(solution)/shard_map/while/body/eval_jaxpr/concatenate | solution.py:87
  151.6 3.1 %constant_dynamic-slice_fusion.26 = f32[4,3,5,64,64]{4,3,2,1,0:T(8,128)} fusion(f32[4,4,5,64,64]{4,3,2,1,0:T(8,128)} %get-tuple-element.630, s32[]{:T(128)S(6)} %select_n.32), kind=kLoop, calls=%fused_computation.99.clone.1 | loop fusion | bytes 1966084 | tf_op jit(solution)/shard_map/while/body/eval_jaxpr/dynamic_slice | solution.py:162
  154.7 2.8 %copy.143 = f32[4,3,5,64,64]{3,4,2,0,1:T(8,128)} copy(f32[4,3,5,64,64]{4,3,2,1,0:T(8,128)} %constant_dynamic-slice_fusion.26) | data formatting | bytes 1966080 | tf_op jit(solution)/shard_map/while/body/eval_jaxpr/dynamic_slice | solution.py:162
  157.5 3.0 %constant_dynamic-slice_fusion.24 = f32[4,3,5,64,64]{4,3,2,1,0:T(8,128)} fusion(f32[4,4,5,64,64]{4,3,2,1,0:T(8,128)} %get-tuple-element.631, s32[]{:T(128)S(6)} %select_n.32), kind=kLoop, calls=%fused_computation.93.clone.1 | loop fusion | bytes 1966084 | tf_op jit(solution)/shard_map/while/body/eval_jaxpr/dynamic_slice | solution.py:168
  160.6 2.9 %copy.132 = f32[4,3,5,64,64]{3,4,2,0,1:T(8,128)} copy(f32[4,3,5,64,64]{4,3,2,1,0:T(8,128)} %constant_dynamic-slice_fusion.24) | data formatting | bytes 1966080 | tf_op jit(solution)/shard_map/while/body/eval_jaxpr/dynamic_slice | solution.py:168
  165.1 8.1 %fusion.148 = bf16[4,3,64,640]{3,2,1,0:T(8,128)(2,1)S(1)} fusion(bf16[4,3,64,640]{3,2,1,0:T(8,128)(2,1)S(1)} %copy-done.6, f32[4,3,64]{2,1,0:T(4,128)S(1)} %fusion.144, f32[4,3,64]{2,1,0:T(4,128)S(1)} %reduce_max.33, f32[4,3,64,64]{3,2,1,0:T(8,128)S(1)} %get-tuple-element.563, f32[4,3,64,576]{3,2,1,0:T(8,128)S(1)} %get-tuple-element.573), kind=kOutput, calls=%fused_computation.5.clone.1 | output fusion | flops 5899647 | bytes 3938304 | tf_op jit(solution)/shard_map/while/body/eval_jaxpr/sub | solution.py:143
  179.8 1.3 copy-done.1
  181.1 1.7 maximum_add_fusion.4
  182.8 2.9 %copy.142 = f32[4,3,5,64,64]{4,3,2,1,0:T(8,128)} copy(f32[4,3,5,64,64]{3,4,2,0,1:T(8,128)} %maximum_add_fusion.4) | data formatting | bytes 1966080 | tf_op jit(solution)/shard_map/while/body/eval_jaxpr/dynamic_update_slice | solution.py:166
  188.3 1.7 copy.153
  190.0 4.7 %constant_dynamic-update-slice_fusion.3 = (f32[4,4,5,64,64]{4,3,2,1,0:T(8,128)}, f32[4,4,5,64,64]{4,3,2,1,0:T(8,128)}) fusion(f32[4,4,5,64,64]{4,3,2,1,0:T(8,128)} %get-tuple-element.631, f32[4,3,5,64,64]{4,3,2,1,0:T(8,128)} %copy.142, s32[]{:T(128)S(6)} %select_n.32, f32[4,4,5,64,64]{4,3,2,1,0:T(8,128)} %get-tuple-element.630, ...), kind=kLoop, calls=%fused_computation.92.clone.1 | loop fusion | bytes 7864324 | tf_op jit(solution)/shard_map/while/body/eval_jaxpr/dynamic_update_slice | solution.py:166
  195.0 1.5 slice_bitcast_fusion.1
  203.1 1.8 pad_maximum_fusion.2
  204.9 2.6 %collective-permute-start.2 = (f32[2,8,24,256]{3,2,1,0:T(8,128)}, f32[2,8,24,256]{3,2,1,0:T(8,128)}, u32[]{:S(2)}, u32[]{:S(2)}) collective-permute-start(f32[2,8,24,256]{3,2,1,0:T(8,128)} %pad_maximum_fusion.2), channel_id=1, source_target_pairs={{0,4},{4,8},{8,12},{1,5},{5,9},{9,13},{2,6},{6,10},{10,14},{3,7},{... | collective-permute-start | bytes 1179656 | tf_op jit(solution)/shard_map/ppermute | solution.py:26
  209.8 1.4 collective-permute-start.3
  221.6 13.5 %reduce-scatter.2.cloned.1.call-done = f32[2,16,256]{2,1,0:T(8,128)} async-done(((f32[2,64,256]{2,1,0:T(8,128)}), f32[2,16,256]{2,1,0:T(8,128)}) %reduce-scatter.2.cloned.1.call-update) | async-done | bytes 32784 | tf_op jit(solution)/shard_map/reduce_scatter | solution.py:215
  (273 shorter events, 72.6 us)
Async XLA Ops:
  7.2 25.3 %copy-start.34 = (bf16[16,24,256]{2,1,0:T(8,128)(2,1)S(1)}, bf16[16,24,256]{2,1,0:T(8,128)(2,1)}, u32[]{:S(2)}) copy-start(bf16[16,24,256]{2,1,0:T(8,128)(2,1)} %param.19) | copy-start | bytes 589828
  7.2 227.9 %reduce-scatter.2.cloned.1.call-start = ((), (), s32[]{:S(2)}) async-start(), calls=%async_computation.1 | async-start | bytes 163840 | tf_op jit(solution)/shard_map/reduce_scatter | solution.py:215
  7.2 25.6 %copy-start.26 = (bf16[16,24,256]{2,1,0:T(8,128)(2,1)S(1)}, bf16[16,24,256]{2,1,0:T(8,128)(2,1)}, u32[]{:S(2)}) copy-start(bf16[16,24,256]{2,1,0:T(8,128)(2,1)} %param.16) | copy-start | bytes 589828
  7.2 25.6 %copy-start.27 = (bf16[16,24,256]{2,1,0:T(8,128)(2,1)S(1)}, bf16[16,24,256]{2,1,0:T(8,128)(2,1)}, u32[]{:S(2)}) copy-start(bf16[16,24,256]{2,1,0:T(8,128)(2,1)} %param.17) | copy-start | bytes 589828
  8.4 24.5 %collective-permute-start = (bf16[2,8,24,256]{3,2,1,0:T(8,128)(2,1)S(1)}, bf16[2,8,24,256]{3,2,1,0:T(8,128)(2,1)S(1)}, u32[]{:S(2)}, u32[]{:S(2)}) collective-permute-start(bf16[2,8,24,256]{3,2,1,0:T(8,128)(2,1)S(1)} %get-tuple-element.424), channel_id=1, source_target_pairs={{0,4},{4,8},{8,12},{1,5},{5,9},{9,13},{2,6},{6,10},{10,14},{3,7},{... | collective-permute-start | bytes 589832 | tf_op jit(solution)/shard_map/ppermute | solution.py:17
  13.3 19.5 %collective-permute-start.1 = (bf16[2,8,24,256]{3,2,1,0:T(8,128)(2,1)S(1)}, bf16[2,8,24,256]{3,2,1,0:T(8,128)(2,1)S(1)}, u32[]{:S(2)}, u32[]{:S(2)}) collective-permute-start(bf16[2,8,24,256]{3,2,1,0:T(8,128)(2,1)S(1)} %get-tuple-element.425), channel_id=1, source_target_pairs={{4,0},{8,4},{12,8},{5,1},{9,5},{13,9},{6,2},{10,6},{14,10},{7,3},{... | collective-permute-start | bytes 589832 | tf_op jit(solution)/shard_map/ppermute | solution.py:18
  41.4 6.9 %copy-start.9 = (bf16[4,64,64]{2,1,0:T(8,128)(2,1)}, bf16[4,64,64]{2,1,0:T(8,128)(2,1)S(1)}, u32[]{:S(2)}) copy-start(bf16[4,64,64]{2,1,0:T(8,128)(2,1)S(1)} %get-tuple-element.667) | copy-start | bytes 98308 | tf_op jit(solution)/shard_map/while
  41.4 6.9 %copy-start.11 = (bf16[4,64,64]{2,1,0:T(8,128)(2,1)}, bf16[4,64,64]{2,1,0:T(8,128)(2,1)S(1)}, u32[]{:S(2)}) copy-start(bf16[4,64,64]{2,1,0:T(8,128)(2,1)S(1)} %get-tuple-element.664) | copy-start | bytes 98308 | tf_op jit(solution)/shard_map/while
  41.4 7.9 %copy-start.2 = (bf16[4,4,5,64,64]{4,3,2,1,0:T(8,128)(2,1)}, bf16[4,4,5,64,64]{4,3,2,1,0:T(8,128)(2,1)S(1)}, u32[]{:S(2)}) copy-start(bf16[4,4,5,64,64]{4,3,2,1,0:T(8,128)(2,1)S(1)} %get-tuple-element.666) | copy-start | bytes 1966084 | tf_op jit(solution)/shard_map/while
  60.8 1.5 copy-start.4
  67.5 4.8 %copy-start.7 = (bf16[4,1,3,64,64]{3,4,2,0,1:T(8,128)(2,1)S(1)}, bf16[4,1,3,64,64]{3,4,2,0,1:T(8,128)(2,1)}, u32[]{:S(2)}) copy-start(bf16[4,1,3,64,64]{3,4,2,0,1:T(8,128)(2,1)} %copy.133) | copy-start | bytes 294916 | tf_op jit(solution)/shard_map/while
  68.3 4.0 %copy-start.8 = (bf16[4,1,3,64,64]{3,4,2,0,1:T(8,128)(2,1)S(1)}, bf16[4,1,3,64,64]{3,4,2,0,1:T(8,128)(2,1)}, u32[]{:S(2)}) copy-start(bf16[4,1,3,64,64]{3,4,2,0,1:T(8,128)(2,1)} %copy.134) | copy-start | bytes 294916 | tf_op jit(solution)/shard_map/while
  97.5 1.7 copy-start.31
  97.5 2.9 %copy-start.17 = (f32[4,64,64]{2,1,0:T(8,128)S(1)}, f32[4,64,64]{2,1,0:T(8,128)}, u32[]{:S(2)}) copy-start(f32[4,64,64]{2,1,0:T(8,128)} %get-tuple-element.633) | copy-start | bytes 196612 | tf_op jit(solution)/shard_map/while
  97.5 3.3 %copy-start.20 = (f32[4,64,64]{2,1,0:T(8,128)S(1)}, f32[4,64,64]{2,1,0:T(8,128)}, u32[]{:S(2)}) copy-start(f32[4,64,64]{2,1,0:T(8,128)} %get-tuple-element.632) | copy-start | bytes 196612 | tf_op jit(solution)/shard_map/while
  99.1 2.5 %copy-start.29 = (bf16[2,4,3,64,64]{4,3,2,1,0:T(8,128)(2,1)}, bf16[2,4,3,64,64]{4,3,2,1,0:T(8,128)(2,1)S(1)}, u32[]{:S(2)}) copy-start(bf16[2,4,3,64,64]{4,3,2,1,0:T(8,128)(2,1)S(1)} %fusion.155) | copy-start | bytes 589828 | tf_op jit(solution)/shard_map/while
  102.8 1.5 copy-start.1
  109.6 1.5 copy-start
  113.3 4.7 %copy-start.3 = (bf16[4,4,5,64,64]{4,3,2,1,0:T(8,128)(2,1)S(1)}, bf16[4,4,5,64,64]{4,3,2,1,0:T(8,128)(2,1)}, u32[]{:S(2)}) copy-start(bf16[4,4,5,64,64]{4,3,2,1,0:T(8,128)(2,1)} %copy-done.2) | copy-start | bytes 1966084 | tf_op jit(solution)/shard_map/while
  113.3 4.7 %copy-start.10 = (bf16[4,64,64]{2,1,0:T(8,128)(2,1)S(1)}, bf16[4,64,64]{2,1,0:T(8,128)(2,1)}, u32[]{:S(2)}) copy-start(bf16[4,64,64]{2,1,0:T(8,128)(2,1)} %copy-done.9) | copy-start | bytes 98308 | tf_op jit(solution)/shard_map/while
  113.3 4.7 %copy-start.12 = (bf16[4,64,64]{2,1,0:T(8,128)(2,1)S(1)}, bf16[4,64,64]{2,1,0:T(8,128)(2,1)}, u32[]{:S(2)}) copy-start(bf16[4,64,64]{2,1,0:T(8,128)(2,1)} %copy-done.11) | copy-start | bytes 98308 | tf_op jit(solution)/shard_map/while
  118.1 6.9 %copy-start.9 = (bf16[4,64,64]{2,1,0:T(8,128)(2,1)}, bf16[4,64,64]{2,1,0:T(8,128)(2,1)S(1)}, u32[]{:S(2)}) copy-start(bf16[4,64,64]{2,1,0:T(8,128)(2,1)S(1)} %get-tuple-element.667) | copy-start | bytes 98308 | tf_op jit(solution)/shard_map/while
  118.1 6.9 %copy-start.11 = (bf16[4,64,64]{2,1,0:T(8,128)(2,1)}, bf16[4,64,64]{2,1,0:T(8,128)(2,1)S(1)}, u32[]{:S(2)}) copy-start(bf16[4,64,64]{2,1,0:T(8,128)(2,1)S(1)} %get-tuple-element.664) | copy-start | bytes 98308 | tf_op jit(solution)/shard_map/while
  118.1 7.9 %copy-start.2 = (bf16[4,4,5,64,64]{4,3,2,1,0:T(8,128)(2,1)}, bf16[4,4,5,64,64]{4,3,2,1,0:T(8,128)(2,1)S(1)}, u32[]{:S(2)}) copy-start(bf16[4,4,5,64,64]{4,3,2,1,0:T(8,128)(2,1)S(1)} %get-tuple-element.666) | copy-start | bytes 1966084 | tf_op jit(solution)/shard_map/while
  137.5 1.5 copy-start.4
  144.2 4.8 %copy-start.7 = (bf16[4,1,3,64,64]{3,4,2,0,1:T(8,128)(2,1)S(1)}, bf16[4,1,3,64,64]{3,4,2,0,1:T(8,128)(2,1)}, u32[]{:S(2)}) copy-start(bf16[4,1,3,64,64]{3,4,2,0,1:T(8,128)(2,1)} %copy.133) | copy-start | bytes 294916 | tf_op jit(solution)/shard_map/while
  145.1 4.0 %copy-start.8 = (bf16[4,1,3,64,64]{3,4,2,0,1:T(8,128)(2,1)S(1)}, bf16[4,1,3,64,64]{3,4,2,0,1:T(8,128)(2,1)}, u32[]{:S(2)}) copy-start(bf16[4,1,3,64,64]{3,4,2,0,1:T(8,128)(2,1)} %copy.134) | copy-start | bytes 294916 | tf_op jit(solution)/shard_map/while
  174.2 1.7 copy-start.31
  174.2 2.9 %copy-start.17 = (f32[4,64,64]{2,1,0:T(8,128)S(1)}, f32[4,64,64]{2,1,0:T(8,128)}, u32[]{:S(2)}) copy-start(f32[4,64,64]{2,1,0:T(8,128)} %get-tuple-element.633) | copy-start | bytes 196612 | tf_op jit(solution)/shard_map/while
  174.2 3.3 %copy-start.20 = (f32[4,64,64]{2,1,0:T(8,128)S(1)}, f32[4,64,64]{2,1,0:T(8,128)}, u32[]{:S(2)}) copy-start(f32[4,64,64]{2,1,0:T(8,128)} %get-tuple-element.632) | copy-start | bytes 196612 | tf_op jit(solution)/shard_map/while
  175.8 2.5 %copy-start.29 = (bf16[2,4,3,64,64]{4,3,2,1,0:T(8,128)(2,1)}, bf16[2,4,3,64,64]{4,3,2,1,0:T(8,128)(2,1)S(1)}, u32[]{:S(2)}) copy-start(bf16[2,4,3,64,64]{4,3,2,1,0:T(8,128)(2,1)S(1)} %fusion.155) | copy-start | bytes 589828 | tf_op jit(solution)/shard_map/while
  179.5 1.5 copy-start.1
  186.3 1.5 copy-start
  190.0 4.7 %copy-start.3 = (bf16[4,4,5,64,64]{4,3,2,1,0:T(8,128)(2,1)S(1)}, bf16[4,4,5,64,64]{4,3,2,1,0:T(8,128)(2,1)}, u32[]{:S(2)}) copy-start(bf16[4,4,5,64,64]{4,3,2,1,0:T(8,128)(2,1)} %copy-done.2) | copy-start | bytes 1966084 | tf_op jit(solution)/shard_map/while
  190.0 4.7 %copy-start.10 = (bf16[4,64,64]{2,1,0:T(8,128)(2,1)S(1)}, bf16[4,64,64]{2,1,0:T(8,128)(2,1)}, u32[]{:S(2)}) copy-start(bf16[4,64,64]{2,1,0:T(8,128)(2,1)} %copy-done.9) | copy-start | bytes 98308 | tf_op jit(solution)/shard_map/while
  190.0 4.7 %copy-start.12 = (bf16[4,64,64]{2,1,0:T(8,128)(2,1)S(1)}, bf16[4,64,64]{2,1,0:T(8,128)(2,1)}, u32[]{:S(2)}) copy-start(bf16[4,64,64]{2,1,0:T(8,128)(2,1)} %copy-done.11) | copy-start | bytes 98308 | tf_op jit(solution)/shard_map/while
  197.7 2.0 copy-start.5
  201.0 6.4 %copy-start.14 = (f32[4,8,3,8,4,64]{5,3,1,2,0,4:T(8,128)S(1)}, f32[4,8,3,8,4,64]{5,3,1,2,0,4:T(8,128)}, u32[]{:S(2)}) copy-start(f32[4,8,3,8,4,64]{5,3,1,2,0,4:T(8,128)} %copy-done.13) | copy-start | bytes 2359300
  201.8 5.6 %copy-start.16 = (f32[4,8,3,8,4,64]{5,3,1,2,0,4:T(8,128)S(1)}, f32[4,8,3,8,4,64]{5,3,1,2,0,4:T(8,128)}, u32[]{:S(2)}) copy-start(f32[4,8,3,8,4,64]{5,3,1,2,0,4:T(8,128)} %copy-done.15) | copy-start | bytes 2359300
  204.9 14.2 %collective-permute-start.2 = (f32[2,8,24,256]{3,2,1,0:T(8,128)}, f32[2,8,24,256]{3,2,1,0:T(8,128)}, u32[]{:S(2)}, u32[]{:S(2)}) collective-permute-start(f32[2,8,24,256]{3,2,1,0:T(8,128)} %pad_maximum_fusion.2), channel_id=1, source_target_pairs={{0,4},{4,8},{8,12},{1,5},{5,9},{9,13},{2,6},{6,10},{10,14},{3,7},{... | collective-permute-start | bytes 1179656 | tf_op jit(solution)/shard_map/ppermute | solution.py:26
  208.8 2.4 %copy-start.30 = (bf16[2,4,3,64,64]{4,3,2,1,0:T(8,128)(2,1)S(1)}, bf16[2,4,3,64,64]{4,3,2,1,0:T(8,128)(2,1)}, u32[]{:S(2)}) copy-start(bf16[2,4,3,64,64]{4,3,2,1,0:T(8,128)(2,1)} %get-tuple-element.257) | copy-start | bytes 589828
  209.8 2.8 %copy-start.22 = (f32[4,64,64]{2,1,0:T(8,128)S(1)}, f32[4,64,64]{2,1,0:T(8,128)}, u32[]{:S(2)}) copy-start(f32[4,64,64]{2,1,0:T(8,128)} %get-tuple-element.260) | copy-start | bytes 196612
  209.8 8.2 %collective-permute-start.3 = (bf16[2,8,24,256]{3,2,1,0:T(8,128)(2,1)S(1)}, bf16[2,8,24,256]{3,2,1,0:T(8,128)(2,1)}, u32[]{:S(2)}, u32[]{:S(2)}) collective-permute-start(bf16[2,8,24,256]{3,2,1,0:T(8,128)(2,1)S(1)} %pad_maximum_fusion.4), channel_id=1, source_target_pairs={{4,0},{8,4},{12,8},{5,1},{9,5},{13,9},{6,2},{10,6},{14,10},{7,3},{... | collective-permute-start | bytes 589832 | tf_op jit(solution)/shard_map/ppermute | solution.py:26
  211.2 1.5 copy-start.19
  211.2 2.5 %copy-start.33 = (bf16[2,4,3,64,64]{4,3,2,1,0:T(8,128)(2,1)S(1)}, bf16[2,4,3,64,64]{4,3,2,1,0:T(8,128)(2,1)}, u32[]{:S(2)}) copy-start(bf16[2,4,3,64,64]{4,3,2,1,0:T(8,128)(2,1)} %get-tuple-element.256) | copy-start | bytes 589828
  211.3 3.7 %slice-start = ((f32[4,8,3,8,4,64]{5,3,1,2,0,4:T(8,128)}), f32[2,8,3,8,4,64]{5,3,1,2,0,4:T(8,128)S(1)}, s32[]{:S(2)}) async-start(f32[4,8,3,8,4,64]{5,3,1,2,0,4:T(8,128)} %copy-done.13), calls=%async_computation.2 | async-start | bytes 1572864 | tf_op jit(solution)/shard_map/slice | solution.py:213
  213.7 2.3 copy-start.24
  215.5 1.5 slice-start.1
  (14 other events, 16.7 us)
Sparse Core Ops, SparseCore 0:
  213.8 21.1 reduce-scatter.1
where the time goes:
time: 244 us; the launch traced here: 242 us
  local copies, waits for them, and re-layouts  129 us (53%)
  other arithmetic  34.1 us (14%)
  blocking collectives  16.3 us (7%)
  between operations  14.5 us (6%)
  waiting for transfers between devices  13.5 us (6%)
  matrix products  12.6 us (5%)
  loops' own time  11.4 us (5%)
  starting transfers between devices  10.3 us (4%)
    while x116, local copies, waits for them, and re-layouts  43.3 us
    all_gather x1, blocking collectives, shards(): reg_both = lax.all_gather(registers, 'rows', axis=1, tiled=True)  16.3 us
    sub x2, other arithmetic, advance(): d_scores = (probs * (d_wide - row_dot)).astype(jnp.bfloat16)  16.1 us
    dynamic_update_slice x4, local copies, waits for them, and re-layouts, advance(): lax.dynamic_update_slice_in_dim(acc_values, lax.dynamic_slice_in_dim(acc_...  15.2 us
    reduce_scatter x1, waiting for transfers between devices, shards(): lax.psum_scatter(jnp.stack([grad_rk, grad_rv]), 'rows', scatter_dimension...  13.5 us
    dynamic_slice x4, local copies, waits for them, and re-layouts, advance(): lax.dynamic_slice_in_dim(acc_keys, row_idx, 3, 1) + spread_near(grad_near_k)  11.9 us
    dynamic_slice x4, local copies, waits for them, and re-layouts, advance(): lax.dynamic_slice_in_dim(acc_values, row_idx, 3, 1)  11.8 us
    another operation x1, loops' own time, sweep(): lax.scan(advance, start_state, jnp.arange(query_count, dtype=jnp.int32))  11.4 us
  transfers between devices with their start and end apart: 5, of which 1 were waited for; matrix products, arithmetic and copies ran while one was open for 6% of the time, Pallas kernels for 0%

commit v1 on v0

v1 whole, which is shorter than its diff:
```python
import functools

import jax
import jax.numpy as jnp
from jax import lax
from jax.experimental import pallas as pl
from jax.experimental.pallas import tpu as pltpu
from jax.sharding import PartitionSpec as P

HEAD = 64
TILE = 8
PATCH = TILE * TILE
FACTOR = HEAD ** (-0.5)
BF = jnp.bfloat16
F32 = jnp.float32
VMEM = pl.BlockSpec(memory_space=pltpu.VMEM)


def swap(array, pairs):
    return lax.ppermute(array, "rows", pairs)


def pairs_a(count):
    return [(i, i ^ 1) for i in range(count)]


def pairs_b(count):
    return [p for i in range(1, count - 1, 2) for p in ((i, i + 1), (i + 1, i))]


def column_tiles(block, tile_cols):
    feature = block.shape[1]
    wide = block.astype(F32).reshape(-1, tile_cols, TILE, feature)
    return [wide[:, c].reshape(-1, feature) for c in range(tile_cols)]


def patch_order(columns):
    feature = columns[0].shape[1]
    parts = [x.reshape(-1, 1, TILE, feature) for x in columns]
    return jnp.concatenate(parts, axis=1).reshape(-1, feature)


def slots(heads):
    return [0, 2, 1, 3] if heads == 4 else list(range(heads))


def block_diagonal(tile, heads):
    order = slots(heads)
    feature = tile.shape[1]
    lane_head = lax.broadcasted_iota(jnp.int32, tile.shape, 1) // HEAD
    zero = jnp.zeros_like(tile)
    return jnp.concatenate([jnp.where(lane_head == h, tile, zero) for h in order], axis=0)


def from_transposed(out_t, heads):
    if heads == 4:
        first = lax.broadcasted_iota(jnp.int32, (HEAD, 2 * PATCH), 1) < PATCH
        left = jnp.where(first, out_t[:HEAD, : 2 * PATCH], out_t[2 * HEAD : 3 * HEAD, : 2 * PATCH])
        right = jnp.where(first, out_t[HEAD : 2 * HEAD, 2 * PATCH :], out_t[3 * HEAD :, 2 * PATCH :])
        turned = jnp.concatenate([left, right], axis=0).T
        return jnp.concatenate([turned[:PATCH], turned[PATCH:]], axis=1)
    turned = out_t.T
    lane_head = lax.broadcasted_iota(jnp.int32, (PATCH, heads * HEAD), 1) // HEAD
    total = turned[:PATCH]
    for h in range(1, heads):
        total = jnp.where(lane_head == h, turned[h * PATCH : (h + 1) * PATCH], total)
    return total


def dot_nt(a, b):
    return lax.dot_general(a, b, (((1,), (1,)), ((), ())), preferred_element_type=F32)


def dot_nn(a, b):
    return lax.dot_general(a, b, (((1,), (0,)), ((), ())), preferred_element_type=F32)


def prepare_kernel(k_ref, v_ref, reg_ref, a_ref, b_ref):
    even = lax.rem(lax.axis_index("rows"), 2) == 0
    edge = b_ref.shape[0] // 2
    last = k_ref.shape[0] - edge
    for n, ref in enumerate((k_ref, v_ref)):
        top, bottom = ref[:edge], ref[last:]
        a_ref[n * edge : (n + 1) * edge] = jnp.where(even, bottom, top)
        b_ref[n * edge : (n + 1) * edge] = jnp.where(even, top, bottom)
    own = reg_ref.shape[1]
    if a_ref.shape[0] > 2 * edge:
        a_ref[2 * edge : 2 * edge + own] = reg_ref[0]
        a_ref[2 * edge + own :] = reg_ref[1]


def attention_kernel(
    tile_cols,
    q_ref,
    g_ref,
    k_ref,
    v_ref,
    a_ref,
    b_ref,
    *refs,
    split_regs,
):
    if split_regs:
        own_ref, c_ref, e_ref = refs[:3]
        refs = refs[3:]
    else:
        all_ref = refs[0]
        refs = refs[1:]
    o_ref, dq_ref, dk_ref, dv_ref, back_a_ref, back_b_ref, dreg_ref = refs[:7]
    kw_ref, vw_ref, kt_ref, vt_ref, acck_ref, accv_ref, accr_ref = refs[7:]
    feature = q_ref.shape[1]
    heads = feature // HEAD
    line = tile_cols * PATCH
    tile_rows = q_ref.shape[0] // line
    near = 3 * PATCH
    me = lax.axis_index("rows")
    even = lax.rem(me, 2) == 0
    has_top = me > 0
    has_bottom = me < lax.axis_size("rows") - 1

    a_rows = b_ref.shape[0] // 2
    for n, (x_ref, w_ref, t_ref) in enumerate(((k_ref, kw_ref, kt_ref), (v_ref, vw_ref, vt_ref))):
        from_a = a_ref[n * a_rows : (n + 1) * a_rows]
        from_b = b_ref[n * a_rows : (n + 1) * a_rows]
        top = column_tiles(jnp.where(even, from_b, from_a), tile_cols)
        bottom = column_tiles(jnp.where(even, from_a, from_b), tile_cols)
        own = column_tiles(x_ref[...], tile_cols)
        if split_regs:
            cut = own_ref.shape[1]
            base = 2 * a_rows + n * cut
            regs = jnp.concatenate(
                [
                    own_ref[n],
                    a_ref[base : base + cut],
                    c_ref[n],
                    e_ref[n],
                ],
                axis=0,
            )
        else:
            regs = all_ref[n]
        for c in range(tile_cols):
            column = jnp.concatenate([top[c], own[c], bottom[c]], axis=0).astype(BF)
            for t in range(tile_rows):
                window = jnp.concatenate([column[t * PATCH : t * PATCH + near], regs], axis=0)
                w_ref[t, c] = window
                t_ref[t, c] = window.T

    seen = set()

    def add(ref, at, rows, value):
        key = (id(ref), at, rows.start)
        if key in seen:
            ref[at, rows] += value
        else:
            seen.add(key)
            ref[at, rows] = value

    for t in range(tile_rows):
        q_cols = column_tiles(q_ref[t * line : (t + 1) * line], tile_cols)
        g_cols = column_tiles(g_ref[t * line : (t + 1) * line], tile_cols)
        o_cols, dq_cols = [], []
        for c in range(tile_cols):
            q_bd = block_diagonal((q_cols[c] * FACTOR).astype(BF), heads)
            g_bd = block_diagonal(g_cols[c].astype(BF), heads)
            across = [x for x in (c - 1, c, c + 1) if 0 <= x < tile_cols]
            scores, grads = [], []
            for x in across:
                size = kw_ref.shape[2] if x == c else near
                s = dot_nt(kw_ref[t, x, :size], q_bd)
                parts = [s[n * PATCH : (n + 1) * PATCH] for n in range(3)] + [s[near:]]
                if t == 0:
                    parts[0] = jnp.where(has_top, parts[0], -1e30)
                if t == tile_rows - 1:
                    parts[2] = jnp.where(has_bottom, parts[2], -1e30)
                if x != c:
                    parts = parts[:3]
                scores.append(jnp.concatenate(parts, axis=0))
                grads.append(dot_nt(vw_ref[t, x, :size], g_bd).astype(BF).astype(F32))
            top_score = functools.reduce(jnp.maximum, [jnp.max(s, axis=0, keepdims=True) for s in scores])
            exps = [jnp.exp(s - top_score) for s in scores]
            inverse = 1.0 / sum(jnp.sum(e, axis=0, keepdims=True) for e in exps)
            probs = [e * inverse for e in exps]
            row_dot = sum(jnp.sum(p * d, axis=0, keepdims=True) for p, d in zip(probs, grads))
            o_t = dq_t = None
            for x, p, d in zip(across, probs, grads):
                weights = p.astype(BF)
                d_scores = (p * (d - row_dot)).astype(BF)
                dk = dot_nn(d_scores, q_bd)
                dv = dot_nn(weights, g_bd)
                window = slice(t * PATCH, t * PATCH + near)
                for a in range(3):
                    rows = slice((t + a) * PATCH, (t + a + 1) * PATCH)
                    add(acck_ref, x, rows, dk[a * PATCH : (a + 1) * PATCH])
                    add(accv_ref, x, rows, dv[a * PATCH : (a + 1) * PATCH])
                if x == c:
                    add(accr_ref, 0, slice(0, p.shape[0] - near), dk[near:])
                    add(accr_ref, 1, slice(0, p.shape[0] - near), dv[near:])
                else:
                    rest = jnp.zeros((kw_ref.shape[2] - near, feature), BF)
                    weights = jnp.concatenate([weights, rest], axis=0)
                    d_scores = jnp.concatenate([d_scores, rest], axis=0)
                o_x = dot_nn(vt_ref[t, x], weights)
                dq_x = dot_nn(kt_ref[t, x], d_scores)
                o_t = o_x if o_t is None else o_t + o_x
                dq_t = dq_x if dq_t is None else dq_t + dq_x
            o_cols.append(from_transposed(o_t, heads))
            dq_cols.append(from_transposed(dq_t, heads) * FACTOR)
        o_ref[t * line : (t + 1) * line] = patch_order(o_cols).astype(BF)
        dq_ref[t * line : (t + 1) * line] = patch_order(dq_cols).astype(BF)

    last = (tile_rows + 1) * PATCH
    for n, (acc_ref, out_ref) in enumerate(((acck_ref, dk_ref), (accv_ref, dv_ref))):
        top = jnp.concatenate([acc_ref[c, :PATCH] for c in range(tile_cols)], axis=0)
        bottom = jnp.concatenate([acc_ref[c, last:] for c in range(tile_cols)], axis=0)
        back_a_ref[n * a_rows : (n + 1) * a_rows] = jnp.where(even, bottom, top).astype(BF)
        back_b_ref[n * a_rows : (n + 1) * a_rows] = jnp.where(even, top, bottom).astype(BF)
        for c in range(tile_cols):
            out_ref[c] = acc_ref[c, PATCH:last]
        if split_regs:
            base = 2 * a_rows + n * cut
            back_a_ref[base : base + cut] = accr_ref[n, cut : 2 * cut].astype(BF)
    dreg_ref[...] = accr_ref[...]


def finish_kernel(dk_ref, dv_ref, a_ref, b_ref, *refs, split_regs):
    if split_regs:
        dreg_ref, c_ref, e_ref = refs[:3]
        refs = refs[3:]
    gk_ref, gv_ref = refs[:2]
    even = lax.rem(lax.axis_index("rows"), 2) == 0
    tile_cols = dk_ref.shape[0]
    edge = b_ref.shape[0] // 2
    for n, (acc_ref, out_ref) in enumerate(((dk_ref, gk_ref), (dv_ref, gv_ref))):
        from_a = a_ref[n * edge : (n + 1) * edge]
        from_b = b_ref[n * edge : (n + 1) * edge]
        top = jnp.where(even, from_b, from_a).astype(F32)
        bottom = jnp.where(even, from_a, from_b).astype(F32)
        rows = acc_ref.shape[1]
        columns = []
        for c in range(tile_cols):
            high = top[c * PATCH : (c + 1) * PATCH]
            low = bottom[c * PATCH : (c + 1) * PATCH]
            if rows == PATCH:
                columns.append(acc_ref[c] + high + low)
                continue
            columns.append(
                jnp.concatenate(
                    [acc_ref[c, :PATCH] + high, acc_ref[c, PATCH : rows - PATCH], acc_ref[c, rows - PATCH :] + low]
                    if rows > 2 * PATCH
                    else [acc_ref[c, :PATCH] + high, acc_ref[c, PATCH:] + low],
                    axis=0,
                )
            )
        out_ref[...] = patch_order(columns).astype(BF)
        if split_regs:
            cut = c_ref.shape[1]
            base = 2 * edge + n * cut
            refs[2][n] = (
                dreg_ref[n, :cut]
                + a_ref[base : base + cut].astype(F32)
                + c_ref[n].astype(F32)
                + e_ref[n].astype(F32)
            )


def shape(dims, dtype):
    return jax.ShapeDtypeStruct(dims, dtype)


def params():
    return pltpu.CompilerParams(vmem_limit_bytes=48 * 1024 * 1024)


def shards(query, keys, values, registers, cotangent):
    count = lax.axis_size("rows")
    split_regs = count == 4
    tile_cols = query.shape[1] // TILE
    tile_rows = query.shape[0] // TILE
    feature = query.shape[2]
    total = query.shape[0] * query.shape[1]
    edge = tile_cols * PATCH
    own = registers.shape[1]
    reg_count = own * count
    q, k, v, g = (x.reshape(total, feature) for x in (query, keys, values, cotangent))
    extra = 2 * own if split_regs else 0

    pay_a, pay_b = pl.pallas_call(
        prepare_kernel,
        out_shape=(shape((2 * edge + extra, feature), BF), shape((2 * edge, feature), BF)),
        in_specs=[VMEM] * 3,
        out_specs=(VMEM, VMEM),
        compiler_params=params(),
        name="prepare",
    )(k, v, registers)
    got_b = swap(pay_b, pairs_b(count))
    got_a = swap(pay_a, pairs_a(count))
    if split_regs:
        two = [(i, i ^ 2) for i in range(count)]
        three = [(i, i ^ 3) for i in range(count)]
        regs = (registers, swap(registers, two), swap(registers, three))
    else:
        regs = (lax.all_gather(registers, "rows", axis=1, tiled=True),)

    span = (tile_rows + 2) * PATCH
    window = 3 * PATCH + reg_count
    attended, grad_query, dk, dv, back_a, back_b, dreg = pl.pallas_call(
        functools.partial(attention_kernel, tile_cols, split_regs=split_regs),
        out_shape=(
            shape((total, feature), BF),
            shape((total, feature), BF),
            shape((tile_cols, tile_rows * PATCH, feature), F32),
            shape((tile_cols, tile_rows * PATCH, feature), F32),
            shape((2 * edge + extra, feature), BF),
            shape((2 * edge, feature), BF),
            shape((2, reg_count, feature), F32),
        ),
        in_specs=[VMEM] * (6 + len(regs)),
        out_specs=(VMEM,) * 7,
        scratch_shapes=[
            pltpu.VMEM((tile_rows, tile_cols, window, feature), BF),
            pltpu.VMEM((tile_rows, tile_cols, window, feature), BF),
            pltpu.VMEM((tile_rows, tile_cols, feature, window), BF),
            pltpu.VMEM((tile_rows, tile_cols, feature, window), BF),
            pltpu.VMEM((tile_cols, span, feature), F32),
            pltpu.VMEM((tile_cols, span, feature), F32),
            pltpu.VMEM((2, reg_count, feature), F32),
        ],
        compiler_params=params(),
        name="attention",
    )(q, g, k, v, got_a, got_b, *regs)

    back_from_b = swap(back_b, pairs_b(count))
    back_from_a = swap(back_a, pairs_a(count))
    if split_regs:
        tails = dreg.astype(BF)
        rest = (
            dreg,
            swap(tails[:, 2 * own : 3 * own], two),
            swap(tails[:, 3 * own :], three),
        )
        last_shapes = (shape((2, own, feature), F32),)
    else:
        rest = ()
        last_shapes = ()
    outs = pl.pallas_call(
        functools.partial(finish_kernel, split_regs=split_regs),
        out_shape=(shape((total, feature), BF), shape((total, feature), BF)) + last_shapes,
        in_specs=[VMEM] * (4 + len(rest)),
        out_specs=(VMEM,) * (2 + len(last_shapes)),
        compiler_params=params(),
        name="finish",
    )(dk, dv, back_from_a, back_from_b, *rest)
    if split_regs:
        grad_registers = outs[2]
    else:
        grad_registers = lax.psum_scatter(dreg, "rows", scatter_dimension=1, tiled=True)
    whole = query.shape
    return (
        attended.reshape(whole),
        grad_query.reshape(whole),
        outs[0].reshape(whole),
        outs[1].reshape(whole),
        grad_registers,
    )


def solution(mesh):
    slab = P(("groups", "rows"), None, "cols")
    in_specs = (slab, slab, slab, P(None, "rows", "cols"), slab)
    out_specs = (slab, slab, slab, slab, P("groups", "rows", "cols"))
    return jax.shard_map(shards, mesh=mesh, in_specs=in_specs, out_specs=out_specs, check_vma=False)
```

time: 244 us -> 33.7 us (0.14)
  local copies, waits for them, and re-layouts: 129 us -> 2.57 us
  other arithmetic: 34.1 us -> 0.01 us
  blocking collectives: 16.3 us -> 0 us
  between operations: 14.5 us -> 0.7 us
  matrix products: 12.6 us -> 0 us
  loops' own time: 11.4 us -> 0 us
  Pallas kernels: 0 us -> 6.51 us
  waiting for transfers between devices: 13.5 us -> 7.28 us
  starting transfers between devices: 10.3 us -> 16.4 us
    while x116 -> x0, local copies, waits for them, and re-layouts: 43.3 us -> none
    dynamic_slice x10 -> x0, local copies, waits for them, and re-layouts: 25.1 us -> none  [the longest x4 11.9 us: advance(): lax.dynamic_slice_in_dim(acc_keys, row_idx, 3, 1) + spread_near(grad_near_k)]
    dynamic_update_slice x6 -> x0, local copies, waits for them, and re-layouts: 18.7 us -> none  [the longest x4 15.2 us: advance(): lax.dynamic_update_slice_in_dim(acc_values, lax.dynamic_slice_in_dim(acc_...]
    all_gather x1 -> x0, blocking collectives: 16.3 us -> none  [shards(): reg_both = lax.all_gather(registers, 'rows', axis=1, tiled=True)]
    sub x2 -> x0, other arithmetic: 16.1 us -> none  [advance(): d_scores = (probs * (d_wide - row_dot)).astype(jnp.bfloat16)]
    reduce_scatter x1 -> x0, waiting for transfers between devices: 13.5 us -> none  [shards(): lax.psum_scatter(jnp.stack([grad_rk, grad_rv]), 'rows', scatter_dimension...]
    dot_general x24 -> x0, matrix products: 12.6 us -> none  [the longest x2 2.39 us: advance(): jnp.einsum('hcqg,hgd->hcqd', reg_weights, reg_v, preferred_element_type=f...]
    another operation x1 -> x0, loops' own time: 11.4 us -> none  [sweep(): lax.scan(advance, start_state, jnp.arange(query_count, dtype=jnp.int32))]
  transfers between devices with their start and end apart: 5 -> 8, of which waited for: 1 -> 3; matrix products, arithmetic and copies ran while one was open for 6% -> 0% of each run, Pallas kernels for 0% -> 0%
where the time goes in v1:
time: 33.7 us; the launch traced here: 33.5 us
  starting transfers between devices  16.4 us (49%)
  waiting for transfers between devices  7.28 us (22%)
  Pallas kernels  6.51 us (19%)
  local copies, waits for them, and re-layouts  2.57 us (8%)
  between operations  0.7 us (2%)
    ppermute x8, starting transfers between devices, swap(): return lax.ppermute(array, 'rows', pairs)  16.4 us
    ppermute x8, waiting for transfers between devices, swap(): return lax.ppermute(array, 'rows', pairs)  7.28 us
    pallas_call x1, Pallas kernels, shards(): pl.pallas_call(functools.partial(attention_kernel, tile_cols, split_regs=...  5.67 us
    unnamed x10, local copies, waits for them, and re-layouts  2.57 us
    pallas_call x1, Pallas kernels, shards(): pl.pallas_call(functools.partial(finish_kernel, split_regs=split_regs), o...  0.8 us
  transfers between devices with their start and end apart: 8, of which 3 were waited for; matrix products, arithmetic and copies ran while one was open for 0% of the time, Pallas kernels for 0%

profile of v1, /device:TPU:0, one launch (start us, length us, event | category | flops | bytes accessed | tf_op | source)
XLA Modules:
  0.0 33.5 jit_solution(13310166469271503502)
XLA Ops:
  0.6 0.0 copy-start
  0.6 0.9 %copy-done = bf16[16,24,256]{2,1,0:T(8,128)(2,1)S(1)} copy-done((bf16[16,24,256]{2,1,0:T(8,128)(2,1)S(1)}, bf16[16,24,256]{2,1,0:T(8,128)(2,1)}, u32[]{:S(2)}) %copy-start) | copy-done | bytes 196632
  1.6 0.0 copy-start.1
  1.6 0.9 %copy-done.1 = bf16[16,24,256]{2,1,0:T(8,128)(2,1)S(1)} copy-done((bf16[16,24,256]{2,1,0:T(8,128)(2,1)S(1)}, bf16[16,24,256]{2,1,0:T(8,128)(2,1)}, u32[]{:S(2)}) %copy-start.1) | copy-done | bytes 196632
  2.5 0.0 copy-start.4
  2.5 0.7 %copy-done.4 = bf16[2,16,256]{2,1,0:T(8,128)(2,1)S(1)} copy-done((bf16[2,16,256]{2,1,0:T(8,128)(2,1)S(1)}, bf16[2,16,256]{2,1,0:T(8,128)(2,1)}, u32[]{:S(2)}) %copy-start.4) | copy-done | bytes 16408
  3.2 0.0 copy-start.2
  3.2 0.0 copy-start.3
  3.3 3.1 %collective-permute-start = (bf16[416,256]{1,0:T(8,128)(2,1)S(1)}, bf16[416,256]{1,0:T(8,128)(2,1)S(1)}, u32[]{:S(2)}, u32[]{:S(2)}) collective-permute-start(bf16[416,256]{1,0:T(8,128)(2,1)S(1)} %get-tuple-element.17), channel_id=1, source_target_pairs={{0,4},{4,0},{8,12},{12,8},{1,5},{5,1},{9,13},{13,9},{2,6},{6,2},{1... | collective-permute-start | bytes 638984 | tf_op jit(solution)/shard_map/ppermute | solution.py:20
  6.3 0.7 %collective-permute-start.1 = (bf16[384,256]{1,0:T(8,128)(2,1)S(1)}, bf16[384,256]{1,0:T(8,128)(2,1)S(1)}, u32[]{:S(2)}, u32[]{:S(2)}) collective-permute-start(bf16[384,256]{1,0:T(8,128)(2,1)S(1)} %get-tuple-element.18), channel_id=1, source_target_pairs={{4,8},{8,4},{5,9},{9,5},{6,10},{10,6},{7,11},{11,7},{20,24},{24,20... | collective-permute-start | bytes 589832 | tf_op jit(solution)/shard_map/ppermute | solution.py:20
  7.0 3.9 %collective-permute-start.2 = (bf16[2,16,256]{2,1,0:T(8,128)(2,1)S(1)}, bf16[2,16,256]{2,1,0:T(8,128)(2,1)S(1)}, u32[]{:S(2)}, u32[]{:S(2)}) collective-permute-start(bf16[2,16,256]{2,1,0:T(8,128)(2,1)S(1)} %copy-done.4), channel_id=1, source_target_pairs={{0,8},{4,12},{8,0},{12,4},{1,9},{5,13},{9,1},{13,5},{2,10},{6,14},... | collective-permute-start | bytes 49160 | tf_op jit(solution)/shard_map/ppermute | solution.py:20
  10.9 2.9 %collective-permute-start.3 = (bf16[2,16,256]{2,1,0:T(8,128)(2,1)S(1)}, bf16[2,16,256]{2,1,0:T(8,128)(2,1)S(1)}, u32[]{:S(2)}, u32[]{:S(2)}) collective-permute-start(bf16[2,16,256]{2,1,0:T(8,128)(2,1)S(1)} %copy-done.4), channel_id=1, source_target_pairs={{0,12},{4,8},{8,4},{12,0},{1,13},{5,9},{9,5},{13,1},{2,14},{6,10},... | collective-permute-start | bytes 49160 | tf_op jit(solution)/shard_map/ppermute | solution.py:20
  13.8 2.8 %collective-permute-done.2.refs_1_ = bf16[2,16,256]{2,1,0:T(8,128)(2,1)S(1)} collective-permute-done((bf16[2,16,256]{2,1,0:T(8,128)(2,1)S(1)}, bf16[2,16,256]{2,1,0:T(8,128)(2,1)S(1)}, u32[]{:S(2)}, u32[]{:S(2)}) %collective-permute-start.2) | collective-permute-done | bytes 16416 | tf_op jit(solution)/shard_map/ppermute | solution.py:20
  16.7 0.0 collective-permute-done.3.refs_2_
  16.7 0.0 collective-permute-done.1.b_ref
  16.7 0.0 collective-permute-done.a_ref
  16.7 0.0 copy-done.2
  16.7 0.0 copy-done.3
  16.7 5.7 %attention.1 = (bf16[384,256]{1,0:T(8,128)(2,1)}, bf16[384,256]{1,0:T(8,128)(2,1)}, f32[3,128,256]{2,1,0:T(8,128)S(1)}, f32[3,128,256]{2,1,0:T(8,128)S(1)}, bf16...) custom-call(bf16[384,256]{1,0:T(8,128)(2,1)S(1)} %bitcast.12, ...), custom_call_target="tpu_custom_call" | custom-call | tf_op jit(solution)/shard_map/attention/pallas_call | solution.py:307
  22.4 0.7 %collective-permute-start.5 = (bf16[384,256]{1,0:T(8,128)(2,1)S(1)}, bf16[384,256]{1,0:T(8,128)(2,1)S(1)}, u32[]{:S(2)}, u32[]{:S(2)}) collective-permute-start(bf16[384,256]{1,0:T(8,128)(2,1)S(1)} %get-tuple-element.24), channel_id=1, source_target_pairs={{4,8},{8,4},{5,9},{9,5},{6,10},{10,6},{7,11},{11,7},{20,24},{24,20... | collective-permute-start | bytes 589832 | tf_op jit(solution)/shard_map/ppermute | solution.py:20
  23.1 3.6 %collective-permute-start.4 = (bf16[416,256]{1,0:T(8,128)(2,1)S(1)}, bf16[416,256]{1,0:T(8,128)(2,1)S(1)}, u32[]{:S(2)}, u32[]{:S(2)}) collective-permute-start(bf16[416,256]{1,0:T(8,128)(2,1)S(1)} %get-tuple-element.23), channel_id=1, source_target_pairs={{0,4},{4,0},{8,12},{12,8},{1,5},{5,1},{9,13},{13,9},{2,6},{6,2},{1... | collective-permute-start | bytes 638984 | tf_op jit(solution)/shard_map/ppermute | solution.py:20
  26.7 1.4 %collective-permute-start.7 = (bf16[2,16,256]{2,1,0:T(8,128)(2,1)S(1)}, bf16[2,16,256]{2,1,0:T(8,128)(2,1)S(1)}, u32[]{:S(2)}, u32[]{:S(2)}) collective-permute-start(bf16[2,16,256]{2,1,0:T(8,128)(2,1)S(1)} %get-tuple-element.29), channel_id=1, source_target_pairs={{0,12},{4,8},{8,4},{12,0},{1,13},{5,9},{9,5},{13,1},{2,14},{6,10},... | collective-permute-start | bytes 49160 | tf_op jit(solution)/shard_map/ppermute | solution.py:20
  28.0 0.2 collective-permute-start.6
  28.2 4.0 %collective-permute-done.7.refs_2_ = bf16[2,16,256]{2,1,0:T(8,128)(2,1)S(1)} collective-permute-done((bf16[2,16,256]{2,1,0:T(8,128)(2,1)S(1)}, bf16[2,16,256]{2,1,0:T(8,128)(2,1)S(1)}, u32[]{:S(2)}, u32[]{:S(2)}) %collective-permute-start.7) | collective-permute-done | bytes 16416 | tf_op jit(solution)/shard_map/ppermute | solution.py:20
  32.2 0.5 %collective-permute-done.6.refs_1_ = bf16[2,16,256]{2,1,0:T(8,128)(2,1)S(1)} collective-permute-done((bf16[2,16,256]{2,1,0:T(8,128)(2,1)S(1)}, bf16[2,16,256]{2,1,0:T(8,128)(2,1)S(1)}, u32[]{:S(2)}, u32[]{:S(2)}) %collective-permute-start.6) | collective-permute-done | bytes 16416 | tf_op jit(solution)/shard_map/ppermute | solution.py:20
  32.7 0.0 collective-permute-done.5.b_ref
  32.7 0.0 collective-permute-done.4.a_ref
  32.7 0.8 %finish.1 = (bf16[384,256]{1,0:T(8,128)(2,1)}, bf16[384,256]{1,0:T(8,128)(2,1)}, f32[2,16,256]{2,1,0:T(8,128)}) custom-call(f32[3,128,256]{2,1,0:T(8,128)S(1)} %get-tuple-element.21.dk_ref, f32[3,128,256]{2,1,0:T(8,128)S(1)} %get-tuple-element.22.dv_ref, bf16[416,256]{1,0:T(8,128)(2,1)S(1)} %collective-permute-done.4.a_ref, ...), custom_call_target="tpu_custom_call" | custom-call | tf_op jit(solution)/shard_map/finish/pallas_call | solution.py:346
  (3 shorter events, 0.0 us)
Async XLA Ops:
  0.6 0.9 %copy-start = (bf16[16,24,256]{2,1,0:T(8,128)(2,1)S(1)}, bf16[16,24,256]{2,1,0:T(8,128)(2,1)}, u32[]{:S(2)}) copy-start(bf16[16,24,256]{2,1,0:T(8,128)(2,1)} %param.6) | copy-start | bytes 589828
  1.6 0.9 %copy-start.1 = (bf16[16,24,256]{2,1,0:T(8,128)(2,1)S(1)}, bf16[16,24,256]{2,1,0:T(8,128)(2,1)}, u32[]{:S(2)}) copy-start(bf16[16,24,256]{2,1,0:T(8,128)(2,1)} %param.7) | copy-start | bytes 589828
  2.5 0.7 %copy-start.4 = (bf16[2,16,256]{2,1,0:T(8,128)(2,1)S(1)}, bf16[2,16,256]{2,1,0:T(8,128)(2,1)}, u32[]{:S(2)}) copy-start(bf16[2,16,256]{2,1,0:T(8,128)(2,1)} %refs_0_.1) | copy-start | bytes 49156
  3.2 13.5 %copy-start.2 = (bf16[16,24,256]{2,1,0:T(8,128)(2,1)S(1)}, bf16[16,24,256]{2,1,0:T(8,128)(2,1)}, u32[]{:S(2)}) copy-start(bf16[16,24,256]{2,1,0:T(8,128)(2,1)} %param.5) | copy-start | bytes 589828
  3.2 13.5 %copy-start.3 = (bf16[16,24,256]{2,1,0:T(8,128)(2,1)S(1)}, bf16[16,24,256]{2,1,0:T(8,128)(2,1)}, u32[]{:S(2)}) copy-start(bf16[16,24,256]{2,1,0:T(8,128)(2,1)} %param.9) | copy-start | bytes 589828
  3.3 13.4 %collective-permute-start = (bf16[416,256]{1,0:T(8,128)(2,1)S(1)}, bf16[416,256]{1,0:T(8,128)(2,1)S(1)}, u32[]{:S(2)}, u32[]{:S(2)}) collective-permute-start(bf16[416,256]{1,0:T(8,128)(2,1)S(1)} %get-tuple-element.17), channel_id=1, source_target_pairs={{0,4},{4,0},{8,12},{12,8},{1,5},{5,1},{9,13},{13,9},{2,6},{6,2},{1... | collective-permute-start | bytes 638984 | tf_op jit(solution)/shard_map/ppermute | solution.py:20
  6.3 10.3 %collective-permute-start.1 = (bf16[384,256]{1,0:T(8,128)(2,1)S(1)}, bf16[384,256]{1,0:T(8,128)(2,1)S(1)}, u32[]{:S(2)}, u32[]{:S(2)}) collective-permute-start(bf16[384,256]{1,0:T(8,128)(2,1)S(1)} %get-tuple-element.18), channel_id=1, source_target_pairs={{4,8},{8,4},{5,9},{9,5},{6,10},{10,6},{7,11},{11,7},{20,24},{24,20... | collective-permute-start | bytes 589832 | tf_op jit(solution)/shard_map/ppermute | solution.py:20
  7.0 9.7 %collective-permute-start.2 = (bf16[2,16,256]{2,1,0:T(8,128)(2,1)S(1)}, bf16[2,16,256]{2,1,0:T(8,128)(2,1)S(1)}, u32[]{:S(2)}, u32[]{:S(2)}) collective-permute-start(bf16[2,16,256]{2,1,0:T(8,128)(2,1)S(1)} %copy-done.4), channel_id=1, source_target_pairs={{0,8},{4,12},{8,0},{12,4},{1,9},{5,13},{9,1},{13,5},{2,10},{6,14},... | collective-permute-start | bytes 49160 | tf_op jit(solution)/shard_map/ppermute | solution.py:20
  10.9 5.8 %collective-permute-start.3 = (bf16[2,16,256]{2,1,0:T(8,128)(2,1)S(1)}, bf16[2,16,256]{2,1,0:T(8,128)(2,1)S(1)}, u32[]{:S(2)}, u32[]{:S(2)}) collective-permute-start(bf16[2,16,256]{2,1,0:T(8,128)(2,1)S(1)} %copy-done.4), channel_id=1, source_target_pairs={{0,12},{4,8},{8,4},{12,0},{1,13},{5,9},{9,5},{13,1},{2,14},{6,10},... | collective-permute-start | bytes 49160 | tf_op jit(solution)/shard_map/ppermute | solution.py:20
  22.4 10.3 %collective-permute-start.5 = (bf16[384,256]{1,0:T(8,128)(2,1)S(1)}, bf16[384,256]{1,0:T(8,128)(2,1)S(1)}, u32[]{:S(2)}, u32[]{:S(2)}) collective-permute-start(bf16[384,256]{1,0:T(8,128)(2,1)S(1)} %get-tuple-element.24), channel_id=1, source_target_pairs={{4,8},{8,4},{5,9},{9,5},{6,10},{10,6},{7,11},{11,7},{20,24},{24,20... | collective-permute-start | bytes 589832 | tf_op jit(solution)/shard_map/ppermute | solution.py:20
  23.1 9.6 %collective-permute-start.4 = (bf16[416,256]{1,0:T(8,128)(2,1)S(1)}, bf16[416,256]{1,0:T(8,128)(2,1)S(1)}, u32[]{:S(2)}, u32[]{:S(2)}) collective-permute-start(bf16[416,256]{1,0:T(8,128)(2,1)S(1)} %get-tuple-element.23), channel_id=1, source_target_pairs={{0,4},{4,0},{8,12},{12,8},{1,5},{5,1},{9,13},{13,9},{2,6},{6,2},{1... | collective-permute-start | bytes 638984 | tf_op jit(solution)/shard_map/ppermute | solution.py:20
  26.7 5.5 %collective-permute-start.7 = (bf16[2,16,256]{2,1,0:T(8,128)(2,1)S(1)}, bf16[2,16,256]{2,1,0:T(8,128)(2,1)S(1)}, u32[]{:S(2)}, u32[]{:S(2)}) collective-permute-start(bf16[2,16,256]{2,1,0:T(8,128)(2,1)S(1)} %get-tuple-element.29), channel_id=1, source_target_pairs={{0,12},{4,8},{8,4},{12,0},{1,13},{5,9},{9,5},{13,1},{2,14},{6,10},... | collective-permute-start | bytes 49160 | tf_op jit(solution)/shard_map/ppermute | solution.py:20
  28.0 4.6 %collective-permute-start.6 = (bf16[2,16,256]{2,1,0:T(8,128)(2,1)S(1)}, bf16[2,16,256]{2,1,0:T(8,128)(2,1)S(1)}, u32[]{:S(2)}, u32[]{:S(2)}) collective-permute-start(bf16[2,16,256]{2,1,0:T(8,128)(2,1)S(1)} %get-tuple-element.30), channel_id=1, source_target_pairs={{0,8},{4,12},{8,0},{12,4},{1,9},{5,13},{9,1},{13,5},{2,10},{6,14},... | collective-permute-start | bytes 49160 | tf_op jit(solution)/shard_map/ppermute | solution.py:20

commit v2 on v1

v2 whole, which is shorter than its diff:
```python
import functools

import jax
import jax.numpy as jnp
from jax import lax
from jax.experimental import pallas as pl
from jax.experimental.pallas import tpu as pltpu
from jax.sharding import PartitionSpec as P

HEAD = 64
TILE = 8
PATCH = TILE * TILE
FACTOR = HEAD ** (-0.5)
BF = jnp.bfloat16
F32 = jnp.float32
VMEM = pl.BlockSpec(memory_space=pltpu.VMEM)


def swap(array, pairs):
    return lax.ppermute(array, "rows", pairs)


def pairs_a(count):
    return [(i, i ^ 1) for i in range(count)]


def pairs_b(count):
    return [p for i in range(1, count - 1, 2) for p in ((i, i + 1), (i + 1, i))]


def column_tiles(block, tile_cols):
    feature = block.shape[1]
    wide = block.astype(F32).reshape(-1, tile_cols, TILE, feature)
    return [wide[:, c].reshape(-1, feature) for c in range(tile_cols)]


def patch_order(columns):
    feature = columns[0].shape[1]
    parts = [x.reshape(-1, 1, TILE, feature) for x in columns]
    return jnp.concatenate(parts, axis=1).reshape(-1, feature)


def slots(heads):
    return [0, 2, 1, 3] if heads == 4 else list(range(heads))


def block_diagonal(tile, heads):
    order = slots(heads)
    feature = tile.shape[1]
    lane_head = lax.broadcasted_iota(jnp.int32, tile.shape, 1) // HEAD
    zero = jnp.zeros_like(tile)
    return jnp.concatenate([jnp.where(lane_head == h, tile, zero) for h in order], axis=0)


def from_transposed(out_t, heads):
    if heads == 4:
        first = lax.broadcasted_iota(jnp.int32, (HEAD, 2 * PATCH), 1) < PATCH
        left = jnp.where(first, out_t[:HEAD, : 2 * PATCH], out_t[2 * HEAD : 3 * HEAD, : 2 * PATCH])
        right = jnp.where(first, out_t[HEAD : 2 * HEAD, 2 * PATCH :], out_t[3 * HEAD :, 2 * PATCH :])
        turned = jnp.concatenate([left, right], axis=0).T
        return jnp.concatenate([turned[:PATCH], turned[PATCH:]], axis=1)
    turned = out_t.T
    lane_head = lax.broadcasted_iota(jnp.int32, (PATCH, heads * HEAD), 1) // HEAD
    total = turned[:PATCH]
    for h in range(1, heads):
        total = jnp.where(lane_head == h, turned[h * PATCH : (h + 1) * PATCH], total)
    return total


def dot_nt(a, b):
    return lax.dot_general(a, b, (((1,), (1,)), ((), ())), preferred_element_type=F32)


def dot_nn(a, b):
    return lax.dot_general(a, b, (((1,), (0,)), ((), ())), preferred_element_type=F32)


def prepare_kernel(k_ref, v_ref, reg_ref, a_ref, b_ref, sems):
    even = lax.rem(lax.axis_index("rows"), 2) == 0
    edge = b_ref.shape[0] // 2
    last = k_ref.shape[0] - edge
    at_a = pl.multiple_of(jnp.where(even, last, 0), edge)
    at_b = pl.multiple_of(jnp.where(even, 0, last), edge)
    moves = []
    for n, ref in enumerate((k_ref, v_ref)):
        moves.append((ref.at[pl.ds(at_a, edge)], a_ref.at[pl.ds(n * edge, edge)]))
        moves.append((ref.at[pl.ds(at_b, edge)], b_ref.at[pl.ds(n * edge, edge)]))
    own = reg_ref.shape[1]
    if a_ref.shape[0] > 2 * edge:
        for n in range(2):
            moves.append((reg_ref.at[n], a_ref.at[pl.ds(2 * edge + n * own, own)]))
    copies = [pltpu.make_async_copy(x, y, sems.at[n]) for n, (x, y) in enumerate(moves)]
    for copy in copies:
        copy.start()
    for copy in copies:
        copy.wait()


def columns_near(c, tile_cols):
    return max(c - 1, 0), min(c + 2, tile_cols)


def own_kernel(
    tile_cols,
    q_ref,
    g_ref,
    k_ref,
    v_ref,
    qbd_ref,
    gbd_ref,
    kt_ref,
    vt_ref,
    exp_ref,
    dw_ref,
    stat_ref,
    kc_ref,
    vc_ref,
):
    heads = q_ref.shape[1] // HEAD
    line = tile_cols * PATCH
    tile_rows = q_ref.shape[0] // line
    rows = tile_rows * PATCH
    for x_ref, c_ref, t_ref in ((k_ref, kc_ref, kt_ref), (v_ref, vc_ref, vt_ref)):
        for c, column in enumerate(column_tiles(x_ref[...], tile_cols)):
            column = column.astype(BF)
            c_ref[c * rows : (c + 1) * rows] = column
            t_ref[:, c * rows : (c + 1) * rows] = column.T
    for t in range(tile_rows):
        q_cols = column_tiles(q_ref[t * line : (t + 1) * line], tile_cols)
        g_cols = column_tiles(g_ref[t * line : (t + 1) * line], tile_cols)
        for c in range(tile_cols):
            tile = t * tile_cols + c
            q_bd = block_diagonal((q_cols[c] * FACTOR).astype(BF), heads)
            g_bd = block_diagonal(g_cols[c].astype(BF), heads)
            qbd_ref[tile] = q_bd
            gbd_ref[tile] = g_bd
            low, high = columns_near(c, tile_cols)
            near = slice(low * rows, high * rows)
            size = (high - low) * rows
            s = dot_nt(kc_ref[near], q_bd)
            d = dot_nt(vc_ref[near], g_bd).astype(BF)
            top = jnp.max(s, axis=0, keepdims=True)
            e = jnp.exp(s - top)
            exp_ref[tile, :size] = e
            dw_ref[tile, :size] = d
            stat_ref[tile, 0:1] = top
            stat_ref[tile, 1:2] = jnp.sum(e, axis=0, keepdims=True)
            stat_ref[tile, 2:3] = jnp.sum(e * d.astype(F32), axis=0, keepdims=True)


def far_kernel(tile_cols, split_regs, *refs):
    qbd_ref, gbd_ref, stat_ref, a_ref, b_ref = refs[:5]
    if split_regs:
        own_ref, two_ref, three_ref = refs[5:8]
        refs = refs[8:]
    else:
        all_ref = refs[5]
        refs = refs[6:]
    final_ref, px_ref, dsx_ref, kx_ref, vx_ref, back_a_ref, back_b_ref = refs[:7]
    reg_outs = refs[7:]
    feature = a_ref.shape[1]
    tile_rows = qbd_ref.shape[0] // tile_cols
    edge = tile_cols * PATCH
    me = lax.axis_index("rows")
    even = lax.rem(me, 2) == 0
    has = (me > 0, me < lax.axis_size("rows") - 1)
    for n, ref in enumerate((kx_ref, vx_ref)):
        from_a = a_ref[n * edge : (n + 1) * edge]
        from_b = b_ref[n * edge : (n + 1) * edge]
        top = column_tiles(jnp.where(even, from_b, from_a), tile_cols)
        bottom = column_tiles(jnp.where(even, from_a, from_b), tile_cols)
        if split_regs:
            cut = own_ref.shape[1]
            base = 2 * edge + n * cut
            regs = jnp.concatenate([own_ref[n], a_ref[base : base + cut], two_ref[n], three_ref[n]], axis=0)
        else:
            regs = all_ref[n]
        for t, halo in enumerate((top, bottom)):
            ref[t, :edge] = jnp.concatenate(halo, axis=0).astype(BF)
            ref[t, edge:] = regs
    dk_reg = dv_reg = None
    dk_halo, dv_halo = [], []
    for t in range(tile_rows):
        dk_t = dv_t = None
        for c in range(tile_cols):
            tile = t * tile_cols + c
            q_bd = qbd_ref[tile]
            g_bd = gbd_ref[tile]
            low, high = columns_near(c, tile_cols)
            s = dot_nt(kx_ref[t], q_bd)
            d = dot_nt(vx_ref[t], g_bd)
            s_near = jnp.where(has[t], s[low * PATCH : high * PATCH], -1e30)
            s = jnp.concatenate([s_near, s[edge:]], axis=0)
            d = jnp.concatenate([d[low * PATCH : high * PATCH], d[edge:]], axis=0)
            d = d.astype(BF).astype(F32)
            own_top = stat_ref[tile, 0:1]
            top = jnp.maximum(own_top, jnp.max(s, axis=0, keepdims=True))
            e = jnp.exp(s - top)
            ratio = jnp.exp(own_top - top)
            inverse = 1.0 / (stat_ref[tile, 1:2] * ratio + jnp.sum(e, axis=0, keepdims=True))
            row_dot = (stat_ref[tile, 2:3] * ratio + jnp.sum(e * d, axis=0, keepdims=True)) * inverse
            final_ref[tile, 0:1] = ratio * inverse
            final_ref[tile, 1:2] = row_dot
            p = e * inverse
            parts = []
            for x in (p, p * (d - row_dot)):
                x = x.astype(BF)
                pieces = [x]
                size = (high - low) * PATCH
                if low > 0 or high < tile_cols:
                    pieces = [x[:size], x[size:]]
                    if high < tile_cols:
                        pieces.insert(1, jnp.zeros(((tile_cols - high) * PATCH, feature), BF))
                    if low > 0:
                        pieces.insert(0, jnp.zeros((low * PATCH, feature), BF))
                parts.append(jnp.concatenate(pieces, axis=0))
            weights, d_scores = parts
            px_ref[tile] = weights
            dsx_ref[tile] = d_scores
            dk = dot_nn(d_scores, q_bd)
            dv = dot_nn(weights, g_bd)
            dk_t = dk if dk_t is None else dk_t + dk
            dv_t = dv if dv_t is None else dv_t + dv
        dk_halo.append(dk_t[:edge])
        dv_halo.append(dv_t[:edge])
        dk_reg = dk_t[edge:] if dk_reg is None else dk_reg + dk_t[edge:]
        dv_reg = dv_t[edge:] if dv_reg is None else dv_reg + dv_t[edge:]
    for n, (halo, reg) in enumerate(((dk_halo, dk_reg), (dv_halo, dv_reg))):
        top, bottom = halo
        back_a_ref[n * edge : (n + 1) * edge] = jnp.where(even, bottom, top).astype(BF)
        back_b_ref[n * edge : (n + 1) * edge] = jnp.where(even, top, bottom).astype(BF)
        if split_regs:
            base = 2 * edge + n * cut
            reg_outs[0][n] = reg[:cut]
            back_a_ref[base : base + cut] = reg[cut : 2 * cut].astype(BF)
            reg_outs[1][n] = reg[2 * cut : 3 * cut].astype(BF)
            reg_outs[2][n] = reg[3 * cut :].astype(BF)
        else:
            reg_outs[0][n] = reg


def rest_kernel(
    tile_cols,
    qbd_ref,
    gbd_ref,
    kt_ref,
    vt_ref,
    exp_ref,
    dw_ref,
    final_ref,
    px_ref,
    dsx_ref,
    kx_ref,
    vx_ref,
    o_ref,
    dq_ref,
    dk_ref,
    dv_ref,
):
    feature = kt_ref.shape[0]
    heads = feature // HEAD
    line = tile_cols * PATCH
    tile_rows = qbd_ref.shape[0] // tile_cols
    rows = tile_rows * PATCH
    for t in range(tile_rows):
        kxt = kx_ref[t].T
        vxt = vx_ref[t].T
        o_cols, dq_cols = [], []
        for c in range(tile_cols):
            tile = t * tile_cols + c
            low, high = columns_near(c, tile_cols)
            near = slice(low * rows, high * rows)
            size = (high - low) * rows
            p = exp_ref[tile, :size] * final_ref[tile, 0:1]
            d_scores = (p * (dw_ref[tile, :size].astype(F32) - final_ref[tile, 1:2])).astype(BF)
            weights = p.astype(BF)
            dk = dot_nn(d_scores, qbd_ref[tile])
            dv = dot_nn(weights, gbd_ref[tile])
            first = t == 0
            for ref, value in ((dk_ref, dk), (dv_ref, dv)):
                for x in range(low, high):
                    part = value[(x - low) * rows : (x - low + 1) * rows]
                    if first and (x == c + 1 or (c == 0)):
                        ref[x] = part
                    else:
                        ref[x] += part
            o_t = dot_nn(vt_ref[:, near], weights) + dot_nn(vxt, px_ref[tile])
            dq_t = dot_nn(kt_ref[:, near], d_scores) + dot_nn(kxt, dsx_ref[tile])
            o_cols.append(from_transposed(o_t, heads))
            dq_cols.append(from_transposed(dq_t, heads) * FACTOR)
        o_ref[t * line : (t + 1) * line] = patch_order(o_cols).astype(BF)
        dq_ref[t * line : (t + 1) * line] = patch_order(dq_cols).astype(BF)


def finish_kernel(dk_ref, dv_ref, a_ref, b_ref, *refs, split_regs):
    if split_regs:
        dreg_ref, c_ref, e_ref = refs[:3]
        refs = refs[3:]
    gk_ref, gv_ref = refs[:2]
    even = lax.rem(lax.axis_index("rows"), 2) == 0
    tile_cols = dk_ref.shape[0]
    edge = b_ref.shape[0] // 2
    for n, (acc_ref, out_ref) in enumerate(((dk_ref, gk_ref), (dv_ref, gv_ref))):
        from_a = a_ref[n * edge : (n + 1) * edge]
        from_b = b_ref[n * edge : (n + 1) * edge]
        top = jnp.where(even, from_b, from_a).astype(F32)
        bottom = jnp.where(even, from_a, from_b).astype(F32)
        rows = acc_ref.shape[1]
        columns = []
        for c in range(tile_cols):
            high = top[c * PATCH : (c + 1) * PATCH]
            low = bottom[c * PATCH : (c + 1) * PATCH]
            if rows == PATCH:
                columns.append(acc_ref[c] + high + low)
                continue
            columns.append(
                jnp.concatenate(
                    [acc_ref[c, :PATCH] + high, acc_ref[c, PATCH : rows - PATCH], acc_ref[c, rows - PATCH :] + low]
                    if rows > 2 * PATCH
                    else [acc_ref[c, :PATCH] + high, acc_ref[c, PATCH:] + low],
                    axis=0,
                )
            )
        out_ref[...] = patch_order(columns).astype(BF)
        if split_regs:
            cut = c_ref.shape[1]
            base = 2 * edge + n * cut
            refs[2][n] = (
                dreg_ref[n, :cut]
                + a_ref[base : base + cut].astype(F32)
                + c_ref[n].astype(F32)
                + e_ref[n].astype(F32)
            )


def shape(dims, dtype):
    return jax.ShapeDtypeStruct(dims, dtype)


def call(kernel, name, ins, outs, flops, in_specs=None, scratch=()):
    size = sum(x.size * x.dtype.itemsize for x in ins) + sum(x.size * x.dtype.itemsize for x in outs)
    return pl.pallas_call(
        kernel,
        out_shape=tuple(outs),
        in_specs=in_specs or [VMEM] * len(ins),
        out_specs=(VMEM,) * len(outs),
        scratch_shapes=list(scratch),
        compiler_params=pltpu.CompilerParams(vmem_limit_bytes=24 * 1024 * 1024),
        cost_estimate=pl.CostEstimate(flops=flops, bytes_accessed=size, transcendentals=0),
        name=name,
    )(*ins)


def shards(query, keys, values, registers, cotangent):
    count = lax.axis_size("rows")
    split_regs = count == 4
    tile_cols = query.shape[1] // TILE
    tile_rows = query.shape[0] // TILE
    assert tile_rows == 2
    feature = query.shape[2]
    total = query.shape[0] * query.shape[1]
    edge = tile_cols * PATCH
    own = registers.shape[1]
    reg_count = own * count
    q, k, v, g = (x.reshape(total, feature) for x in (query, keys, values, cotangent))
    extra = 2 * own if split_regs else 0
    two = [(i, i ^ 2) for i in range(count)]
    three = [(i, i ^ 3) for i in range(count)]

    if split_regs:
        regs = (registers, swap(registers, two), swap(registers, three))
    else:
        regs = (lax.all_gather(registers, "rows", axis=1, tiled=True),)
    pay_a, pay_b = call(
        prepare_kernel,
        "prepare",
        (k, v, registers),
        (shape((2 * edge + extra, feature), BF), shape((2 * edge, feature), BF)),
        0,
        in_specs=[pl.BlockSpec(memory_space=pl.ANY)] * 3,
        scratch=[pltpu.SemaphoreType.DMA((6,))],
    )
    got_b = swap(pay_b, pairs_b(count))
    got_a = swap(pay_a, pairs_a(count))

    tiles = tile_rows * tile_cols
    rows = tile_rows * PATCH
    most = min(3, tile_cols) * rows
    window = edge + reg_count
    qbd, gbd, kt, vt, exps, dw, stats = call(
        functools.partial(own_kernel, tile_cols),
        "own",
        (q, g, k, v),
        (
            shape((tiles, feature, feature), BF),
            shape((tiles, feature, feature), BF),
            shape((feature, total), BF),
            shape((feature, total), BF),
            shape((tiles, most, feature), F32),
            shape((tiles, most, feature), BF),
            shape((tiles, 8, feature), F32),
        ),
        4 * tiles * most * feature * feature,
        scratch=[pltpu.VMEM((total, feature), BF)] * 2,
    )
    if split_regs:
        reg_shapes = (
            shape((2, own, feature), F32),
            shape((2, own, feature), BF),
            shape((2, own, feature), BF),
        )
    else:
        reg_shapes = (shape((2, reg_count, feature), F32),)
    final, px, dsx, kx, vx, back_a, back_b, *back_regs = call(
        functools.partial(far_kernel, tile_cols, split_regs),
        "far",
        (qbd, gbd, stats, got_a, got_b) + regs,
        (
            shape((tiles, 8, feature), F32),
            shape((tiles, window, feature), BF),
            shape((tiles, window, feature), BF),
            shape((tile_rows, window, feature), BF),
            shape((tile_rows, window, feature), BF),
            shape((2 * edge + extra, feature), BF),
            shape((2 * edge, feature), BF),
        )
        + reg_shapes,
        8 * tiles * window * feature * feature,
    )
    back_from_b = swap(back_b, pairs_b(count))
    back_from_a = swap(back_a, pairs_a(count))
    if split_regs:
        rest = (back_regs[0], swap(back_regs[1], two), swap(back_regs[2], three))
        last_shapes = (shape((2, own, feature), F32),)
    else:
        rest = ()
        last_shapes = ()
    attended, grad_query, dk, dv = call(
        functools.partial(rest_kernel, tile_cols),
        "rest",
        (qbd, gbd, kt, vt, exps, dw, final, px, dsx, kx, vx),
        (
            shape((total, feature), BF),
            shape((total, feature), BF),
            shape((tile_cols, rows, feature), F32),
            shape((tile_cols, rows, feature), F32),
        ),
        8 * tiles * most * feature * feature,
    )
    outs = call(
        functools.partial(finish_kernel, split_regs=split_regs),
        "finish",
        (dk, dv, back_from_a, back_from_b) + rest,
        (shape((total, feature), BF), shape((total, feature), BF)) + last_shapes,
        0,
    )
    if split_regs:
        grad_registers = outs[2]
    else:
        grad_registers = lax.psum_scatter(back_regs[0], "rows", scatter_dimension=1, tiled=True)
    whole = query.shape
    return (
        attended.reshape(whole),
        grad_query.reshape(whole),
        outs[0].reshape(whole),
        outs[1].reshape(whole),
        grad_registers,
    )


def solution(mesh):
    slab = P(("groups", "rows"), None, "cols")
    in_specs = (slab, slab, slab, P(None, "rows", "cols"), slab)
    out_specs = (slab, slab, slab, slab, P("groups", "rows", "cols"))
    return jax.shard_map(shards, mesh=mesh, in_specs=in_specs, out_specs=out_specs, check_vma=False)
```

time: 33.7 us -> 34.2 us (1.015)
  waiting for transfers between devices: 7.28 us -> 2.23 us
  local copies, waits for them, and re-layouts: 2.57 us -> 5.55 us
  Pallas kernels: 6.51 us -> 8.28 us
  starting transfers between devices: 16.4 us -> 17 us
    ppermute x8, waiting for transfers between devices: 7.28 us -> 2.23 us  [swap(): return lax.ppermute(array, 'rows', pairs)]
    unnamed x10 -> x12, local copies, waits for them, and re-layouts: 2.57 us -> 5.55 us
    pallas_call x3 -> x5, Pallas kernels: 6.51 us -> 8.28 us  [call(): pl.pallas_call(kernel, out_shape=tuple(outs), in_specs=in_specs or [VMEM]...]
    ppermute x8, starting transfers between devices: 16.4 us -> 17 us  [swap(): return lax.ppermute(array, 'rows', pairs)]
  transfers between devices with their start and end apart: 8 -> 8, of which waited for: 3 -> 2; matrix products, arithmetic and copies ran while one was open for 0% -> 0% of each run, Pallas kernels for 0% -> 11%
where the time goes in v2:
time: 34.2 us; the launch traced here: 33.8 us
  starting transfers between devices  17 us (50%)
  Pallas kernels  8.28 us (24%)
  local copies, waits for them, and re-layouts  5.55 us (16%)
  waiting for transfers between devices  2.23 us (7%)
  between operations  0.73 us (2%)
    ppermute x8, starting transfers between devices, swap(): return lax.ppermute(array, 'rows', pairs)  17 us
    pallas_call x5, Pallas kernels, call(): pl.pallas_call(kernel, out_shape=tuple(outs), in_specs=in_specs or [VMEM]...  8.28 us
    unnamed x12, local copies, waits for them, and re-layouts  5.55 us
    ppermute x8, waiting for transfers between devices, swap(): return lax.ppermute(array, 'rows', pairs)  2.23 us
  transfers between devices with their start and end apart: 8, of which 2 were waited for; matrix products, arithmetic and copies ran while one was open for 0% of the time, Pallas kernels for 11%

profile of v2, /device:TPU:0, one launch (start us, length us, event | category | flops | bytes accessed | tf_op | source)
XLA Modules:
  0.0 33.8 jit_solution(3742203445756083631)
XLA Ops:
  0.6 0.0 copy-start
  0.6 0.9 %copy-done = bf16[16,24,256]{2,1,0:T(8,128)(2,1)S(1)} copy-done((bf16[16,24,256]{2,1,0:T(8,128)(2,1)S(1)}, bf16[16,24,256]{2,1,0:T(8,128)(2,1)}, u32[]{:S(2)}) %copy-start) | copy-done | bytes 196632
  1.6 0.0 copy-start.2
  1.6 0.9 %copy-done.2 = bf16[16,24,256]{2,1,0:T(8,128)(2,1)S(1)} copy-done((bf16[16,24,256]{2,1,0:T(8,128)(2,1)S(1)}, bf16[16,24,256]{2,1,0:T(8,128)(2,1)}, u32[]{:S(2)}) %copy-start.2) | copy-done | bytes 196632
  2.5 1.2 %prepare.1 = (bf16[416,256]{1,0:T(8,128)(2,1)S(1)}, bf16[384,256]{1,0:T(8,128)(2,1)S(1)}) custom-call(bf16[384,256]{1,0:T(8,128)(2,1)S(1)} %bitcast.8, bf16[384,256]{1,0:T(8,128)(2,1)S(1)} %bitcast.10, bf16[2,16,256]{2,1,0:T(8,128)(2,1)} %refs_5_.1), custom_call_target="tpu_custom_call" | custom-call | bytes 819200 | tf_op jit(solution)/shard_map/prepare/pallas_call | solution.py:342
  3.7 3.1 %collective-permute-start = (bf16[416,256]{1,0:T(8,128)(2,1)S(1)}, bf16[416,256]{1,0:T(8,128)(2,1)S(1)}, u32[]{:S(2)}, u32[]{:S(2)}) collective-permute-start(bf16[416,256]{1,0:T(8,128)(2,1)S(1)} %get-tuple-element.38), channel_id=1, source_target_pairs={{0,4},{4,0},{8,12},{12,8},{1,5},{5,1},{9,13},{13,9},{2,6},{6,2},{1... | collective-permute-start | bytes 638984 | tf_op jit(solution)/shard_map/ppermute | solution.py:20
  6.8 0.7 %collective-permute-start.1 = (bf16[384,256]{1,0:T(8,128)(2,1)S(1)}, bf16[384,256]{1,0:T(8,128)(2,1)S(1)}, u32[]{:S(2)}, u32[]{:S(2)}) collective-permute-start(bf16[384,256]{1,0:T(8,128)(2,1)S(1)} %get-tuple-element.39), channel_id=1, source_target_pairs={{4,8},{8,4},{5,9},{9,5},{6,10},{10,6},{7,11},{11,7},{20,24},{24,20... | collective-permute-start | bytes 589832 | tf_op jit(solution)/shard_map/ppermute | solution.py:20
  7.5 3.9 %collective-permute-start.2 = (bf16[2,16,256]{2,1,0:T(8,128)(2,1)}, bf16[2,16,256]{2,1,0:T(8,128)(2,1)S(1)}, u32[]{:S(2)}, u32[]{:S(2)}) collective-permute-start(bf16[2,16,256]{2,1,0:T(8,128)(2,1)} %refs_5_.1), channel_id=1, source_target_pairs={{0,8},{4,12},{8,0},{12,4},{1,9},{5,13},{9,1},{13,5},{2,10},{6,14},... | collective-permute-start | bytes 49160 | tf_op jit(solution)/shard_map/ppermute | solution.py:20
  11.4 2.9 %collective-permute-start.3 = (bf16[2,16,256]{2,1,0:T(8,128)(2,1)}, bf16[2,16,256]{2,1,0:T(8,128)(2,1)S(1)}, u32[]{:S(2)}, u32[]{:S(2)}) collective-permute-start(bf16[2,16,256]{2,1,0:T(8,128)(2,1)} %refs_5_.1), channel_id=1, source_target_pairs={{0,12},{4,8},{8,4},{12,0},{1,13},{5,9},{9,5},{13,1},{2,14},{6,10},... | collective-permute-start | bytes 49160 | tf_op jit(solution)/shard_map/ppermute | solution.py:20
  14.3 0.0 copy-start.1
  14.3 0.9 %copy-done.1 = bf16[16,24,256]{2,1,0:T(8,128)(2,1)S(1)} copy-done((bf16[16,24,256]{2,1,0:T(8,128)(2,1)S(1)}, bf16[16,24,256]{2,1,0:T(8,128)(2,1)}, u32[]{:S(2)}) %copy-start.1) | copy-done | bytes 196632
  15.2 0.0 copy-start.3
  15.3 0.9 %copy-done.3 = bf16[16,24,256]{2,1,0:T(8,128)(2,1)S(1)} copy-done((bf16[16,24,256]{2,1,0:T(8,128)(2,1)S(1)}, bf16[16,24,256]{2,1,0:T(8,128)(2,1)}, u32[]{:S(2)}) %copy-start.3) | copy-done | bytes 196632
  16.2 0.0 copy-start.4
  16.2 0.9 %copy-done.4 = bf16[16,24,256]{2,1,0:T(8,128)(2,1)S(1)} copy-done((bf16[16,24,256]{2,1,0:T(8,128)(2,1)S(1)}, bf16[16,24,256]{2,1,0:T(8,128)(2,1)}, u32[]{:S(2)}) %copy-start.4) | copy-done | bytes 196632
  17.1 0.0 copy-start.5
  17.1 0.9 %copy-done.5 = bf16[16,24,256]{2,1,0:T(8,128)(2,1)S(1)} copy-done((bf16[16,24,256]{2,1,0:T(8,128)(2,1)S(1)}, bf16[16,24,256]{2,1,0:T(8,128)(2,1)}, u32[]{:S(2)}) %copy-start.5) | copy-done | bytes 196632
  18.0 1.1 %own.1 = (bf16[6,256,256]{2,1,0:T(8,128)(2,1)S(1)}, bf16[6,256,256]{2,1,0:T(8,128)(2,1)S(1)}, bf16[256,384]{1,0:T(8,128)(2,1)S(1)}, bf16[256,384]{1,0:T(8,128)(2...) custom-call(bf16[384,256]{1,0:T(8,128)(2,1)S(1)} %bitcast.12, ...), custom_call_target="tpu_custom_call" | custom-call | flops 603979776 | bytes 6340608 | tf_op jit(solution)/shard_map/own/pallas_call | solution.py:342
  19.2 0.0 collective-permute-done.2.refs_6_
  19.2 0.0 collective-permute-done.3.refs_7_
  19.2 0.0 collective-permute-done.1.refs_4_
  19.2 0.0 collective-permute-done.refs_3_
  19.2 2.7 %far.1 = (f32[6,8,256]{2,1,0:T(8,128)S(1)}, bf16[6,256,256]{2,1,0:T(8,128)(2,1)S(1)}, bf16[6,256,256]{2,1,0:T(8,128)(2,1)S(1)}, bf16[2,256,256]{2,1,0:T(8,128)(2...) custom-call(bf16[6,256,256]{2,1,0:T(8,128)(2,1)S(1)} %get-tuple-elem, ...), custom_call_target="tpu_custom_call" | custom-call | flops 805306368 | bytes 4702208 | tf_op jit(solution)/shard_map/far/pallas_call | solution.py:342
  21.9 0.1 collective-permute-start.4
  22.0 0.7 %collective-permute-start.5 = (bf16[384,256]{1,0:T(8,128)(2,1)S(1)}, bf16[384,256]{1,0:T(8,128)(2,1)S(1)}, u32[]{:S(2)}, u32[]{:S(2)}) collective-permute-start(bf16[384,256]{1,0:T(8,128)(2,1)S(1)} %get-tuple-element.50), channel_id=1, source_target_pairs={{4,8},{8,4},{5,9},{9,5},{6,10},{10,6},{7,11},{11,7},{20,24},{24,20... | collective-permute-start | bytes 589832 | tf_op jit(solution)/shard_map/ppermute | solution.py:20
  22.7 4.8 %collective-permute-start.6 = (bf16[2,16,256]{2,1,0:T(8,128)(2,1)S(1)}, bf16[2,16,256]{2,1,0:T(8,128)(2,1)S(1)}, u32[]{:S(2)}, u32[]{:S(2)}) collective-permute-start(bf16[2,16,256]{2,1,0:T(8,128)(2,1)S(1)} %get-tuple-element.52), channel_id=1, source_target_pairs={{0,8},{4,12},{8,0},{12,4},{1,9},{5,13},{9,1},{13,5},{2,10},{6,14},... | collective-permute-start | bytes 49160 | tf_op jit(solution)/shard_map/ppermute | solution.py:20
  27.4 0.9 %collective-permute-start.7 = (bf16[2,16,256]{2,1,0:T(8,128)(2,1)S(1)}, bf16[2,16,256]{2,1,0:T(8,128)(2,1)S(1)}, u32[]{:S(2)}, u32[]{:S(2)}) collective-permute-start(bf16[2,16,256]{2,1,0:T(8,128)(2,1)S(1)} %get-tuple-element.53), channel_id=1, source_target_pairs={{0,12},{4,8},{8,4},{12,0},{1,13},{5,9},{9,5},{13,1},{2,14},{6,10},... | collective-permute-start | bytes 49160 | tf_op jit(solution)/shard_map/ppermute | solution.py:20
  28.4 2.4 %rest.1 = (bf16[384,256]{1,0:T(8,128)(2,1)}, bf16[384,256]{1,0:T(8,128)(2,1)}, f32[3,128,256]{2,1,0:T(8,128)S(1)}, f32[3,128,256]{2,1,0:T(8,128)S(1)}) custom-call(bf16[6,256,256]{2,1,0:T(8,128)(2,1)S(1)} %get-tuple-element.31.refs_0_.qbd_ref, bf16[6,256,256]{2,1,0:T(8,128)(2,1)S(1)} %get-tuple-element.32.refs_1_.gbd_ref, ...), custom_call_target="tpu_custom_call" | custom-call | flops 1207959552 | bytes 8830976 | tf_op jit(solution)/shard_map/rest/pallas_call | solution.py:342
  30.8 0.8 %collective-permute-done.6.refs_1_ = bf16[2,16,256]{2,1,0:T(8,128)(2,1)S(1)} collective-permute-done((bf16[2,16,256]{2,1,0:T(8,128)(2,1)S(1)}, bf16[2,16,256]{2,1,0:T(8,128)(2,1)S(1)}, u32[]{:S(2)}, u32[]{:S(2)}) %collective-permute-start.6) | collective-permute-done | bytes 16416 | tf_op jit(solution)/shard_map/ppermute | solution.py:20
  31.6 1.4 %collective-permute-done.7.refs_2_ = bf16[2,16,256]{2,1,0:T(8,128)(2,1)S(1)} collective-permute-done((bf16[2,16,256]{2,1,0:T(8,128)(2,1)S(1)}, bf16[2,16,256]{2,1,0:T(8,128)(2,1)S(1)}, u32[]{:S(2)}, u32[]{:S(2)}) %collective-permute-start.7) | collective-permute-done | bytes 16416 | tf_op jit(solution)/shard_map/ppermute | solution.py:20
  33.0 0.0 collective-permute-done.5.b_ref
  33.0 0.0 collective-permute-done.4.a_ref
  33.0 0.8 %finish.1 = (bf16[384,256]{1,0:T(8,128)(2,1)}, bf16[384,256]{1,0:T(8,128)(2,1)}, f32[2,16,256]{2,1,0:T(8,128)}) custom-call(f32[3,128,256]{2,1,0:T(8,128)S(1)} %get-tuple-element.47.dk_ref, f32[3,128,256]{2,1,0:T(8,128)S(1)} %get-tuple-element.48.dv_ref, bf16[416,256]{1,0:T(8,128)(2,1)S(1)} %collective-permute-done.4.a_ref, ...), custom_call_target="tpu_custom_call" | custom-call | bytes 1687552 | tf_op jit(solution)/shard_map/finish/pallas_call | solution.py:342
Async XLA Ops:
  0.6 0.9 %copy-start = (bf16[16,24,256]{2,1,0:T(8,128)(2,1)S(1)}, bf16[16,24,256]{2,1,0:T(8,128)(2,1)}, u32[]{:S(2)}) copy-start(bf16[16,24,256]{2,1,0:T(8,128)(2,1)} %param.6) | copy-start | bytes 589828
  1.6 0.9 %copy-start.2 = (bf16[16,24,256]{2,1,0:T(8,128)(2,1)S(1)}, bf16[16,24,256]{2,1,0:T(8,128)(2,1)}, u32[]{:S(2)}) copy-start(bf16[16,24,256]{2,1,0:T(8,128)(2,1)} %param.7) | copy-start | bytes 589828
  3.7 15.5 %collective-permute-start = (bf16[416,256]{1,0:T(8,128)(2,1)S(1)}, bf16[416,256]{1,0:T(8,128)(2,1)S(1)}, u32[]{:S(2)}, u32[]{:S(2)}) collective-permute-start(bf16[416,256]{1,0:T(8,128)(2,1)S(1)} %get-tuple-element.38), channel_id=1, source_target_pairs={{0,4},{4,0},{8,12},{12,8},{1,5},{5,1},{9,13},{13,9},{2,6},{6,2},{1... | collective-permute-start | bytes 638984 | tf_op jit(solution)/shard_map/ppermute | solution.py:20
  6.8 12.4 %collective-permute-start.1 = (bf16[384,256]{1,0:T(8,128)(2,1)S(1)}, bf16[384,256]{1,0:T(8,128)(2,1)S(1)}, u32[]{:S(2)}, u32[]{:S(2)}) collective-permute-start(bf16[384,256]{1,0:T(8,128)(2,1)S(1)} %get-tuple-element.39), channel_id=1, source_target_pairs={{4,8},{8,4},{5,9},{9,5},{6,10},{10,6},{7,11},{11,7},{20,24},{24,20... | collective-permute-start | bytes 589832 | tf_op jit(solution)/shard_map/ppermute | solution.py:20
  7.5 11.7 %collective-permute-start.2 = (bf16[2,16,256]{2,1,0:T(8,128)(2,1)}, bf16[2,16,256]{2,1,0:T(8,128)(2,1)S(1)}, u32[]{:S(2)}, u32[]{:S(2)}) collective-permute-start(bf16[2,16,256]{2,1,0:T(8,128)(2,1)} %refs_5_.1), channel_id=1, source_target_pairs={{0,8},{4,12},{8,0},{12,4},{1,9},{5,13},{9,1},{13,5},{2,10},{6,14},... | collective-permute-start | bytes 49160 | tf_op jit(solution)/shard_map/ppermute | solution.py:20
  11.4 7.8 %collective-permute-start.3 = (bf16[2,16,256]{2,1,0:T(8,128)(2,1)}, bf16[2,16,256]{2,1,0:T(8,128)(2,1)S(1)}, u32[]{:S(2)}, u32[]{:S(2)}) collective-permute-start(bf16[2,16,256]{2,1,0:T(8,128)(2,1)} %refs_5_.1), channel_id=1, source_target_pairs={{0,12},{4,8},{8,4},{12,0},{1,13},{5,9},{9,5},{13,1},{2,14},{6,10},... | collective-permute-start | bytes 49160 | tf_op jit(solution)/shard_map/ppermute | solution.py:20
  14.3 0.9 %copy-start.1 = (bf16[16,24,256]{2,1,0:T(8,128)(2,1)S(1)}, bf16[16,24,256]{2,1,0:T(8,128)(2,1)}, u32[]{:S(2)}) copy-start(bf16[16,24,256]{2,1,0:T(8,128)(2,1)} %param.6) | copy-start | bytes 589828
  15.2 0.9 %copy-start.3 = (bf16[16,24,256]{2,1,0:T(8,128)(2,1)S(1)}, bf16[16,24,256]{2,1,0:T(8,128)(2,1)}, u32[]{:S(2)}) copy-start(bf16[16,24,256]{2,1,0:T(8,128)(2,1)} %param.7) | copy-start | bytes 589828
  16.2 0.9 %copy-start.4 = (bf16[16,24,256]{2,1,0:T(8,128)(2,1)S(1)}, bf16[16,24,256]{2,1,0:T(8,128)(2,1)}, u32[]{:S(2)}) copy-start(bf16[16,24,256]{2,1,0:T(8,128)(2,1)} %param.5) | copy-start | bytes 589828
  17.1 0.9 %copy-start.5 = (bf16[16,24,256]{2,1,0:T(8,128)(2,1)S(1)}, bf16[16,24,256]{2,1,0:T(8,128)(2,1)}, u32[]{:S(2)}) copy-start(bf16[16,24,256]{2,1,0:T(8,128)(2,1)} %param.9) | copy-start | bytes 589828
  21.9 11.1 %collective-permute-start.4 = (bf16[416,256]{1,0:T(8,128)(2,1)S(1)}, bf16[416,256]{1,0:T(8,128)(2,1)S(1)}, u32[]{:S(2)}, u32[]{:S(2)}) collective-permute-start(bf16[416,256]{1,0:T(8,128)(2,1)S(1)} %get-tuple-element.49), channel_id=1, source_target_pairs={{0,4},{4,0},{8,12},{12,8},{1,5},{5,1},{9,13},{13,9},{2,6},{6,2},{1... | collective-permute-start | bytes 638984 | tf_op jit(solution)/shard_map/ppermute | solution.py:20
  22.0 11.0 %collective-permute-start.5 = (bf16[384,256]{1,0:T(8,128)(2,1)S(1)}, bf16[384,256]{1,0:T(8,128)(2,1)S(1)}, u32[]{:S(2)}, u32[]{:S(2)}) collective-permute-start(bf16[384,256]{1,0:T(8,128)(2,1)S(1)} %get-tuple-element.50), channel_id=1, source_target_pairs={{4,8},{8,4},{5,9},{9,5},{6,10},{10,6},{7,11},{11,7},{20,24},{24,20... | collective-permute-start | bytes 589832 | tf_op jit(solution)/shard_map/ppermute | solution.py:20
  22.7 8.9 %collective-permute-start.6 = (bf16[2,16,256]{2,1,0:T(8,128)(2,1)S(1)}, bf16[2,16,256]{2,1,0:T(8,128)(2,1)S(1)}, u32[]{:S(2)}, u32[]{:S(2)}) collective-permute-start(bf16[2,16,256]{2,1,0:T(8,128)(2,1)S(1)} %get-tuple-element.52), channel_id=1, source_target_pairs={{0,8},{4,12},{8,0},{12,4},{1,9},{5,13},{9,1},{13,5},{2,10},{6,14},... | collective-permute-start | bytes 49160 | tf_op jit(solution)/shard_map/ppermute | solution.py:20
  27.4 5.5 %collective-permute-start.7 = (bf16[2,16,256]{2,1,0:T(8,128)(2,1)S(1)}, bf16[2,16,256]{2,1,0:T(8,128)(2,1)S(1)}, u32[]{:S(2)}, u32[]{:S(2)}) collective-permute-start(bf16[2,16,256]{2,1,0:T(8,128)(2,1)S(1)} %get-tuple-element.53), channel_id=1, source_target_pairs={{0,12},{4,8},{8,4},{12,0},{1,13},{5,9},{9,5},{13,1},{2,14},{6,10},... | collective-permute-start | bytes 49160 | tf_op jit(solution)/shard_map/ppermute | solution.py:20

commit v3 on v2

--- a/solution.py
+++ b/solution.py
@@ -11,9 +11,11 @@
 TILE = 8
 PATCH = TILE * TILE
 FACTOR = HEAD ** (-0.5)
+HEAVY = 20_000_000_000
 BF = jnp.bfloat16
 F32 = jnp.float32
 VMEM = pl.BlockSpec(memory_space=pltpu.VMEM)
+HBM = pl.BlockSpec(memory_space=pltpu.HBM)
 
 
 def swap(array, pairs):
@@ -100,22 +102,19 @@
     return max(c - 1, 0), min(c + 2, tile_cols)
 
 
-def own_kernel(
-    tile_cols,
-    q_ref,
-    g_ref,
-    k_ref,
-    v_ref,
-    qbd_ref,
-    gbd_ref,
-    kt_ref,
-    vt_ref,
-    exp_ref,
-    dw_ref,
-    stat_ref,
-    kc_ref,
-    vc_ref,
-):
+def own_kernel(tile_cols, split_regs, *refs):
+    whole, regs, refs = refs[:4], refs[4 : 7 if split_regs else 5], refs[7 if split_regs else 5 :]
+    qbd_ref, gbd_ref, kt_ref, vt_ref, exp_ref, dw_ref, stat_ref, regx_ref, kc_ref, vc_ref = refs[:10]
+    held, sems = refs[10:14], refs[14]
+    copies = [pltpu.make_async_copy(x, y, sems.at[n]) for n, (x, y) in enumerate(zip(whole, held))]
+    for copy in copies:
+        copy.start()
+    own = regs[0].shape[1]
+    for n, ref in enumerate(regs):
+        regx_ref[:, n * own : (n + 1) * own] = ref[...]
+    for copy in copies:
+        copy.wait()
+    q_ref, g_ref, k_ref, v_ref = held
     heads = q_ref.shape[1] // HEAD
     line = tile_cols * PATCH
     tile_rows = q_ref.shape[0] // line
@@ -149,13 +148,9 @@
 
 
 def far_kernel(tile_cols, split_regs, *refs):
-    qbd_ref, gbd_ref, stat_ref, a_ref, b_ref = refs[:5]
-    if split_regs:
-        own_ref, two_ref, three_ref = refs[5:8]
-        refs = refs[8:]
-    else:
-        all_ref = refs[5]
-        refs = refs[6:]
+    qbd_ref, gbd_ref, stat_ref, regx_ref, a_ref, b_ref = refs[:6]
+    refs = refs[6:]
+    cut = (a_ref.shape[0] - b_ref.shape[0]) // 2
     final_ref, px_ref, dsx_ref, kx_ref, vx_ref, back_a_ref, back_b_ref = refs[:7]
     reg_outs = refs[7:]
     feature = a_ref.shape[1]
@@ -169,12 +164,10 @@
         from_b = b_ref[n * edge : (n + 1) * edge]
         top = column_tiles(jnp.where(even, from_b, from_a), tile_cols)
         bottom = column_tiles(jnp.where(even, from_a, from_b), tile_cols)
+        regs = regx_ref[n]
         if split_regs:
-            cut = own_ref.shape[1]
             base = 2 * edge + n * cut
-            regs = jnp.concatenate([own_ref[n], a_ref[base : base + cut], two_ref[n], three_ref[n]], axis=0)
-        else:
-            regs = all_ref[n]
+            regs = jnp.concatenate([regs, a_ref[base : base + cut]], axis=0)
         for t, halo in enumerate((top, bottom)):
             ref[t, :edge] = jnp.concatenate(halo, axis=0).astype(BF)
             ref[t, edge:] = regs
@@ -232,9 +225,9 @@
         if split_regs:
             base = 2 * edge + n * cut
             reg_outs[0][n] = reg[:cut]
-            back_a_ref[base : base + cut] = reg[cut : 2 * cut].astype(BF)
-            reg_outs[1][n] = reg[2 * cut : 3 * cut].astype(BF)
-            reg_outs[2][n] = reg[3 * cut :].astype(BF)
+            reg_outs[1][n] = reg[cut : 2 * cut].astype(BF)
+            reg_outs[2][n] = reg[2 * cut : 3 * cut].astype(BF)
+            back_a_ref[base : base + cut] = reg[3 * cut :].astype(BF)
         else:
             reg_outs[0][n] = reg
 
@@ -252,11 +245,12 @@
     dsx_ref,
     kx_ref,
     vx_ref,
-    o_ref,
-    dq_ref,
-    dk_ref,
-    dv_ref,
+    *refs,
 ):
+    if len(refs) > 4:
+        own_ref, two_ref, three_ref, *refs = refs
+        refs[4][...] = own_ref[...] + two_ref[...].astype(F32) + three_ref[...].astype(F32)
+    o_ref, dq_ref, dk_ref, dv_ref = refs[:4]
     feature = kt_ref.shape[0]
     heads = feature // HEAD
     line = tile_cols * PATCH
@@ -294,43 +288,30 @@
 
 def finish_kernel(dk_ref, dv_ref, a_ref, b_ref, *refs, split_regs):
     if split_regs:
-        dreg_ref, c_ref, e_ref = refs[:3]
-        refs = refs[3:]
+        dreg_ref, *refs = refs
     gk_ref, gv_ref = refs[:2]
-    even = lax.rem(lax.axis_index("rows"), 2) == 0
+    me = lax.axis_index("rows")
+    even = lax.rem(me, 2) == 0
+    has_top = me > 0
+    has_bottom = me < lax.axis_size("rows") - 1
     tile_cols = dk_ref.shape[0]
     edge = b_ref.shape[0] // 2
     for n, (acc_ref, out_ref) in enumerate(((dk_ref, gk_ref), (dv_ref, gv_ref))):
         from_a = a_ref[n * edge : (n + 1) * edge]
         from_b = b_ref[n * edge : (n + 1) * edge]
-        top = jnp.where(even, from_b, from_a).astype(F32)
-        bottom = jnp.where(even, from_a, from_b).astype(F32)
+        top = jnp.where(has_top, jnp.where(even, from_b, from_a).astype(F32), 0.0)
+        bottom = jnp.where(has_bottom, jnp.where(even, from_a, from_b).astype(F32), 0.0)
         rows = acc_ref.shape[1]
         columns = []
         for c in range(tile_cols):
-            high = top[c * PATCH : (c + 1) * PATCH]
-            low = bottom[c * PATCH : (c + 1) * PATCH]
-            if rows == PATCH:
-                columns.append(acc_ref[c] + high + low)
-                continue
-            columns.append(
-                jnp.concatenate(
-                    [acc_ref[c, :PATCH] + high, acc_ref[c, PATCH : rows - PATCH], acc_ref[c, rows - PATCH :] + low]
-                    if rows > 2 * PATCH
-                    else [acc_ref[c, :PATCH] + high, acc_ref[c, PATCH:] + low],
-                    axis=0,
-                )
-            )
+            high = acc_ref[c, :PATCH] + top[c * PATCH : (c + 1) * PATCH]
+            low = acc_ref[c, rows - PATCH :] + bottom[c * PATCH : (c + 1) * PATCH]
+            columns.append(jnp.concatenate([high, low], axis=0))
         out_ref[...] = patch_order(columns).astype(BF)
         if split_regs:
-            cut = c_ref.shape[1]
+            cut = dreg_ref.shape[1]
             base = 2 * edge + n * cut
-            refs[2][n] = (
-                dreg_ref[n, :cut]
-                + a_ref[base : base + cut].astype(F32)
-                + c_ref[n].astype(F32)
-                + e_ref[n].astype(F32)
-            )
+            refs[2][n] = dreg_ref[n] + a_ref[base : base + cut].astype(F32)
 
 
 def shape(dims, dtype):
@@ -377,7 +358,7 @@
         (k, v, registers),
         (shape((2 * edge + extra, feature), BF), shape((2 * edge, feature), BF)),
         0,
-        in_specs=[pl.BlockSpec(memory_space=pl.ANY)] * 3,
+        in_specs=[HBM] * 3,
         scratch=[pltpu.SemaphoreType.DMA((6,))],
     )
     got_b = swap(pay_b, pairs_b(count))
@@ -387,10 +368,10 @@
     rows = tile_rows * PATCH
     most = min(3, tile_cols) * rows
     window = edge + reg_count
-    qbd, gbd, kt, vt, exps, dw, stats = call(
-        functools.partial(own_kernel, tile_cols),
+    qbd, gbd, kt, vt, exps, dw, stats, regx = call(
+        functools.partial(own_kernel, tile_cols, split_regs),
         "own",
-        (q, g, k, v),
+        (q, g, k, v) + regs,
         (
             shape((tiles, feature, feature), BF),
             shape((tiles, feature, feature), BF),
@@ -399,9 +380,11 @@
             shape((tiles, most, feature), F32),
             shape((tiles, most, feature), BF),
             shape((tiles, 8, feature), F32),
+            shape((2, len(regs) * regs[0].shape[1], feature), BF),
         ),
-        4 * tiles * most * feature * feature,
-        scratch=[pltpu.VMEM((total, feature), BF)] * 2,
+        HEAVY,
+        in_specs=[HBM] * 4 + [VMEM] * len(regs),
+        scratch=[pltpu.VMEM((total, feature), BF)] * 6 + [pltpu.SemaphoreType.DMA((4,))],
     )
     if split_regs:
         reg_shapes = (
@@ -414,7 +397,7 @@
     final, px, dsx, kx, vx, back_a, back_b, *back_regs = call(
         functools.partial(far_kernel, tile_cols, split_regs),
         "far",
-        (qbd, gbd, stats, got_a, got_b) + regs,
+        (qbd, gbd, stats, regx, got_a, got_b),
         (
             shape((tiles, 8, feature), F32),
             shape((tiles, window, feature), BF),
@@ -435,22 +418,23 @@
     else:
         rest = ()
         last_shapes = ()
-    attended, grad_query, dk, dv = call(
+    attended, grad_query, dk, dv, *reg_part = call(
         functools.partial(rest_kernel, tile_cols),
         "rest",
-        (qbd, gbd, kt, vt, exps, dw, final, px, dsx, kx, vx),
+        (qbd, gbd, kt, vt, exps, dw, final, px, dsx, kx, vx) + rest,
         (
             shape((total, feature), BF),
             shape((total, feature), BF),
             shape((tile_cols, rows, feature), F32),
             shape((tile_cols, rows, feature), F32),
-        ),
-        8 * tiles * most * feature * feature,
+        )
+        + last_shapes,
+        HEAVY,
     )
     outs = call(
         functools.partial(finish_kernel, split_regs=split_regs),
         "finish",
-        (dk, dv, back_from_a, back_from_b) + rest,
+        (dk, dv, back_from_a, back_from_b) + tuple(reg_part),
         (shape((total, feature), BF), shape((total, feature), BF)) + last_shapes,
         0,
     )

time: 34.2 us -> 33.6 us (0.982)
  local copies, waits for them, and re-layouts: 5.55 us -> 6.99 us
  starting transfers between devices: 17 us -> 16.1 us
  waiting for transfers between devices: 2.23 us -> 1.5 us
  Pallas kernels: 8.28 us -> 7.9 us
    unnamed x12 -> x16, local copies, waits for them, and re-layouts: 5.55 us -> 6.99 us
    ppermute x8, starting transfers between devices: 17 us -> 16.1 us  [swap(): return lax.ppermute(array, 'rows', pairs)]
    ppermute x8, waiting for transfers between devices: 2.23 us -> 1.5 us  [swap(): return lax.ppermute(array, 'rows', pairs)]
    pallas_call x5, Pallas kernels: 8.28 us -> 7.9 us  [call(): pl.pallas_call(kernel, out_shape=tuple(outs), in_specs=in_specs or [VMEM]...]
  transfers between devices with their start and end apart: 8 -> 8, of which waited for: 2 -> 2; matrix products, arithmetic and copies ran while one was open for 0% -> 0% of each run, Pallas kernels for 11% -> 15%
where the time goes in v3:
time: 33.6 us; the launch traced here: 33.2 us
  starting transfers between devices  16.1 us (48%)
  Pallas kernels  7.9 us (24%)
  local copies, waits for them, and re-layouts  6.99 us (21%)
  waiting for transfers between devices  1.5 us (4%)
  between operations  0.71 us (2%)
    ppermute x8, starting transfers between devices, swap(): return lax.ppermute(array, 'rows', pairs)  16.1 us
    pallas_call x5, Pallas kernels, call(): pl.pallas_call(kernel, out_shape=tuple(outs), in_specs=in_specs or [VMEM]...  7.9 us
    unnamed x16, local copies, waits for them, and re-layouts  6.99 us
    ppermute x8, waiting for transfers between devices, swap(): return lax.ppermute(array, 'rows', pairs)  1.5 us
  transfers between devices with their start and end apart: 8, of which 2 were waited for; matrix products, arithmetic and copies ran while one was open for 0% of the time, Pallas kernels for 15%

profile of v3, /device:TPU:0, one launch (start us, length us, event | category | flops | bytes accessed | tf_op | source)
XLA Modules:
  0.0 33.2 jit_solution(2408355237375022285)
XLA Ops:
  0.6 5.1 %collective-permute-start.1 = (bf16[2,16,256]{2,1,0:T(8,128)(2,1)}, bf16[2,16,256]{2,1,0:T(8,128)(2,1)S(1)}, u32[]{:S(2)}, u32[]{:S(2)}) collective-permute-start(bf16[2,16,256]{2,1,0:T(8,128)(2,1)} %reg_ref.1), channel_id=1, source_target_pairs={{0,12},{4,8},{8,4},{12,0},{1,13},{5,9},{9,5},{13,1},{2,14},{6,10},... | collective-permute-start | bytes 49160 | tf_op jit(solution)/shard_map/ppermute | solution.py:22
  5.7 0.0 collective-permute-start
  5.7 0.0 copy-start
  5.8 0.9 %copy-done = bf16[16,24,256]{2,1,0:T(8,128)(2,1)S(1)} copy-done((bf16[16,24,256]{2,1,0:T(8,128)(2,1)S(1)}, bf16[16,24,256]{2,1,0:T(8,128)(2,1)}, u32[]{:S(2)}) %copy-start) | copy-done | bytes 196632
  6.7 0.0 copy-start.2
  6.7 0.9 %copy-done.2 = bf16[16,24,256]{2,1,0:T(8,128)(2,1)S(1)} copy-done((bf16[16,24,256]{2,1,0:T(8,128)(2,1)S(1)}, bf16[16,24,256]{2,1,0:T(8,128)(2,1)}, u32[]{:S(2)}) %copy-start.2) | copy-done | bytes 196632
  7.6 0.0 copy-start.4
  7.6 0.7 %copy-done.4 = bf16[2,16,256]{2,1,0:T(8,128)(2,1)S(1)} copy-done((bf16[2,16,256]{2,1,0:T(8,128)(2,1)S(1)}, bf16[2,16,256]{2,1,0:T(8,128)(2,1)}, u32[]{:S(2)}) %copy-start.4) | copy-done | bytes 16408
  8.3 0.6 %prepare.1 = (bf16[416,256]{1,0:T(8,128)(2,1)S(1)}, bf16[384,256]{1,0:T(8,128)(2,1)S(1)}) custom-call(bf16[384,256]{1,0:T(8,128)(2,1)S(1)} %bitcast.8, bf16[384,256]{1,0:T(8,128)(2,1)S(1)} %bitcast.10, bf16[2,16,256]{2,1,0:T(8,128)(2,1)S(1)} %copy-done.4), custom_call_target="tpu_custom_call" | custom-call | bytes 819200 | tf_op jit(solution)/shard_map/prepare/pallas_call | solution.py:323
  8.9 0.7 %collective-permute-start.3 = (bf16[384,256]{1,0:T(8,128)(2,1)S(1)}, bf16[384,256]{1,0:T(8,128)(2,1)S(1)}, u32[]{:S(2)}, u32[]{:S(2)}) collective-permute-start(bf16[384,256]{1,0:T(8,128)(2,1)S(1)} %get-tuple-element.42), channel_id=1, source_target_pairs={{4,8},{8,4},{5,9},{9,5},{6,10},{10,6},{7,11},{11,7},{20,24},{24,20... | collective-permute-start | bytes 589832 | tf_op jit(solution)/shard_map/ppermute | solution.py:22
  9.6 4.8 %collective-permute-start.2 = (bf16[416,256]{1,0:T(8,128)(2,1)S(1)}, bf16[416,256]{1,0:T(8,128)(2,1)S(1)}, u32[]{:S(2)}, u32[]{:S(2)}) collective-permute-start(bf16[416,256]{1,0:T(8,128)(2,1)S(1)} %get-tuple-element.41), channel_id=1, source_target_pairs={{0,4},{4,0},{8,12},{12,8},{1,5},{5,1},{9,13},{13,9},{2,6},{6,2},{1... | collective-permute-start | bytes 638984 | tf_op jit(solution)/shard_map/ppermute | solution.py:22
  14.4 0.0 collective-permute-done.1.refs_6_
  14.4 0.0 collective-permute-done.refs_5_
  14.4 0.0 copy-start.1
  14.4 0.9 %copy-done.1 = bf16[16,24,256]{2,1,0:T(8,128)(2,1)S(1)} copy-done((bf16[16,24,256]{2,1,0:T(8,128)(2,1)S(1)}, bf16[16,24,256]{2,1,0:T(8,128)(2,1)}, u32[]{:S(2)}) %copy-start.1) | copy-done | bytes 196632
  15.3 0.0 copy-start.3
  15.3 0.9 %copy-done.3 = bf16[16,24,256]{2,1,0:T(8,128)(2,1)S(1)} copy-done((bf16[16,24,256]{2,1,0:T(8,128)(2,1)S(1)}, bf16[16,24,256]{2,1,0:T(8,128)(2,1)}, u32[]{:S(2)}) %copy-start.3) | copy-done | bytes 196632
  16.2 0.0 copy-start.5
  16.2 0.7 %copy-done.5 = bf16[2,16,256]{2,1,0:T(8,128)(2,1)S(1)} copy-done((bf16[2,16,256]{2,1,0:T(8,128)(2,1)S(1)}, bf16[2,16,256]{2,1,0:T(8,128)(2,1)}, u32[]{:S(2)}) %copy-start.5) | copy-done | bytes 16408
  16.9 0.0 copy-start.6
  16.9 0.9 %copy-done.6 = bf16[16,24,256]{2,1,0:T(8,128)(2,1)S(1)} copy-done((bf16[16,24,256]{2,1,0:T(8,128)(2,1)S(1)}, bf16[16,24,256]{2,1,0:T(8,128)(2,1)}, u32[]{:S(2)}) %copy-start.6) | copy-done | bytes 196632
  17.9 0.0 copy-start.7
  17.9 0.9 %copy-done.7 = bf16[16,24,256]{2,1,0:T(8,128)(2,1)S(1)} copy-done((bf16[16,24,256]{2,1,0:T(8,128)(2,1)S(1)}, bf16[16,24,256]{2,1,0:T(8,128)(2,1)}, u32[]{:S(2)}) %copy-start.7) | copy-done | bytes 196632
  18.8 2.1 %own.1 = (bf16[6,256,256]{2,1,0:T(8,128)(2,1)S(1)}, bf16[6,256,256]{2,1,0:T(8,128)(2,1)S(1)}, bf16[256,384]{1,0:T(8,128)(2,1)S(1)}, bf16[256,384]{1,0:T(8,128)(2...) custom-call(bf16[384,256]{1,0:T(8,128)(2,1)S(1)} %bitcast.12, ...), custom_call_target="tpu_custom_call" | custom-call | flops 20000000000 | bytes 6438912 | tf_op jit(solution)/shard_map/own/pallas_call | solution.py:323
  20.9 0.0 collective-permute-done.3.refs_5_
  20.9 0.0 collective-permute-done.2.refs_4_
  20.9 2.0 %far.1 = (f32[6,8,256]{2,1,0:T(8,128)S(1)}, bf16[6,256,256]{2,1,0:T(8,128)(2,1)S(1)}, bf16[6,256,256]{2,1,0:T(8,128)(2,1)S(1)}, bf16[2,256,256]{2,1,0:T(8,128)(2...) custom-call(bf16[6,256,256]{2,1,0:T(8,128)(2,1)S(1)} %get-tuple-elem, ...), custom_call_target="tpu_custom_call" | custom-call | flops 805306368 | bytes 4702208 | tf_op jit(solution)/shard_map/far/pallas_call | solution.py:323
  23.0 0.1 collective-permute-start.4
  23.0 2.4 %collective-permute-start.5 = (bf16[2,16,256]{2,1,0:T(8,128)(2,1)S(1)}, bf16[2,16,256]{2,1,0:T(8,128)(2,1)S(1)}, u32[]{:S(2)}, u32[]{:S(2)}) collective-permute-start(bf16[2,16,256]{2,1,0:T(8,128)(2,1)S(1)} %get-tuple-element.50), channel_id=1, source_target_pairs={{0,12},{4,8},{8,4},{12,0},{1,13},{5,9},{9,5},{13,1},{2,14},{6,10},... | collective-permute-start | bytes 49160 | tf_op jit(solution)/shard_map/ppermute | solution.py:22
  25.4 0.7 %collective-permute-start.7 = (bf16[384,256]{1,0:T(8,128)(2,1)S(1)}, bf16[384,256]{1,0:T(8,128)(2,1)S(1)}, u32[]{:S(2)}, u32[]{:S(2)}) collective-permute-start(bf16[384,256]{1,0:T(8,128)(2,1)S(1)} %get-tuple-element.56), channel_id=1, source_target_pairs={{4,8},{8,4},{5,9},{9,5},{6,10},{10,6},{7,11},{11,7},{20,24},{24,20... | collective-permute-start | bytes 589832 | tf_op jit(solution)/shard_map/ppermute | solution.py:22
  26.1 2.4 %collective-permute-start.6 = (bf16[416,256]{1,0:T(8,128)(2,1)S(1)}, bf16[416,256]{1,0:T(8,128)(2,1)S(1)}, u32[]{:S(2)}, u32[]{:S(2)}) collective-permute-start(bf16[416,256]{1,0:T(8,128)(2,1)S(1)} %get-tuple-element.55), channel_id=1, source_target_pairs={{0,4},{4,0},{8,12},{12,8},{1,5},{5,1},{9,13},{13,9},{2,6},{6,2},{1... | collective-permute-start | bytes 638984 | tf_op jit(solution)/shard_map/ppermute | solution.py:22
  28.5 0.0 collective-permute-done.4.refs_1_
  28.5 0.2 collective-permute-done.5.refs_2_
  28.7 2.4 %rest.1 = (bf16[384,256]{1,0:T(8,128)(2,1)}, bf16[384,256]{1,0:T(8,128)(2,1)}, f32[3,128,256]{2,1,0:T(8,128)S(1)}, f32[3,128,256]{2,1,0:T(8,128)S(1)}, f32[2,16,256]{2,1,0:T(8,128)S(1)}) custom-call(bf16[6,256,256]{2,1,0:T(8,128)(2,1)S(1)} %get-tuple-element.33.refs_0_.qbd_ref, bf16[6,256,256]{2,1,0:T(8,128)(2,1)S(1)} %get-tuple-element.34.refs_1_.gbd_ref, ...), custom_call_target="tpu_custom_call" | custom-call | flops 20000000000 | bytes 8929280 | tf_op jit(solution)/shard_map/rest/pallas_call | solution.py:323
  31.2 0.0 collective-permute-done.7.b_ref
  31.2 1.2 %collective-permute-done.6.a_ref = bf16[416,256]{1,0:T(8,128)(2,1)S(1)} collective-permute-done((bf16[416,256]{1,0:T(8,128)(2,1)S(1)}, bf16[416,256]{1,0:T(8,128)(2,1)S(1)}, u32[]{:S(2)}, u32[]{:S(2)}) %collective-permute-start.6) | collective-permute-done | bytes 213024 | tf_op jit(solution)/shard_map/ppermute | solution.py:22
  32.4 0.8 %finish.1 = (bf16[384,256]{1,0:T(8,128)(2,1)}, bf16[384,256]{1,0:T(8,128)(2,1)}, f32[2,16,256]{2,1,0:T(8,128)}) custom-call(f32[3,128,256]{2,1,0:T(8,128)S(1)} %get-tuple-element.53.dk_ref, f32[3,128,256]{2,1,0:T(8,128)S(1)} %get-tuple-element.54.dv_ref, bf16[416,256]{1,0:T(8,128)(2,1)S(1)} %collective-permute-done.6.a_ref, ...), custom_call_target="tpu_custom_call" | custom-call | bytes 1654784 | tf_op jit(solution)/shard_map/finish/pallas_call | solution.py:323
Async XLA Ops:
  0.6 13.7 %collective-permute-start.1 = (bf16[2,16,256]{2,1,0:T(8,128)(2,1)}, bf16[2,16,256]{2,1,0:T(8,128)(2,1)S(1)}, u32[]{:S(2)}, u32[]{:S(2)}) collective-permute-start(bf16[2,16,256]{2,1,0:T(8,128)(2,1)} %reg_ref.1), channel_id=1, source_target_pairs={{0,12},{4,8},{8,4},{12,0},{1,13},{5,9},{9,5},{13,1},{2,14},{6,10},... | collective-permute-start | bytes 49160 | tf_op jit(solution)/shard_map/ppermute | solution.py:22
  5.7 8.6 %collective-permute-start = (bf16[2,16,256]{2,1,0:T(8,128)(2,1)}, bf16[2,16,256]{2,1,0:T(8,128)(2,1)S(1)}, u32[]{:S(2)}, u32[]{:S(2)}) collective-permute-start(bf16[2,16,256]{2,1,0:T(8,128)(2,1)} %reg_ref.1), channel_id=1, source_target_pairs={{0,8},{4,12},{8,0},{12,4},{1,9},{5,13},{9,1},{13,5},{2,10},{6,14},... | collective-permute-start | bytes 49160 | tf_op jit(solution)/shard_map/ppermute | solution.py:22
  5.7 0.9 %copy-start = (bf16[16,24,256]{2,1,0:T(8,128)(2,1)S(1)}, bf16[16,24,256]{2,1,0:T(8,128)(2,1)}, u32[]{:S(2)}) copy-start(bf16[16,24,256]{2,1,0:T(8,128)(2,1)} %param.6) | copy-start | bytes 589828
  6.7 0.9 %copy-start.2 = (bf16[16,24,256]{2,1,0:T(8,128)(2,1)S(1)}, bf16[16,24,256]{2,1,0:T(8,128)(2,1)}, u32[]{:S(2)}) copy-start(bf16[16,24,256]{2,1,0:T(8,128)(2,1)} %param.7) | copy-start | bytes 589828
  7.6 0.7 %copy-start.4 = (bf16[2,16,256]{2,1,0:T(8,128)(2,1)S(1)}, bf16[2,16,256]{2,1,0:T(8,128)(2,1)}, u32[]{:S(2)}) copy-start(bf16[2,16,256]{2,1,0:T(8,128)(2,1)} %reg_ref.1) | copy-start | bytes 49156
  8.9 12.0 %collective-permute-start.3 = (bf16[384,256]{1,0:T(8,128)(2,1)S(1)}, bf16[384,256]{1,0:T(8,128)(2,1)S(1)}, u32[]{:S(2)}, u32[]{:S(2)}) collective-permute-start(bf16[384,256]{1,0:T(8,128)(2,1)S(1)} %get-tuple-element.42), channel_id=1, source_target_pairs={{4,8},{8,4},{5,9},{9,5},{6,10},{10,6},{7,11},{11,7},{20,24},{24,20... | collective-permute-start | bytes 589832 | tf_op jit(solution)/shard_map/ppermute | solution.py:22
  9.6 11.4 %collective-permute-start.2 = (bf16[416,256]{1,0:T(8,128)(2,1)S(1)}, bf16[416,256]{1,0:T(8,128)(2,1)S(1)}, u32[]{:S(2)}, u32[]{:S(2)}) collective-permute-start(bf16[416,256]{1,0:T(8,128)(2,1)S(1)} %get-tuple-element.41), channel_id=1, source_target_pairs={{0,4},{4,0},{8,12},{12,8},{1,5},{5,1},{9,13},{13,9},{2,6},{6,2},{1... | collective-permute-start | bytes 638984 | tf_op jit(solution)/shard_map/ppermute | solution.py:22
  14.4 0.9 %copy-start.1 = (bf16[16,24,256]{2,1,0:T(8,128)(2,1)S(1)}, bf16[16,24,256]{2,1,0:T(8,128)(2,1)}, u32[]{:S(2)}) copy-start(bf16[16,24,256]{2,1,0:T(8,128)(2,1)} %param.6) | copy-start | bytes 589828
  15.3 0.9 %copy-start.3 = (bf16[16,24,256]{2,1,0:T(8,128)(2,1)S(1)}, bf16[16,24,256]{2,1,0:T(8,128)(2,1)}, u32[]{:S(2)}) copy-start(bf16[16,24,256]{2,1,0:T(8,128)(2,1)} %param.7) | copy-start | bytes 589828
  16.2 0.7 %copy-start.5 = (bf16[2,16,256]{2,1,0:T(8,128)(2,1)S(1)}, bf16[2,16,256]{2,1,0:T(8,128)(2,1)}, u32[]{:S(2)}) copy-start(bf16[2,16,256]{2,1,0:T(8,128)(2,1)} %reg_ref.1) | copy-start | bytes 49156
  16.9 0.9 %copy-start.6 = (bf16[16,24,256]{2,1,0:T(8,128)(2,1)S(1)}, bf16[16,24,256]{2,1,0:T(8,128)(2,1)}, u32[]{:S(2)}) copy-start(bf16[16,24,256]{2,1,0:T(8,128)(2,1)} %param.5) | copy-start | bytes 589828
  17.9 0.9 %copy-start.7 = (bf16[16,24,256]{2,1,0:T(8,128)(2,1)S(1)}, bf16[16,24,256]{2,1,0:T(8,128)(2,1)}, u32[]{:S(2)}) copy-start(bf16[16,24,256]{2,1,0:T(8,128)(2,1)} %param.9) | copy-start | bytes 589828
  23.0 5.5 %collective-permute-start.4 = (bf16[2,16,256]{2,1,0:T(8,128)(2,1)S(1)}, bf16[2,16,256]{2,1,0:T(8,128)(2,1)S(1)}, u32[]{:S(2)}, u32[]{:S(2)}) collective-permute-start(bf16[2,16,256]{2,1,0:T(8,128)(2,1)S(1)} %get-tuple-element.49), channel_id=1, source_target_pairs={{0,8},{4,12},{8,0},{12,4},{1,9},{5,13},{9,1},{13,5},{2,10},{6,14},... | collective-permute-start | bytes 49160 | tf_op jit(solution)/shard_map/ppermute | solution.py:22
  23.0 5.7 %collective-permute-start.5 = (bf16[2,16,256]{2,1,0:T(8,128)(2,1)S(1)}, bf16[2,16,256]{2,1,0:T(8,128)(2,1)S(1)}, u32[]{:S(2)}, u32[]{:S(2)}) collective-permute-start(bf16[2,16,256]{2,1,0:T(8,128)(2,1)S(1)} %get-tuple-element.50), channel_id=1, source_target_pairs={{0,12},{4,8},{8,4},{12,0},{1,13},{5,9},{9,5},{13,1},{2,14},{6,10},... | collective-permute-start | bytes 49160 | tf_op jit(solution)/shard_map/ppermute | solution.py:22
  25.4 5.8 %collective-permute-start.7 = (bf16[384,256]{1,0:T(8,128)(2,1)S(1)}, bf16[384,256]{1,0:T(8,128)(2,1)S(1)}, u32[]{:S(2)}, u32[]{:S(2)}) collective-permute-start(bf16[384,256]{1,0:T(8,128)(2,1)S(1)} %get-tuple-element.56), channel_id=1, source_target_pairs={{4,8},{8,4},{5,9},{9,5},{6,10},{10,6},{7,11},{11,7},{20,24},{24,20... | collective-permute-start | bytes 589832 | tf_op jit(solution)/shard_map/ppermute | solution.py:22
  26.1 6.3 %collective-permute-start.6 = (bf16[416,256]{1,0:T(8,128)(2,1)S(1)}, bf16[416,256]{1,0:T(8,128)(2,1)S(1)}, u32[]{:S(2)}, u32[]{:S(2)}) collective-permute-start(bf16[416,256]{1,0:T(8,128)(2,1)S(1)} %get-tuple-element.55), channel_id=1, source_target_pairs={{0,4},{4,0},{8,12},{12,8},{1,5},{5,1},{9,13},{13,9},{2,6},{6,2},{1... | collective-permute-start | bytes 638984 | tf_op jit(solution)/shard_map/ppermute | solution.py:22

commit v4 on v2

--- a/solution.py
+++ b/solution.py
@@ -11,9 +11,11 @@
 TILE = 8
 PATCH = TILE * TILE
 FACTOR = HEAD ** (-0.5)
+HEAVY = 20_000_000_000
 BF = jnp.bfloat16
 F32 = jnp.float32
 VMEM = pl.BlockSpec(memory_space=pltpu.VMEM)
+HBM = pl.BlockSpec(memory_space=pltpu.HBM)
 
 
 def swap(array, pairs):
@@ -24,8 +26,15 @@
     return [(i, i ^ 1) for i in range(count)]
 
 
-def pairs_b(count):
-    return [p for i in range(1, count - 1, 2) for p in ((i, i + 1), (i + 1, i))]
+def swap_b(array):
+    count, across = lax.axis_size("rows"), lax.axis_size("cols")
+    pairs = []
+    for row in range(count):
+        other = row if row in (0, count - 1) else row + 1 if row % 2 else row - 1
+        for col in range(across):
+            to = min(col ^ 1, across - 1) if other == row else col
+            pairs.append((row * across + col, other * across + to))
+    return lax.ppermute(array, ("rows", "cols"), pairs)
 
 
 def column_tiles(block, tile_cols):
@@ -75,9 +84,12 @@
     return lax.dot_general(a, b, (((1,), (0,)), ((), ())), preferred_element_type=F32)
 
 
-def prepare_kernel(k_ref, v_ref, reg_ref, a_ref, b_ref, sems):
+def prepare_kernel(q_ref, g_ref, k_ref, v_ref, reg_ref, *refs):
+    a_ref, b_ref, sems = refs[0], refs[1], refs[-1]
+    if b_ref.shape[0] > k_ref.shape[0]:
+        b_ref[k_ref.shape[0] :] = jnp.zeros((b_ref.shape[0] - k_ref.shape[0], b_ref.shape[1]), BF)
     even = lax.rem(lax.axis_index("rows"), 2) == 0
-    edge = b_ref.shape[0] // 2
+    edge = k_ref.shape[0] // 2
     last = k_ref.shape[0] - edge
     at_a = pl.multiple_of(jnp.where(even, last, 0), edge)
     at_b = pl.multiple_of(jnp.where(even, 0, last), edge)
@@ -89,6 +101,7 @@
     if a_ref.shape[0] > 2 * edge:
         for n in range(2):
             moves.append((reg_ref.at[n], a_ref.at[pl.ds(2 * edge + n * own, own)]))
+    moves += list(zip((q_ref, g_ref, k_ref, v_ref, reg_ref), refs[2:7]))
     copies = [pltpu.make_async_copy(x, y, sems.at[n]) for n, (x, y) in enumerate(moves)]
     for copy in copies:
         copy.start()
@@ -152,6 +165,7 @@
     qbd_ref, gbd_ref, stat_ref, a_ref, b_ref = refs[:5]
     if split_regs:
         own_ref, two_ref, three_ref = refs[5:8]
+        cut = own_ref.shape[1]
         refs = refs[8:]
     else:
         all_ref = refs[5]
@@ -170,14 +184,15 @@
         top = column_tiles(jnp.where(even, from_b, from_a), tile_cols)
         bottom = column_tiles(jnp.where(even, from_a, from_b), tile_cols)
         if split_regs:
-            cut = own_ref.shape[1]
             base = 2 * edge + n * cut
-            regs = jnp.concatenate([own_ref[n], a_ref[base : base + cut], two_ref[n], three_ref[n]], axis=0)
+            regs = jnp.concatenate([own_ref[n], two_ref[n], three_ref[n], a_ref[base : base + cut]], axis=0)
         else:
             regs = all_ref[n]
         for t, halo in enumerate((top, bottom)):
             ref[t, :edge] = jnp.concatenate(halo, axis=0).astype(BF)
             ref[t, edge:] = regs
+    if back_b_ref.shape[0] > 2 * edge:
+        back_b_ref[2 * edge :] = jnp.zeros((back_b_ref.shape[0] - 2 * edge, feature), BF)
     dk_reg = dv_reg = None
     dk_halo, dv_halo = [], []
     for t in range(tile_rows):
@@ -232,9 +247,9 @@
         if split_regs:
             base = 2 * edge + n * cut
             reg_outs[0][n] = reg[:cut]
-            back_a_ref[base : base + cut] = reg[cut : 2 * cut].astype(BF)
-            reg_outs[1][n] = reg[2 * cut : 3 * cut].astype(BF)
-            reg_outs[2][n] = reg[3 * cut :].astype(BF)
+            reg_outs[1][n] = reg[cut : 2 * cut].astype(BF)
+            reg_outs[2][n] = reg[2 * cut : 3 * cut].astype(BF)
+            back_a_ref[base : base + cut] = reg[3 * cut :].astype(BF)
         else:
             reg_outs[0][n] = reg
 
@@ -252,11 +267,9 @@
     dsx_ref,
     kx_ref,
     vx_ref,
-    o_ref,
-    dq_ref,
-    dk_ref,
-    dv_ref,
+    *refs,
 ):
+    o_ref, dq_ref, dk_ref, dv_ref = refs[:4]
     feature = kt_ref.shape[0]
     heads = feature // HEAD
     line = tile_cols * PATCH
@@ -294,43 +307,31 @@
 
 def finish_kernel(dk_ref, dv_ref, a_ref, b_ref, *refs, split_regs):
     if split_regs:
-        dreg_ref, c_ref, e_ref = refs[:3]
-        refs = refs[3:]
+        dreg_ref, two_ref, three_ref, *refs = refs
     gk_ref, gv_ref = refs[:2]
-    even = lax.rem(lax.axis_index("rows"), 2) == 0
+    me = lax.axis_index("rows")
+    even = lax.rem(me, 2) == 0
+    has_top = me > 0
+    has_bottom = me < lax.axis_size("rows") - 1
     tile_cols = dk_ref.shape[0]
-    edge = b_ref.shape[0] // 2
+    edge = tile_cols * PATCH
     for n, (acc_ref, out_ref) in enumerate(((dk_ref, gk_ref), (dv_ref, gv_ref))):
         from_a = a_ref[n * edge : (n + 1) * edge]
         from_b = b_ref[n * edge : (n + 1) * edge]
-        top = jnp.where(even, from_b, from_a).astype(F32)
-        bottom = jnp.where(even, from_a, from_b).astype(F32)
+        top = jnp.where(has_top, jnp.where(even, from_b, from_a).astype(F32), 0.0)
+        bottom = jnp.where(has_bottom, jnp.where(even, from_a, from_b).astype(F32), 0.0)
         rows = acc_ref.shape[1]
         columns = []
         for c in range(tile_cols):
-            high = top[c * PATCH : (c + 1) * PATCH]
-            low = bottom[c * PATCH : (c + 1) * PATCH]
-            if rows == PATCH:
-                columns.append(acc_ref[c] + high + low)
-                continue
-            columns.append(
-                jnp.concatenate(
-                    [acc_ref[c, :PATCH] + high, acc_ref[c, PATCH : rows - PATCH], acc_ref[c, rows - PATCH :] + low]
-                    if rows > 2 * PATCH
-                    else [acc_ref[c, :PATCH] + high, acc_ref[c, PATCH:] + low],
-                    axis=0,
-                )
-            )
+            high = acc_ref[c, :PATCH] + top[c * PATCH : (c + 1) * PATCH]
+            low = acc_ref[c, rows - PATCH :] + bottom[c * PATCH : (c + 1) * PATCH]
+            columns.append(jnp.concatenate([high, low], axis=0))
         out_ref[...] = patch_order(columns).astype(BF)
         if split_regs:
-            cut = c_ref.shape[1]
+            cut = dreg_ref.shape[1]
             base = 2 * edge + n * cut
-            refs[2][n] = (
-                dreg_ref[n, :cut]
-                + a_ref[base : base + cut].astype(F32)
-                + c_ref[n].astype(F32)
-                + e_ref[n].astype(F32)
-            )
+            received = a_ref[base : base + cut].astype(F32) + two_ref[n].astype(F32) + three_ref[n].astype(F32)
+            refs[2][n] = dreg_ref[n] + received
 
 
 def shape(dims, dtype):
@@ -362,26 +363,33 @@
     edge = tile_cols * PATCH
     own = registers.shape[1]
     reg_count = own * count
-    q, k, v, g = (x.reshape(total, feature) for x in (query, keys, values, cotangent))
+    q, k, v, g = (
+        pltpu.with_memory_space_constraint(x.reshape(total, feature), pltpu.HBM)
+        for x in (query, keys, values, cotangent)
+    )
     extra = 2 * own if split_regs else 0
+    pad = 2 * extra
     two = [(i, i ^ 2) for i in range(count)]
     three = [(i, i ^ 3) for i in range(count)]
 
-    if split_regs:
-        regs = (registers, swap(registers, two), swap(registers, three))
+    registers = pltpu.with_memory_space_constraint(registers, pltpu.HBM)
+    pay_a, pay_b, q, g, k, v, reg_held = call(
+        prepare_kernel,
+        "prepare",
+        (q, g, k, v, registers),
+        (shape((2 * edge + extra, feature), BF), shape((2 * edge + pad, feature), BF))
+        + tuple(shape((total, feature), BF) for _ in range(4))
+        + (shape(registers.shape, BF),),
+        0,
+        in_specs=[HBM] * 5,
+        scratch=[pltpu.SemaphoreType.DMA((11,))],
+    )
+    got_b = swap_b(pay_b)
+    got_a = swap(pay_a, pairs_a(count))
+    if split_regs:
+        regs = (reg_held, swap(reg_held, two), swap(reg_held, three))
     else:
         regs = (lax.all_gather(registers, "rows", axis=1, tiled=True),)
-    pay_a, pay_b = call(
-        prepare_kernel,
-        "prepare",
-        (k, v, registers),
-        (shape((2 * edge + extra, feature), BF), shape((2 * edge, feature), BF)),
-        0,
-        in_specs=[pl.BlockSpec(memory_space=pl.ANY)] * 3,
-        scratch=[pltpu.SemaphoreType.DMA((6,))],
-    )
-    got_b = swap(pay_b, pairs_b(count))
-    got_a = swap(pay_a, pairs_a(count))
 
     tiles = tile_rows * tile_cols
     rows = tile_rows * PATCH
@@ -400,7 +408,7 @@
             shape((tiles, most, feature), BF),
             shape((tiles, 8, feature), F32),
         ),
-        4 * tiles * most * feature * feature,
+        600_000_000,
         scratch=[pltpu.VMEM((total, feature), BF)] * 2,
     )
     if split_regs:
@@ -422,12 +430,12 @@
             shape((tile_rows, window, feature), BF),
             shape((tile_rows, window, feature), BF),
             shape((2 * edge + extra, feature), BF),
-            shape((2 * edge, feature), BF),
+            shape((2 * edge + pad, feature), BF),
         )
         + reg_shapes,
         8 * tiles * window * feature * feature,
     )
-    back_from_b = swap(back_b, pairs_b(count))
+    back_from_b = swap_b(back_b)
     back_from_a = swap(back_a, pairs_a(count))
     if split_regs:
         rest = (back_regs[0], swap(back_regs[1], two), swap(back_regs[2], three))
@@ -445,7 +453,7 @@
             shape((tile_cols, rows, feature), F32),
             shape((tile_cols, rows, feature), F32),
         ),
-        8 * tiles * most * feature * feature,
+        600_000_000,
     )
     outs = call(
         functools.partial(finish_kernel, split_regs=split_regs),

time: 34.2 us -> 25.5 us (0.75)
  starting transfers between devices: 17 us -> 10.7 us
  local copies, waits for them, and re-layouts: 5.55 us -> 0 us
  waiting for transfers between devices: 2.23 us -> 6.19 us
  Pallas kernels: 8.28 us -> 7.84 us
    ppermute x8 -> x6, starting transfers between devices: 17 us -> 10.1 us  [swap(): return lax.ppermute(array, 'rows', pairs)]
    unnamed x12 -> x0, local copies, waits for them, and re-layouts: 5.55 us -> none
    ppermute x8 -> x6, waiting for transfers between devices: 2.23 us -> 6.18 us  [swap(): return lax.ppermute(array, 'rows', pairs)]
    ppermute x0 -> x2, starting transfers between devices: none -> 0.59 us  [swap_b(): return lax.ppermute(array, ('rows', 'cols'), pairs)]
    pallas_call x5, Pallas kernels: 8.28 us -> 7.84 us  [call(): pl.pallas_call(kernel, out_shape=tuple(outs), in_specs=in_specs or [VMEM]...]
  transfers between devices with their start and end apart: 8 -> 8, of which waited for: 2 -> 3; matrix products, arithmetic and copies ran while one was open for 0% -> 0% of each run, Pallas kernels for 11% -> 14%
where the time goes in v4:
time: 25.5 us; the launch traced here: 25.4 us
  starting transfers between devices  10.7 us (42%)
  Pallas kernels  7.84 us (31%)
  waiting for transfers between devices  6.19 us (24%)
  between operations  0.68 us (3%)
    ppermute x6, starting transfers between devices, swap(): return lax.ppermute(array, 'rows', pairs)  10.1 us
    pallas_call x5, Pallas kernels, call(): pl.pallas_call(kernel, out_shape=tuple(outs), in_specs=in_specs or [VMEM]...  7.84 us
    ppermute x6, waiting for transfers between devices, swap(): return lax.ppermute(array, 'rows', pairs)  6.18 us
    ppermute x2, starting transfers between devices, swap_b(): return lax.ppermute(array, ('rows', 'cols'), pairs)  0.59 us
  transfers between devices with their start and end apart: 8, of which 3 were waited for; matrix products, arithmetic and copies ran while one was open for 0% of the time, Pallas kernels for 14%

profile of v4, /device:TPU:0, one launch (start us, length us, event | category | flops | bytes accessed | tf_op | source)
XLA Modules:
  0.0 25.4 jit_solution(1101294026336642834)
XLA Ops:
  0.6 1.5 %prepare.1 = (bf16[416,256]{1,0:T(8,128)(2,1)S(1)}, bf16[448,256]{1,0:T(8,128)(2,1)S(1)}, bf16[384,256]{1,0:T(8,128)(2,1)S(1)}, bf16[384,256]{1,0:T(8,128)(2,1)S...) custom-call(bf16[384,256]{1,0:T(8,128)(2,1)} %bitcast.8, ...), custom_call_target="tpu_custom_call" | custom-call | bytes 2048000 | tf_op jit(solution)/shard_map/prepare/pallas_call | solution.py:343
  2.1 0.5 %collective-permute-start.1 = (bf16[448,256]{1,0:T(8,128)(2,1)S(1)}, bf16[448,256]{1,0:T(8,128)(2,1)S(1)}, u32[]{:S(2)}, u32[]{:S(2)}) collective-permute-start(bf16[448,256]{1,0:T(8,128)(2,1)S(1)} %get-tuple-element.48), channel_id=1, source_target_pairs={{0,1},{1,0},{2,3},{3,2},{4,8},{5,9},{6,10},{7,11},{8,4},{9,5},{10,... | collective-permute-start | bytes 688136 | tf_op jit(solution)/shard_map/ppermute | solution.py:37
  2.6 4.1 %collective-permute-start = (bf16[416,256]{1,0:T(8,128)(2,1)S(1)}, bf16[416,256]{1,0:T(8,128)(2,1)S(1)}, u32[]{:S(2)}, u32[]{:S(2)}) collective-permute-start(bf16[416,256]{1,0:T(8,128)(2,1)S(1)} %get-tuple-element.47), channel_id=1, source_target_pairs={{0,4},{4,0},{8,12},{12,8},{1,5},{5,1},{9,13},{13,9},{2,6},{6,2},{1... | collective-permute-start | bytes 638984 | tf_op jit(solution)/shard_map/ppermute | solution.py:22
  6.8 1.3 %collective-permute-start.3 = (bf16[2,16,256]{2,1,0:T(8,128)(2,1)S(1)}, bf16[2,16,256]{2,1,0:T(8,128)(2,1)S(1)}, u32[]{:S(2)}, u32[]{:S(2)}) collective-permute-start(bf16[2,16,256]{2,1,0:T(8,128)(2,1)S(1)} %get-tuple-element.49.refs_5_), channel_id=1, source_target_pairs={{0,12},{4,8},{8,4},{12,0},{1,13},{5,9},{9,5},{13,1},{2,14},{6,10},... | collective-permute-start | bytes 49160 | tf_op jit(solution)/shard_map/ppermute | solution.py:22
  8.1 0.1 collective-permute-start.2
  8.3 1.1 %own.1 = (bf16[6,256,256]{2,1,0:T(8,128)(2,1)S(1)}, bf16[6,256,256]{2,1,0:T(8,128)(2,1)S(1)}, bf16[256,384]{1,0:T(8,128)(2,1)S(1)}, bf16[256,384]{1,0:T(8,128)(2...) custom-call(bf16[384,256]{1,0:T(8,128)(2,1)S(1)} %get-tuple-element.36.q_ref, ...), custom_call_target="tpu_custom_call" | custom-call | flops 600000000 | bytes 6340608 | tf_op jit(solution)/shard_map/own/pallas_call | solution.py:343
  9.4 4.3 %collective-permute-done.3.refs_7_ = bf16[2,16,256]{2,1,0:T(8,128)(2,1)S(1)} collective-permute-done((bf16[2,16,256]{2,1,0:T(8,128)(2,1)S(1)}, bf16[2,16,256]{2,1,0:T(8,128)(2,1)S(1)}, u32[]{:S(2)}, u32[]{:S(2)}) %collective-permute-start.3) | collective-permute-done | bytes 16416 | tf_op jit(solution)/shard_map/ppermute | solution.py:22
  13.7 0.0 collective-permute-done.2.refs_6_
  13.7 0.0 collective-permute-done.refs_3_
  13.7 0.0 collective-permute-done.1.refs_4_
  13.7 2.0 %far.1 = (f32[6,8,256]{2,1,0:T(8,128)S(1)}, bf16[6,256,256]{2,1,0:T(8,128)(2,1)S(1)}, bf16[6,256,256]{2,1,0:T(8,128)(2,1)S(1)}, bf16[2,256,256]{2,1,0:T(8,128)(2...) custom-call(bf16[6,256,256]{2,1,0:T(8,128)(2,1)S(1)} %get-tuple-elem, ...), custom_call_target="tpu_custom_call" | custom-call | flops 805306368 | bytes 4767744 | tf_op jit(solution)/shard_map/far/pallas_call | solution.py:343
  15.7 0.1 collective-permute-start.5
  15.8 2.0 %collective-permute-start.4 = (bf16[416,256]{1,0:T(8,128)(2,1)S(1)}, bf16[416,256]{1,0:T(8,128)(2,1)S(1)}, u32[]{:S(2)}, u32[]{:S(2)}) collective-permute-start(bf16[416,256]{1,0:T(8,128)(2,1)S(1)} %get-tuple-element.59), channel_id=1, source_target_pairs={{0,4},{4,0},{8,12},{12,8},{1,5},{5,1},{9,13},{13,9},{2,6},{6,2},{1... | collective-permute-start | bytes 638984 | tf_op jit(solution)/shard_map/ppermute | solution.py:22
  17.7 0.8 %collective-permute-start.6 = (bf16[2,16,256]{2,1,0:T(8,128)(2,1)S(1)}, bf16[2,16,256]{2,1,0:T(8,128)(2,1)S(1)}, u32[]{:S(2)}, u32[]{:S(2)}) collective-permute-start(bf16[2,16,256]{2,1,0:T(8,128)(2,1)S(1)} %get-tuple-element.62), channel_id=1, source_target_pairs={{0,8},{4,12},{8,0},{12,4},{1,9},{5,13},{9,1},{13,5},{2,10},{6,14},... | collective-permute-start | bytes 49160 | tf_op jit(solution)/shard_map/ppermute | solution.py:22
  18.6 1.7 %collective-permute-start.7 = (bf16[2,16,256]{2,1,0:T(8,128)(2,1)S(1)}, bf16[2,16,256]{2,1,0:T(8,128)(2,1)S(1)}, u32[]{:S(2)}, u32[]{:S(2)}) collective-permute-start(bf16[2,16,256]{2,1,0:T(8,128)(2,1)S(1)} %get-tuple-element.63), channel_id=1, source_target_pairs={{0,12},{4,8},{8,4},{12,0},{1,13},{5,9},{9,5},{13,1},{2,14},{6,10},... | collective-permute-start | bytes 49160 | tf_op jit(solution)/shard_map/ppermute | solution.py:22
  20.2 2.4 %rest.1 = (bf16[384,256]{1,0:T(8,128)(2,1)}, bf16[384,256]{1,0:T(8,128)(2,1)}, f32[3,128,256]{2,1,0:T(8,128)S(1)}, f32[3,128,256]{2,1,0:T(8,128)S(1)}) custom-call(bf16[6,256,256]{2,1,0:T(8,128)(2,1)S(1)} %get-tuple-element.40.refs_0_.qbd_ref, bf16[6,256,256]{2,1,0:T(8,128)(2,1)S(1)} %get-tuple-element.41.refs_1_.gbd_ref, ...), custom_call_target="tpu_custom_call" | custom-call | flops 600000000 | bytes 8830976 | tf_op jit(solution)/shard_map/rest/pallas_call | solution.py:343
  22.7 0.3 %collective-permute-done.6.refs_1_ = bf16[2,16,256]{2,1,0:T(8,128)(2,1)S(1)} collective-permute-done((bf16[2,16,256]{2,1,0:T(8,128)(2,1)S(1)}, bf16[2,16,256]{2,1,0:T(8,128)(2,1)S(1)}, u32[]{:S(2)}, u32[]{:S(2)}) %collective-permute-start.6) | collective-permute-done | bytes 16416 | tf_op jit(solution)/shard_map/ppermute | solution.py:22
  23.0 1.6 %collective-permute-done.7.refs_2_ = bf16[2,16,256]{2,1,0:T(8,128)(2,1)S(1)} collective-permute-done((bf16[2,16,256]{2,1,0:T(8,128)(2,1)S(1)}, bf16[2,16,256]{2,1,0:T(8,128)(2,1)S(1)}, u32[]{:S(2)}, u32[]{:S(2)}) %collective-permute-start.7) | collective-permute-done | bytes 16416 | tf_op jit(solution)/shard_map/ppermute | solution.py:22
  24.5 0.0 collective-permute-done.4.a_ref
  24.5 0.0 collective-permute-done.5.b_ref
  24.5 0.8 %finish.1 = (bf16[384,256]{1,0:T(8,128)(2,1)}, bf16[384,256]{1,0:T(8,128)(2,1)}, f32[2,16,256]{2,1,0:T(8,128)}) custom-call(f32[3,128,256]{2,1,0:T(8,128)S(1)} %get-tuple-element.57.dk_ref, f32[3,128,256]{2,1,0:T(8,128)S(1)} %get-tuple-element.58.dv_ref, bf16[416,256]{1,0:T(8,128)(2,1)S(1)} %collective-permute-done.4.a_ref, ...), custom_call_target="tpu_custom_call" | custom-call | bytes 1720320 | tf_op jit(solution)/shard_map/finish/pallas_call | solution.py:343
Async XLA Ops:
  2.1 11.6 %collective-permute-start.1 = (bf16[448,256]{1,0:T(8,128)(2,1)S(1)}, bf16[448,256]{1,0:T(8,128)(2,1)S(1)}, u32[]{:S(2)}, u32[]{:S(2)}) collective-permute-start(bf16[448,256]{1,0:T(8,128)(2,1)S(1)} %get-tuple-element.48), channel_id=1, source_target_pairs={{0,1},{1,0},{2,3},{3,2},{4,8},{5,9},{6,10},{7,11},{8,4},{9,5},{10,... | collective-permute-start | bytes 688136 | tf_op jit(solution)/shard_map/ppermute | solution.py:37
  2.6 11.1 %collective-permute-start = (bf16[416,256]{1,0:T(8,128)(2,1)S(1)}, bf16[416,256]{1,0:T(8,128)(2,1)S(1)}, u32[]{:S(2)}, u32[]{:S(2)}) collective-permute-start(bf16[416,256]{1,0:T(8,128)(2,1)S(1)} %get-tuple-element.47), channel_id=1, source_target_pairs={{0,4},{4,0},{8,12},{12,8},{1,5},{5,1},{9,13},{13,9},{2,6},{6,2},{1... | collective-permute-start | bytes 638984 | tf_op jit(solution)/shard_map/ppermute | solution.py:22
  6.8 6.9 %collective-permute-start.3 = (bf16[2,16,256]{2,1,0:T(8,128)(2,1)S(1)}, bf16[2,16,256]{2,1,0:T(8,128)(2,1)S(1)}, u32[]{:S(2)}, u32[]{:S(2)}) collective-permute-start(bf16[2,16,256]{2,1,0:T(8,128)(2,1)S(1)} %get-tuple-element.49.refs_5_), channel_id=1, source_target_pairs={{0,12},{4,8},{8,4},{12,0},{1,13},{5,9},{9,5},{13,1},{2,14},{6,10},... | collective-permute-start | bytes 49160 | tf_op jit(solution)/shard_map/ppermute | solution.py:22
  8.1 5.6 %collective-permute-start.2 = (bf16[2,16,256]{2,1,0:T(8,128)(2,1)S(1)}, bf16[2,16,256]{2,1,0:T(8,128)(2,1)S(1)}, u32[]{:S(2)}, u32[]{:S(2)}) collective-permute-start(bf16[2,16,256]{2,1,0:T(8,128)(2,1)S(1)} %get-tuple-element.49.refs_5_), channel_id=1, source_target_pairs={{0,8},{4,12},{8,0},{12,4},{1,9},{5,13},{9,1},{13,5},{2,10},{6,14},... | collective-permute-start | bytes 49160 | tf_op jit(solution)/shard_map/ppermute | solution.py:22
  15.7 8.8 %collective-permute-start.5 = (bf16[448,256]{1,0:T(8,128)(2,1)S(1)}, bf16[448,256]{1,0:T(8,128)(2,1)S(1)}, u32[]{:S(2)}, u32[]{:S(2)}) collective-permute-start(bf16[448,256]{1,0:T(8,128)(2,1)S(1)} %get-tuple-element.60), channel_id=1, source_target_pairs={{0,1},{1,0},{2,3},{3,2},{4,8},{5,9},{6,10},{7,11},{8,4},{9,5},{10,... | collective-permute-start | bytes 688136 | tf_op jit(solution)/shard_map/ppermute | solution.py:37
  15.8 8.8 %collective-permute-start.4 = (bf16[416,256]{1,0:T(8,128)(2,1)S(1)}, bf16[416,256]{1,0:T(8,128)(2,1)S(1)}, u32[]{:S(2)}, u32[]{:S(2)}) collective-permute-start(bf16[416,256]{1,0:T(8,128)(2,1)S(1)} %get-tuple-element.59), channel_id=1, source_target_pairs={{0,4},{4,0},{8,12},{12,8},{1,5},{5,1},{9,13},{13,9},{2,6},{6,2},{1... | collective-permute-start | bytes 638984 | tf_op jit(solution)/shard_map/ppermute | solution.py:22
  17.7 5.2 %collective-permute-start.6 = (bf16[2,16,256]{2,1,0:T(8,128)(2,1)S(1)}, bf16[2,16,256]{2,1,0:T(8,128)(2,1)S(1)}, u32[]{:S(2)}, u32[]{:S(2)}) collective-permute-start(bf16[2,16,256]{2,1,0:T(8,128)(2,1)S(1)} %get-tuple-element.62), channel_id=1, source_target_pairs={{0,8},{4,12},{8,0},{12,4},{1,9},{5,13},{9,1},{13,5},{2,10},{6,14},... | collective-permute-start | bytes 49160 | tf_op jit(solution)/shard_map/ppermute | solution.py:22
  18.6 6.0 %collective-permute-start.7 = (bf16[2,16,256]{2,1,0:T(8,128)(2,1)S(1)}, bf16[2,16,256]{2,1,0:T(8,128)(2,1)S(1)}, u32[]{:S(2)}, u32[]{:S(2)}) collective-permute-start(bf16[2,16,256]{2,1,0:T(8,128)(2,1)S(1)} %get-tuple-element.63), channel_id=1, source_target_pairs={{0,12},{4,8},{8,4},{12,0},{1,13},{5,9},{9,5},{13,1},{2,14},{6,10},... | collective-permute-start | bytes 49160 | tf_op jit(solution)/shard_map/ppermute | solution.py:22

commit v5 on v4

--- a/solution.py
+++ b/solution.py
@@ -84,8 +84,15 @@
     return lax.dot_general(a, b, (((1,), (0,)), ((), ())), preferred_element_type=F32)
 
 
-def prepare_kernel(q_ref, g_ref, k_ref, v_ref, reg_ref, *refs):
-    a_ref, b_ref, sems = refs[0], refs[1], refs[-1]
+def copy_all(moves, sems):
+    copies = [pltpu.make_async_copy(x, y, sems.at[n]) for n, (x, y) in enumerate(moves)]
+    for copy in copies:
+        copy.start()
+    for copy in copies:
+        copy.wait()
+
+
+def prepare_kernel(k_ref, v_ref, reg_ref, a_ref, b_ref, held_ref, sems):
     if b_ref.shape[0] > k_ref.shape[0]:
         b_ref[k_ref.shape[0] :] = jnp.zeros((b_ref.shape[0] - k_ref.shape[0], b_ref.shape[1]), BF)
     even = lax.rem(lax.axis_index("rows"), 2) == 0
@@ -95,40 +102,24 @@
     at_b = pl.multiple_of(jnp.where(even, 0, last), edge)
     moves = []
     for n, ref in enumerate((k_ref, v_ref)):
+        moves.append((ref.at[pl.ds(at_b, edge)], b_ref.at[pl.ds(n * edge, edge)]))
         moves.append((ref.at[pl.ds(at_a, edge)], a_ref.at[pl.ds(n * edge, edge)]))
-        moves.append((ref.at[pl.ds(at_b, edge)], b_ref.at[pl.ds(n * edge, edge)]))
     own = reg_ref.shape[1]
     if a_ref.shape[0] > 2 * edge:
         for n in range(2):
             moves.append((reg_ref.at[n], a_ref.at[pl.ds(2 * edge + n * own, own)]))
-    moves += list(zip((q_ref, g_ref, k_ref, v_ref, reg_ref), refs[2:7]))
-    copies = [pltpu.make_async_copy(x, y, sems.at[n]) for n, (x, y) in enumerate(moves)]
-    for copy in copies:
-        copy.start()
-    for copy in copies:
-        copy.wait()
+    moves.append((reg_ref, held_ref))
+    copy_all(moves, sems)
 
 
 def columns_near(c, tile_cols):
     return max(c - 1, 0), min(c + 2, tile_cols)
 
 
-def own_kernel(
-    tile_cols,
-    q_ref,
-    g_ref,
-    k_ref,
-    v_ref,
-    qbd_ref,
-    gbd_ref,
-    kt_ref,
-    vt_ref,
-    exp_ref,
-    dw_ref,
-    stat_ref,
-    kc_ref,
-    vc_ref,
-):
+def own_kernel(tile_cols, *refs):
+    qbd_ref, gbd_ref, kt_ref, vt_ref, exp_ref, dw_ref, stat_ref, kc_ref, vc_ref = refs[4:13]
+    q_ref, g_ref, k_ref, v_ref = held = refs[13:17]
+    copy_all(list(zip(refs[:4], held)), refs[17])
     heads = q_ref.shape[1] // HEAD
     line = tile_cols * PATCH
     tile_rows = q_ref.shape[0] // line
@@ -161,18 +152,7 @@
             stat_ref[tile, 2:3] = jnp.sum(e * d.astype(F32), axis=0, keepdims=True)
 
 
-def far_kernel(tile_cols, split_regs, *refs):
-    qbd_ref, gbd_ref, stat_ref, a_ref, b_ref = refs[:5]
-    if split_regs:
-        own_ref, two_ref, three_ref = refs[5:8]
-        cut = own_ref.shape[1]
-        refs = refs[8:]
-    else:
-        all_ref = refs[5]
-        refs = refs[6:]
-    final_ref, px_ref, dsx_ref, kx_ref, vx_ref, back_a_ref, back_b_ref = refs[:7]
-    reg_outs = refs[7:]
-    feature = a_ref.shape[1]
+def halo_kernel(tile_cols, qbd_ref, gbd_ref, stat_ref, a_ref, b_ref, exp_ref, dw_ref, sum_ref, kx_ref, vx_ref):
     tile_rows = qbd_ref.shape[0] // tile_cols
     edge = tile_cols * PATCH
     me = lax.axis_index("rows")
@@ -181,16 +161,47 @@
     for n, ref in enumerate((kx_ref, vx_ref)):
         from_a = a_ref[n * edge : (n + 1) * edge]
         from_b = b_ref[n * edge : (n + 1) * edge]
-        top = column_tiles(jnp.where(even, from_b, from_a), tile_cols)
-        bottom = column_tiles(jnp.where(even, from_a, from_b), tile_cols)
-        if split_regs:
+        for t, halo in enumerate((jnp.where(even, from_b, from_a), jnp.where(even, from_a, from_b))):
+            ref[t] = jnp.concatenate(column_tiles(halo, tile_cols), axis=0).astype(BF)
+    for t in range(tile_rows):
+        for c in range(tile_cols):
+            tile = t * tile_cols + c
+            low, high = columns_near(c, tile_cols)
+            near = slice(low * PATCH, high * PATCH)
+            s = jnp.where(has[t], dot_nt(kx_ref[t, near], qbd_ref[tile]), -1e30)
+            d = dot_nt(vx_ref[t, near], gbd_ref[tile]).astype(BF)
+            own_top = stat_ref[tile, 0:1]
+            top = jnp.maximum(own_top, jnp.max(s, axis=0, keepdims=True))
+            e = jnp.exp(s - top)
+            ratio = jnp.exp(own_top - top)
+            exp_ref[tile, near] = e
+            dw_ref[tile, near] = d
+            sum_ref[tile, 0:1] = top
+            sum_ref[tile, 1:2] = stat_ref[tile, 1:2] * ratio + jnp.sum(e, axis=0, keepdims=True)
+            sum_ref[tile, 2:3] = stat_ref[tile, 2:3] * ratio + jnp.sum(e * d.astype(F32), axis=0, keepdims=True)
+            sum_ref[tile, 3:4] = ratio
+
+
+def far_kernel(tile_cols, split_regs, *refs):
+    qbd_ref, gbd_ref, exp_ref, dw_ref, sum_ref, a_ref = refs[:6]
+    edge = tile_cols * PATCH
+    regs = []
+    if split_regs:
+        own_ref, two_ref, three_ref = refs[6:9]
+        refs = refs[9:]
+        cut = own_ref.shape[1]
+        for n in range(2):
             base = 2 * edge + n * cut
-            regs = jnp.concatenate([own_ref[n], two_ref[n], three_ref[n], a_ref[base : base + cut]], axis=0)
-        else:
-            regs = all_ref[n]
-        for t, halo in enumerate((top, bottom)):
-            ref[t, :edge] = jnp.concatenate(halo, axis=0).astype(BF)
-            ref[t, edge:] = regs
+            regs.append(jnp.concatenate([own_ref[n], two_ref[n], three_ref[n], a_ref[base : base + cut]], axis=0))
+    else:
+        regs = [refs[6][n] for n in range(2)]
+        refs = refs[7:]
+    final_ref, px_ref, dsx_ref, kr_ref, vr_ref, back_a_ref, back_b_ref = refs[:7]
+    reg_outs = refs[7:]
+    kr_ref[...], vr_ref[...] = regs
+    feature = a_ref.shape[1]
+    tile_rows = qbd_ref.shape[0] // tile_cols
+    even = lax.rem(lax.axis_index("rows"), 2) == 0
     if back_b_ref.shape[0] > 2 * edge:
         back_b_ref[2 * edge :] = jnp.zeros((back_b_ref.shape[0] - 2 * edge, feature), BF)
     dk_reg = dv_reg = None
@@ -202,32 +213,29 @@
             q_bd = qbd_ref[tile]
             g_bd = gbd_ref[tile]
             low, high = columns_near(c, tile_cols)
-            s = dot_nt(kx_ref[t], q_bd)
-            d = dot_nt(vx_ref[t], g_bd)
-            s_near = jnp.where(has[t], s[low * PATCH : high * PATCH], -1e30)
-            s = jnp.concatenate([s_near, s[edge:]], axis=0)
-            d = jnp.concatenate([d[low * PATCH : high * PATCH], d[edge:]], axis=0)
-            d = d.astype(BF).astype(F32)
-            own_top = stat_ref[tile, 0:1]
-            top = jnp.maximum(own_top, jnp.max(s, axis=0, keepdims=True))
+            near = slice(low * PATCH, high * PATCH)
+            s = dot_nt(kr_ref[...], q_bd)
+            d = dot_nt(vr_ref[...], g_bd).astype(BF).astype(F32)
+            old_top = sum_ref[tile, 0:1]
+            top = jnp.maximum(old_top, jnp.max(s, axis=0, keepdims=True))
             e = jnp.exp(s - top)
-            ratio = jnp.exp(own_top - top)
-            inverse = 1.0 / (stat_ref[tile, 1:2] * ratio + jnp.sum(e, axis=0, keepdims=True))
-            row_dot = (stat_ref[tile, 2:3] * ratio + jnp.sum(e * d, axis=0, keepdims=True)) * inverse
-            final_ref[tile, 0:1] = ratio * inverse
+            ratio = jnp.exp(old_top - top)
+            inverse = 1.0 / (sum_ref[tile, 1:2] * ratio + jnp.sum(e, axis=0, keepdims=True))
+            row_dot = (sum_ref[tile, 2:3] * ratio + jnp.sum(e * d, axis=0, keepdims=True)) * inverse
+            scale = ratio * inverse
+            final_ref[tile, 0:1] = sum_ref[tile, 3:4] * scale
             final_ref[tile, 1:2] = row_dot
-            p = e * inverse
+            p_near = exp_ref[tile, near] * scale
+            p_reg = e * inverse
+            ds_near = p_near * (dw_ref[tile, near].astype(F32) - row_dot)
+            ds_reg = p_reg * (d - row_dot)
             parts = []
-            for x in (p, p * (d - row_dot)):
-                x = x.astype(BF)
-                pieces = [x]
-                size = (high - low) * PATCH
-                if low > 0 or high < tile_cols:
-                    pieces = [x[:size], x[size:]]
-                    if high < tile_cols:
-                        pieces.insert(1, jnp.zeros(((tile_cols - high) * PATCH, feature), BF))
-                    if low > 0:
-                        pieces.insert(0, jnp.zeros((low * PATCH, feature), BF))
+            for x_near, x_reg in ((p_near, p_reg), (ds_near, ds_reg)):
+                pieces = [x_near.astype(BF), x_reg.astype(BF)]
+                if high < tile_cols:
+                    pieces.insert(1, jnp.zeros(((tile_cols - high) * PATCH, feature), BF))
+                if low > 0:
+                    pieces.insert(0, jnp.zeros((low * PATCH, feature), BF))
                 parts.append(jnp.concatenate(pieces, axis=0))
             weights, d_scores = parts
             px_ref[tile] = weights
@@ -267,6 +275,8 @@
     dsx_ref,
     kx_ref,
     vx_ref,
+    kr_ref,
+    vr_ref,
     *refs,
 ):
     o_ref, dq_ref, dk_ref, dv_ref = refs[:4]
@@ -276,8 +286,8 @@
     tile_rows = qbd_ref.shape[0] // tile_cols
     rows = tile_rows * PATCH
     for t in range(tile_rows):
-        kxt = kx_ref[t].T
-        vxt = vx_ref[t].T
+        kxt = jnp.concatenate([kx_ref[t], kr_ref[...]], axis=0).T
+        vxt = jnp.concatenate([vx_ref[t], vr_ref[...]], axis=0).T
         o_cols, dq_cols = [], []
         for c in range(tile_cols):
             tile = t * tile_cols + c
@@ -305,10 +315,19 @@
         dq_ref[t * line : (t + 1) * line] = patch_order(dq_cols).astype(BF)
 
 
-def finish_kernel(dk_ref, dv_ref, a_ref, b_ref, *refs, split_regs):
+def registers_kernel(part_ref, three_ref, two_ref, out_ref):
+    out_ref[...] = part_ref[...] + two_ref[...].astype(F32) + three_ref[...].astype(F32)
+
+
+def finish_kernel(split_regs, dk_ref, dv_ref, a_ref, b_ref, *refs):
     if split_regs:
-        dreg_ref, two_ref, three_ref, *refs = refs
-    gk_ref, gv_ref = refs[:2]
+        own_ref, gk_ref, gv_ref, part_ref = refs
+        cut = own_ref.shape[1]
+        base = a_ref.shape[0] - 2 * cut
+        for n in range(2):
+            part_ref[n] = own_ref[n] + a_ref[base + n * cut : base + (n + 1) * cut].astype(F32)
+    else:
+        gk_ref, gv_ref = refs
     me = lax.axis_index("rows")
     even = lax.rem(me, 2) == 0
     has_top = me > 0
@@ -327,11 +346,6 @@
             low = acc_ref[c, rows - PATCH :] + bottom[c * PATCH : (c + 1) * PATCH]
             columns.append(jnp.concatenate([high, low], axis=0))
         out_ref[...] = patch_order(columns).astype(BF)
-        if split_regs:
-            cut = dreg_ref.shape[1]
-            base = 2 * edge + n * cut
-            received = a_ref[base : base + cut].astype(F32) + two_ref[n].astype(F32) + three_ref[n].astype(F32)
-            refs[2][n] = dreg_ref[n] + received
 
 
 def shape(dims, dtype):
@@ -373,16 +387,18 @@
     three = [(i, i ^ 3) for i in range(count)]
 
     registers = pltpu.with_memory_space_constraint(registers, pltpu.HBM)
-    pay_a, pay_b, q, g, k, v, reg_held = call(
+    pay_a, pay_b, reg_held = call(
         prepare_kernel,
         "prepare",
-        (q, g, k, v, registers),
-        (shape((2 * edge + extra, feature), BF), shape((2 * edge + pad, feature), BF))
-        + tuple(shape((total, feature), BF) for _ in range(4))
-        + (shape(registers.shape, BF),),
+        (k, v, registers),
+        (
+            shape((2 * edge + extra, feature), BF),
+            shape((2 * edge + pad, feature), BF),
+            shape(registers.shape, BF),
+        ),
         0,
-        in_specs=[HBM] * 5,
-        scratch=[pltpu.SemaphoreType.DMA((11,))],
+        in_specs=[HBM] * 3,
+        scratch=[pltpu.SemaphoreType.DMA((7,))],
     )
     got_b = swap_b(pay_b)
     got_a = swap(pay_a, pairs_a(count))
@@ -409,7 +425,8 @@
             shape((tiles, 8, feature), F32),
         ),
         600_000_000,
-        scratch=[pltpu.VMEM((total, feature), BF)] * 2,
+        in_specs=[HBM] * 4,
+        scratch=[pltpu.VMEM((total, feature), BF)] * 6 + [pltpu.SemaphoreType.DMA((4,))],
     )
     if split_regs:
         reg_shapes = (
@@ -419,16 +436,29 @@
         )
     else:
         reg_shapes = (shape((2, reg_count, feature), F32),)
-    final, px, dsx, kx, vx, back_a, back_b, *back_regs = call(
+    halo_exps, halo_dw, sums, kx, vx = call(
+        functools.partial(halo_kernel, tile_cols),
+        "halo",
+        (qbd, gbd, stats, got_a, got_b),
+        (
+            shape((tiles, edge, feature), F32),
+            shape((tiles, edge, feature), BF),
+            shape((tiles, 8, feature), F32),
+            shape((tile_rows, edge, feature), BF),
+            shape((tile_rows, edge, feature), BF),
+        ),
+        4 * tiles * edge * feature * feature,
+    )
+    final, px, dsx, kr, vr, back_a, back_b, *back_regs = call(
         functools.partial(far_kernel, tile_cols, split_regs),
         "far",
-        (qbd, gbd, stats, got_a, got_b) + regs,
+        (qbd, gbd, halo_exps, halo_dw, sums, got_a) + regs,
         (
             shape((tiles, 8, feature), F32),
             shape((tiles, window, feature), BF),
             shape((tiles, window, feature), BF),
-            shape((tile_rows, window, feature), BF),
-            shape((tile_rows, window, feature), BF),
+            shape((reg_count, feature), BF),
+            shape((reg_count, feature), BF),
             shape((2 * edge + extra, feature), BF),
             shape((2 * edge + pad, feature), BF),
         )
@@ -437,16 +467,10 @@
     )
     back_from_b = swap_b(back_b)
     back_from_a = swap(back_a, pairs_a(count))
-    if split_regs:
-        rest = (back_regs[0], swap(back_regs[1], two), swap(back_regs[2], three))
-        last_shapes = (shape((2, own, feature), F32),)
-    else:
-        rest = ()
-        last_shapes = ()
     attended, grad_query, dk, dv = call(
         functools.partial(rest_kernel, tile_cols),
         "rest",
-        (qbd, gbd, kt, vt, exps, dw, final, px, dsx, kx, vx),
+        (qbd, gbd, kt, vt, exps, dw, final, px, dsx, kx, vx, kr, vr),
         (
             shape((total, feature), BF),
             shape((total, feature), BF),
@@ -455,23 +479,30 @@
         ),
         600_000_000,
     )
-    outs = call(
-        functools.partial(finish_kernel, split_regs=split_regs),
+    mine = (back_regs[0],) if split_regs else ()
+    grad_keys, grad_values, *part = call(
+        functools.partial(finish_kernel, split_regs),
         "finish",
-        (dk, dv, back_from_a, back_from_b) + rest,
-        (shape((total, feature), BF), shape((total, feature), BF)) + last_shapes,
+        (dk, dv, back_from_a, back_from_b) + mine,
+        (shape((total, feature), BF), shape((total, feature), BF)) + tuple(shape(x.shape, F32) for x in mine),
         0,
     )
     if split_regs:
-        grad_registers = outs[2]
+        (grad_registers,) = call(
+            registers_kernel,
+            "registers",
+            (part[0], swap(back_regs[2], three), swap(back_regs[1], two)),
+            (shape((2, own, feature), F32),),
+            0,
+        )
     else:
         grad_registers = lax.psum_scatter(back_regs[0], "rows", scatter_dimension=1, tiled=True)
     whole = query.shape
     return (
         attended.reshape(whole),
         grad_query.reshape(whole),
-        outs[0].reshape(whole),
-        outs[1].reshape(whole),
+        grad_keys.reshape(whole),
+        grad_values.reshape(whole),
         grad_registers,
     )
 

time: 25.5 us -> 24.6 us (0.965)
  waiting for transfers between devices: 6.19 us -> 4.12 us
  Pallas kernels: 7.84 us -> 9.63 us
  starting transfers between devices: 10.7 us -> 10 us
    ppermute x6, waiting for transfers between devices: 6.18 us -> 4.11 us  [swap(): return lax.ppermute(array, 'rows', pairs)]
    pallas_call x5 -> x7, Pallas kernels: 7.84 us -> 9.63 us  [call(): pl.pallas_call(kernel, out_shape=tuple(outs), in_specs=in_specs or [VMEM]...]
    ppermute x6, starting transfers between devices: 10.1 us -> 9.45 us  [swap(): return lax.ppermute(array, 'rows', pairs)]
  transfers between devices with their start and end apart: 8 -> 8, of which waited for: 3 -> 3; matrix products, arithmetic and copies ran while one was open for 0% -> 0% of each run, Pallas kernels for 14% -> 26%
where the time goes in v5:
time: 24.6 us; the launch traced here: 24.5 us
  starting transfers between devices  10 us (41%)
  Pallas kernels  9.63 us (39%)
  waiting for transfers between devices  4.12 us (17%)
  between operations  0.67 us (3%)
    pallas_call x7, Pallas kernels, call(): pl.pallas_call(kernel, out_shape=tuple(outs), in_specs=in_specs or [VMEM]...  9.63 us
    ppermute x6, starting transfers between devices, swap(): return lax.ppermute(array, 'rows', pairs)  9.45 us
    ppermute x6, waiting for transfers between devices, swap(): return lax.ppermute(array, 'rows', pairs)  4.11 us
    ppermute x2, starting transfers between devices, swap_b(): return lax.ppermute(array, ('rows', 'cols'), pairs)  0.59 us
  transfers between devices with their start and end apart: 8, of which 3 were waited for; matrix products, arithmetic and copies ran while one was open for 0% of the time, Pallas kernels for 26%

profile of v5, /device:TPU:0, one launch (start us, length us, event | category | flops | bytes accessed | tf_op | source)
XLA Modules:
  0.0 24.5 jit_solution(12210047703121808936)
XLA Ops:
  0.6 1.1 %prepare.1 = (bf16[416,256]{1,0:T(8,128)(2,1)S(1)}, bf16[448,256]{1,0:T(8,128)(2,1)S(1)}, bf16[2,16,256]{2,1,0:T(8,128)(2,1)S(1)}) custom-call(bf16[384,256]{1,0:T(8,128)(2,1)} %bitcast.8, bf16[384,256]{1,0:T(8,128)(2,1)} %bitcast.10, bf16[2,16,256]{2,1,0:T(8,128)(2,1)} %reg_ref.1), custom_call_target="tpu_custom_call" | custom-call | bytes 868352 | tf_op jit(solution)/shard_map/prepare/pallas_call | solution.py:357
  1.8 0.5 %collective-permute-start.1 = (bf16[448,256]{1,0:T(8,128)(2,1)S(1)}, bf16[448,256]{1,0:T(8,128)(2,1)S(1)}, u32[]{:S(2)}, u32[]{:S(2)}) collective-permute-start(bf16[448,256]{1,0:T(8,128)(2,1)S(1)} %get-tuple-element.45), channel_id=1, source_target_pairs={{0,1},{1,0},{2,3},{3,2},{4,8},{5,9},{6,10},{7,11},{8,4},{9,5},{10,... | collective-permute-start | bytes 688136 | tf_op jit(solution)/shard_map/ppermute | solution.py:37
  2.3 4.1 %collective-permute-start = (bf16[416,256]{1,0:T(8,128)(2,1)S(1)}, bf16[416,256]{1,0:T(8,128)(2,1)S(1)}, u32[]{:S(2)}, u32[]{:S(2)}) collective-permute-start(bf16[416,256]{1,0:T(8,128)(2,1)S(1)} %get-tuple-element.44), channel_id=1, source_target_pairs={{0,4},{4,0},{8,12},{12,8},{1,5},{5,1},{9,13},{13,9},{2,6},{6,2},{1... | collective-permute-start | bytes 638984 | tf_op jit(solution)/shard_map/ppermute | solution.py:22
  6.4 1.3 %collective-permute-start.3 = (bf16[2,16,256]{2,1,0:T(8,128)(2,1)S(1)}, bf16[2,16,256]{2,1,0:T(8,128)(2,1)S(1)}, u32[]{:S(2)}, u32[]{:S(2)}) collective-permute-start(bf16[2,16,256]{2,1,0:T(8,128)(2,1)S(1)} %get-tuple-element.49.refs_6_), channel_id=1, source_target_pairs={{0,12},{4,8},{8,4},{12,0},{1,13},{5,9},{9,5},{13,1},{2,14},{6,10},... | collective-permute-start | bytes 49160 | tf_op jit(solution)/shard_map/ppermute | solution.py:22
  7.8 0.1 collective-permute-start.2
  7.9 2.3 %own.1 = (bf16[6,256,256]{2,1,0:T(8,128)(2,1)S(1)}, bf16[6,256,256]{2,1,0:T(8,128)(2,1)S(1)}, bf16[256,384]{1,0:T(8,128)(2,1)S(1)}, bf16[256,384]{1,0:T(8,128)(2...) custom-call(bf16[384,256]{1,0:T(8,128)(2,1)} %bitcast.12, ...), custom_call_target="tpu_custom_call" | custom-call | flops 600000000 | bytes 6340608 | tf_op jit(solution)/shard_map/own/pallas_call | solution.py:357
  10.2 1.3 %collective-permute-done.a_ref.refs_5_ = bf16[416,256]{1,0:T(8,128)(2,1)S(1)} collective-permute-done((bf16[416,256]{1,0:T(8,128)(2,1)S(1)}, bf16[416,256]{1,0:T(8,128)(2,1)S(1)}, u32[]{:S(2)}, u32[]{:S(2)}) %collective-permute-start) | collective-permute-done | bytes 213024 | tf_op jit(solution)/shard_map/ppermute | solution.py:22
  11.6 0.0 collective-permute-done.1.b_ref
  11.6 0.7 %halo.1 = (f32[6,192,256]{2,1,0:T(8,128)S(1)}, bf16[6,192,256]{2,1,0:T(8,128)(2,1)S(1)}, f32[6,8,256]{2,1,0:T(8,128)S(1)}, bf16[2,192,256]{2,1,0:T(8,128)(2,1)S(1)}, bf16[2,192,256]{2,1,0:T(8,128)(2,1)S(1)}) custom-call(bf16[6,256,256]{2,1,0:T(8,128)(2,1)S(1)} %get-tuple-element.37.qbd_ref.refs_0_, ...), custom_call_target="tpu_custom_call" | custom-call | flops 301989888 | bytes 4276224 | tf_op jit(solution)/shard_map/halo/pallas_call | solution.py:357
  12.3 1.0 %collective-permute-done.3.refs_8_ = bf16[2,16,256]{2,1,0:T(8,128)(2,1)S(1)} collective-permute-done((bf16[2,16,256]{2,1,0:T(8,128)(2,1)S(1)}, bf16[2,16,256]{2,1,0:T(8,128)(2,1)S(1)}, u32[]{:S(2)}, u32[]{:S(2)}) %collective-permute-start.3) | collective-permute-done | bytes 16416 | tf_op jit(solution)/shard_map/ppermute | solution.py:22
  13.3 0.0 collective-permute-done.2.refs_7_
  13.3 1.6 %far.1 = (f32[6,8,256]{2,1,0:T(8,128)S(1)}, bf16[6,256,256]{2,1,0:T(8,128)(2,1)S(1)}, bf16[6,256,256]{2,1,0:T(8,128)(2,1)S(1)}, bf16[64,256]{1,0:T(8,128)(2,1)S(...) custom-call(bf16[6,256,256]{2,1,0:T(8,128)(2,1)S(1)} %get-tuple-elem, ...), custom_call_target="tpu_custom_call" | custom-call | flops 805306368 | bytes 5849088 | tf_op jit(solution)/shard_map/far/pallas_call | solution.py:357
  14.9 0.1 collective-permute-start.5
  15.0 2.0 %collective-permute-start.4 = (bf16[416,256]{1,0:T(8,128)(2,1)S(1)}, bf16[416,256]{1,0:T(8,128)(2,1)S(1)}, u32[]{:S(2)}, u32[]{:S(2)}) collective-permute-start(bf16[416,256]{1,0:T(8,128)(2,1)S(1)} %get-tuple-element.61), channel_id=1, source_target_pairs={{0,4},{4,0},{8,12},{12,8},{1,5},{5,1},{9,13},{13,9},{2,6},{6,2},{1... | collective-permute-start | bytes 638984 | tf_op jit(solution)/shard_map/ppermute | solution.py:22
  17.0 1.9 %collective-permute-start.6 = (bf16[2,16,256]{2,1,0:T(8,128)(2,1)S(1)}, bf16[2,16,256]{2,1,0:T(8,128)(2,1)S(1)}, u32[]{:S(2)}, u32[]{:S(2)}) collective-permute-start(bf16[2,16,256]{2,1,0:T(8,128)(2,1)S(1)} %get-tuple-element.67), channel_id=1, source_target_pairs={{0,12},{4,8},{8,4},{12,0},{1,13},{5,9},{9,5},{13,1},{2,14},{6,10},... | collective-permute-start | bytes 49160 | tf_op jit(solution)/shard_map/ppermute | solution.py:22
  18.8 0.0 collective-permute-start.7
  18.8 2.4 %rest.1 = (bf16[384,256]{1,0:T(8,128)(2,1)}, bf16[384,256]{1,0:T(8,128)(2,1)}, f32[3,128,256]{2,1,0:T(8,128)S(1)}, f32[3,128,256]{2,1,0:T(8,128)S(1)}) custom-call(bf16[6,256,256]{2,1,0:T(8,128)(2,1)S(1)} %get-tuple-element.37.qbd_ref.refs_0_, bf16[6,256,256]{2,1,0:T(8,128)(2,1)S(1)} %get-tuple-element.38.gbd_ref.refs_1_, ...), custom_call_target="tpu_custom_call" | custom-call | flops 600000000 | bytes 8765440 | tf_op jit(solution)/shard_map/rest/pallas_call | solution.py:357
  21.2 1.8 %collective-permute-done.4.a_ref = bf16[416,256]{1,0:T(8,128)(2,1)S(1)} collective-permute-done((bf16[416,256]{1,0:T(8,128)(2,1)S(1)}, bf16[416,256]{1,0:T(8,128)(2,1)S(1)}, u32[]{:S(2)}, u32[]{:S(2)}) %collective-permute-start.4) | collective-permute-done | bytes 213024 | tf_op jit(solution)/shard_map/ppermute | solution.py:22
  23.0 0.0 collective-permute-done.5.b_ref
  23.0 0.8 %finish.1 = (bf16[384,256]{1,0:T(8,128)(2,1)}, bf16[384,256]{1,0:T(8,128)(2,1)}, f32[2,16,256]{2,1,0:T(8,128)S(1)}) custom-call(f32[3,128,256]{2,1,0:T(8,128)S(1)} %get-tuple-element.59.dk_ref, f32[3,128,256]{2,1,0:T(8,128)S(1)} %get-tuple-element.60.dv_ref, bf16[416,256]{1,0:T(8,128)(2,1)S(1)} %collective-permute-done.4.a_ref, ...), custom_call_target="tpu_custom_call" | custom-call | bytes 1687552 | tf_op jit(solution)/shard_map/finish/pallas_call | solution.py:357
  23.8 0.0 collective-permute-done.6.three_ref
  23.8 0.0 collective-permute-done.7.two_ref
  23.8 0.6 %registers.1 = f32[2,16,256]{2,1,0:T(8,128)} custom-call(f32[2,16,256]{2,1,0:T(8,128)S(1)} %get-tuple-element.66.part_ref, bf16[2,16,256]{2,1,0:T(8,128)(2,1)S(1)} %collective-permute-done.6.three_ref, bf16[2,16,256]{2,1,0:T(8,128)(2,1)S(1)} %collective-permute-done.7.two_ref), custom_call_target="tpu_custom_call" | custom-call | bytes 98304 | tf_op jit(solution)/shard_map/registers/pallas_call | solution.py:357
Async XLA Ops:
  1.8 9.8 %collective-permute-start.1 = (bf16[448,256]{1,0:T(8,128)(2,1)S(1)}, bf16[448,256]{1,0:T(8,128)(2,1)S(1)}, u32[]{:S(2)}, u32[]{:S(2)}) collective-permute-start(bf16[448,256]{1,0:T(8,128)(2,1)S(1)} %get-tuple-element.45), channel_id=1, source_target_pairs={{0,1},{1,0},{2,3},{3,2},{4,8},{5,9},{6,10},{7,11},{8,4},{9,5},{10,... | collective-permute-start | bytes 688136 | tf_op jit(solution)/shard_map/ppermute | solution.py:37
  2.3 9.3 %collective-permute-start = (bf16[416,256]{1,0:T(8,128)(2,1)S(1)}, bf16[416,256]{1,0:T(8,128)(2,1)S(1)}, u32[]{:S(2)}, u32[]{:S(2)}) collective-permute-start(bf16[416,256]{1,0:T(8,128)(2,1)S(1)} %get-tuple-element.44), channel_id=1, source_target_pairs={{0,4},{4,0},{8,12},{12,8},{1,5},{5,1},{9,13},{13,9},{2,6},{6,2},{1... | collective-permute-start | bytes 638984 | tf_op jit(solution)/shard_map/ppermute | solution.py:22
  6.4 6.9 %collective-permute-start.3 = (bf16[2,16,256]{2,1,0:T(8,128)(2,1)S(1)}, bf16[2,16,256]{2,1,0:T(8,128)(2,1)S(1)}, u32[]{:S(2)}, u32[]{:S(2)}) collective-permute-start(bf16[2,16,256]{2,1,0:T(8,128)(2,1)S(1)} %get-tuple-element.49.refs_6_), channel_id=1, source_target_pairs={{0,12},{4,8},{8,4},{12,0},{1,13},{5,9},{9,5},{13,1},{2,14},{6,10},... | collective-permute-start | bytes 49160 | tf_op jit(solution)/shard_map/ppermute | solution.py:22
  7.8 5.6 %collective-permute-start.2 = (bf16[2,16,256]{2,1,0:T(8,128)(2,1)S(1)}, bf16[2,16,256]{2,1,0:T(8,128)(2,1)S(1)}, u32[]{:S(2)}, u32[]{:S(2)}) collective-permute-start(bf16[2,16,256]{2,1,0:T(8,128)(2,1)S(1)} %get-tuple-element.49.refs_6_), channel_id=1, source_target_pairs={{0,8},{4,12},{8,0},{12,4},{1,9},{5,13},{9,1},{13,5},{2,10},{6,14},... | collective-permute-start | bytes 49160 | tf_op jit(solution)/shard_map/ppermute | solution.py:22
  14.9 8.1 %collective-permute-start.5 = (bf16[448,256]{1,0:T(8,128)(2,1)S(1)}, bf16[448,256]{1,0:T(8,128)(2,1)S(1)}, u32[]{:S(2)}, u32[]{:S(2)}) collective-permute-start(bf16[448,256]{1,0:T(8,128)(2,1)S(1)} %get-tuple-element.62), channel_id=1, source_target_pairs={{0,1},{1,0},{2,3},{3,2},{4,8},{5,9},{6,10},{7,11},{8,4},{9,5},{10,... | collective-permute-start | bytes 688136 | tf_op jit(solution)/shard_map/ppermute | solution.py:37
  15.0 8.0 %collective-permute-start.4 = (bf16[416,256]{1,0:T(8,128)(2,1)S(1)}, bf16[416,256]{1,0:T(8,128)(2,1)S(1)}, u32[]{:S(2)}, u32[]{:S(2)}) collective-permute-start(bf16[416,256]{1,0:T(8,128)(2,1)S(1)} %get-tuple-element.61), channel_id=1, source_target_pairs={{0,4},{4,0},{8,12},{12,8},{1,5},{5,1},{9,13},{13,9},{2,6},{6,2},{1... | collective-permute-start | bytes 638984 | tf_op jit(solution)/shard_map/ppermute | solution.py:22
  17.0 6.9 %collective-permute-start.6 = (bf16[2,16,256]{2,1,0:T(8,128)(2,1)S(1)}, bf16[2,16,256]{2,1,0:T(8,128)(2,1)S(1)}, u32[]{:S(2)}, u32[]{:S(2)}) collective-permute-start(bf16[2,16,256]{2,1,0:T(8,128)(2,1)S(1)} %get-tuple-element.67), channel_id=1, source_target_pairs={{0,12},{4,8},{8,4},{12,0},{1,13},{5,9},{9,5},{13,1},{2,14},{6,10},... | collective-permute-start | bytes 49160 | tf_op jit(solution)/shard_map/ppermute | solution.py:22
  18.8 5.0 %collective-permute-start.7 = (bf16[2,16,256]{2,1,0:T(8,128)(2,1)S(1)}, bf16[2,16,256]{2,1,0:T(8,128)(2,1)S(1)}, u32[]{:S(2)}, u32[]{:S(2)}) collective-permute-start(bf16[2,16,256]{2,1,0:T(8,128)(2,1)S(1)} %get-tuple-element.68), channel_id=1, source_target_pairs={{0,8},{4,12},{8,0},{12,4},{1,9},{5,13},{9,1},{13,5},{2,10},{6,14},... | collective-permute-start | bytes 49160 | tf_op jit(solution)/shard_map/ppermute | solution.py:22

commit v6 on v5

--- a/solution.py
+++ b/solution.py
@@ -11,7 +11,6 @@
 TILE = 8
 PATCH = TILE * TILE
 FACTOR = HEAD ** (-0.5)
-HEAVY = 20_000_000_000
 BF = jnp.bfloat16
 F32 = jnp.float32
 VMEM = pl.BlockSpec(memory_space=pltpu.VMEM)
@@ -93,8 +92,6 @@
 
 
 def prepare_kernel(k_ref, v_ref, reg_ref, a_ref, b_ref, held_ref, sems):
-    if b_ref.shape[0] > k_ref.shape[0]:
-        b_ref[k_ref.shape[0] :] = jnp.zeros((b_ref.shape[0] - k_ref.shape[0], b_ref.shape[1]), BF)
     even = lax.rem(lax.axis_index("rows"), 2) == 0
     edge = k_ref.shape[0] // 2
     last = k_ref.shape[0] - edge
@@ -152,38 +149,41 @@
             stat_ref[tile, 2:3] = jnp.sum(e * d.astype(F32), axis=0, keepdims=True)
 
 
-def halo_kernel(tile_cols, qbd_ref, gbd_ref, stat_ref, a_ref, b_ref, exp_ref, dw_ref, sum_ref, kx_ref, vx_ref):
-    tile_rows = qbd_ref.shape[0] // tile_cols
+def tile_row_of(group):
+    odd = lax.rem(lax.axis_index("rows"), 2)
+    return odd if group == 0 else 1 - odd
+
+
+def halo_kernel(tile_cols, group, qbd_ref, gbd_ref, stat_ref, halo_ref, exp_ref, dw_ref, sum_ref, kx_ref, vx_ref):
     edge = tile_cols * PATCH
     me = lax.axis_index("rows")
-    even = lax.rem(me, 2) == 0
-    has = (me > 0, me < lax.axis_size("rows") - 1)
+    inner = (me > 0) & (me < lax.axis_size("rows") - 1)
     for n, ref in enumerate((kx_ref, vx_ref)):
-        from_a = a_ref[n * edge : (n + 1) * edge]
-        from_b = b_ref[n * edge : (n + 1) * edge]
-        for t, halo in enumerate((jnp.where(even, from_b, from_a), jnp.where(even, from_a, from_b))):
-            ref[t] = jnp.concatenate(column_tiles(halo, tile_cols), axis=0).astype(BF)
-    for t in range(tile_rows):
-        for c in range(tile_cols):
-            tile = t * tile_cols + c
-            low, high = columns_near(c, tile_cols)
-            near = slice(low * PATCH, high * PATCH)
-            s = jnp.where(has[t], dot_nt(kx_ref[t, near], qbd_ref[tile]), -1e30)
-            d = dot_nt(vx_ref[t, near], gbd_ref[tile]).astype(BF)
-            own_top = stat_ref[tile, 0:1]
-            top = jnp.maximum(own_top, jnp.max(s, axis=0, keepdims=True))
-            e = jnp.exp(s - top)
-            ratio = jnp.exp(own_top - top)
-            exp_ref[tile, near] = e
-            dw_ref[tile, near] = d
-            sum_ref[tile, 0:1] = top
-            sum_ref[tile, 1:2] = stat_ref[tile, 1:2] * ratio + jnp.sum(e, axis=0, keepdims=True)
-            sum_ref[tile, 2:3] = stat_ref[tile, 2:3] * ratio + jnp.sum(e * d.astype(F32), axis=0, keepdims=True)
-            sum_ref[tile, 3:4] = ratio
+        ref[...] = jnp.concatenate(column_tiles(halo_ref[n * edge : (n + 1) * edge], tile_cols), axis=0).astype(BF)
+    for c in range(tile_cols):
+        tile = tile_row_of(group) * tile_cols + c
+        low, high = columns_near(c, tile_cols)
+        near = slice(low * PATCH, high * PATCH)
+        s = dot_nt(kx_ref[near], qbd_ref[tile])
+        if group == 0:
+            s = jnp.where(inner, s, -1e30)
+        d = dot_nt(vx_ref[near], gbd_ref[tile]).astype(BF)
+        own_top = stat_ref[tile, 0:1]
+        top = jnp.maximum(own_top, jnp.max(s, axis=0, keepdims=True))
+        e = jnp.exp(s - top)
+        ratio = jnp.exp(own_top - top)
+        exp_ref[c, near] = e
+        dw_ref[c, near] = d
+        sum_ref[c, 0:1] = top
+        sum_ref[c, 1:2] = stat_ref[tile, 1:2] * ratio + jnp.sum(e, axis=0, keepdims=True)
+        sum_ref[c, 2:3] = stat_ref[tile, 2:3] * ratio + jnp.sum(e * d.astype(F32), axis=0, keepdims=True)
+        sum_ref[c, 3:4] = ratio
 
 
 def far_kernel(tile_cols, split_regs, *refs):
-    qbd_ref, gbd_ref, exp_ref, dw_ref, sum_ref, a_ref = refs[:6]
+    qbd_ref, gbd_ref = refs[:2]
+    halos, a_ref = (refs[2:5], refs[5:8]), refs[8]
+    refs = refs[3:]
     edge = tile_cols * PATCH
     regs = []
     if split_regs:
@@ -200,34 +200,29 @@
     reg_outs = refs[7:]
     kr_ref[...], vr_ref[...] = regs
     feature = a_ref.shape[1]
-    tile_rows = qbd_ref.shape[0] // tile_cols
-    even = lax.rem(lax.axis_index("rows"), 2) == 0
-    if back_b_ref.shape[0] > 2 * edge:
-        back_b_ref[2 * edge :] = jnp.zeros((back_b_ref.shape[0] - 2 * edge, feature), BF)
     dk_reg = dv_reg = None
-    dk_halo, dv_halo = [], []
-    for t in range(tile_rows):
+    for group, (exp_ref, dw_ref, sum_ref) in enumerate(halos):
         dk_t = dv_t = None
         for c in range(tile_cols):
-            tile = t * tile_cols + c
+            tile = tile_row_of(group) * tile_cols + c
             q_bd = qbd_ref[tile]
             g_bd = gbd_ref[tile]
             low, high = columns_near(c, tile_cols)
             near = slice(low * PATCH, high * PATCH)
             s = dot_nt(kr_ref[...], q_bd)
             d = dot_nt(vr_ref[...], g_bd).astype(BF).astype(F32)
-            old_top = sum_ref[tile, 0:1]
+            old_top = sum_ref[c, 0:1]
             top = jnp.maximum(old_top, jnp.max(s, axis=0, keepdims=True))
             e = jnp.exp(s - top)
             ratio = jnp.exp(old_top - top)
-            inverse = 1.0 / (sum_ref[tile, 1:2] * ratio + jnp.sum(e, axis=0, keepdims=True))
-            row_dot = (sum_ref[tile, 2:3] * ratio + jnp.sum(e * d, axis=0, keepdims=True)) * inverse
+            inverse = 1.0 / (sum_ref[c, 1:2] * ratio + jnp.sum(e, axis=0, keepdims=True))
+            row_dot = (sum_ref[c, 2:3] * ratio + jnp.sum(e * d, axis=0, keepdims=True)) * inverse
             scale = ratio * inverse
-            final_ref[tile, 0:1] = sum_ref[tile, 3:4] * scale
+            final_ref[tile, 0:1] = sum_ref[c, 3:4] * scale
             final_ref[tile, 1:2] = row_dot
-            p_near = exp_ref[tile, near] * scale
+            p_near = exp_ref[c, near] * scale
             p_reg = e * inverse
-            ds_near = p_near * (dw_ref[tile, near].astype(F32) - row_dot)
+            ds_near = p_near * (dw_ref[c, near].astype(F32) - row_dot)
             ds_reg = p_reg * (d - row_dot)
             parts = []
             for x_near, x_reg in ((p_near, p_reg), (ds_near, ds_reg)):
@@ -244,14 +239,12 @@
             dv = dot_nn(weights, g_bd)
             dk_t = dk if dk_t is None else dk_t + dk
             dv_t = dv if dv_t is None else dv_t + dv
-        dk_halo.append(dk_t[:edge])
-        dv_halo.append(dv_t[:edge])
+        back_ref = (back_b_ref, back_a_ref)[group]
+        back_ref[:edge] = dk_t[:edge].astype(BF)
+        back_ref[edge : 2 * edge] = dv_t[:edge].astype(BF)
         dk_reg = dk_t[edge:] if dk_reg is None else dk_reg + dk_t[edge:]
         dv_reg = dv_t[edge:] if dv_reg is None else dv_reg + dv_t[edge:]
-    for n, (halo, reg) in enumerate(((dk_halo, dk_reg), (dv_halo, dv_reg))):
-        top, bottom = halo
-        back_a_ref[n * edge : (n + 1) * edge] = jnp.where(even, bottom, top).astype(BF)
-        back_b_ref[n * edge : (n + 1) * edge] = jnp.where(even, top, bottom).astype(BF)
+    for n, reg in enumerate((dk_reg, dv_reg)):
         if split_regs:
             base = 2 * edge + n * cut
             reg_outs[0][n] = reg[:cut]
@@ -273,8 +266,10 @@
     final_ref,
     px_ref,
     dsx_ref,
-    kx_ref,
-    vx_ref,
+    kb_ref,
+    vb_ref,
+    ka_ref,
+    va_ref,
     kr_ref,
     vr_ref,
     *refs,
@@ -285,9 +280,10 @@
     line = tile_cols * PATCH
     tile_rows = qbd_ref.shape[0] // tile_cols
     rows = tile_rows * PATCH
-    for t in range(tile_rows):
-        kxt = jnp.concatenate([kx_ref[t], kr_ref[...]], axis=0).T
-        vxt = jnp.concatenate([vx_ref[t], vr_ref[...]], axis=0).T
+    for group, (kx_ref, vx_ref) in enumerate(((kb_ref, vb_ref), (ka_ref, va_ref))):
+        t = tile_row_of(group)
+        kxt = jnp.concatenate([kx_ref[...], kr_ref[...]], axis=0).T
+        vxt = jnp.concatenate([vx_ref[...], vr_ref[...]], axis=0).T
         o_cols, dq_cols = [], []
         for c in range(tile_cols):
             tile = t * tile_cols + c
@@ -299,7 +295,7 @@
             weights = p.astype(BF)
             dk = dot_nn(d_scores, qbd_ref[tile])
             dv = dot_nn(weights, gbd_ref[tile])
-            first = t == 0
+            first = group == 0
             for ref, value in ((dk_ref, dk), (dv_ref, dv)):
                 for x in range(low, high):
                     part = value[(x - low) * rows : (x - low + 1) * rows]
@@ -311,8 +307,9 @@
             dq_t = dot_nn(kt_ref[:, near], d_scores) + dot_nn(kxt, dsx_ref[tile])
             o_cols.append(from_transposed(o_t, heads))
             dq_cols.append(from_transposed(dq_t, heads) * FACTOR)
-        o_ref[t * line : (t + 1) * line] = patch_order(o_cols).astype(BF)
-        dq_ref[t * line : (t + 1) * line] = patch_order(dq_cols).astype(BF)
+        lines = pl.ds(pl.multiple_of(t * line, line), line)
+        o_ref[lines] = patch_order(o_cols).astype(BF)
+        dq_ref[lines] = patch_order(dq_cols).astype(BF)
 
 
 def registers_kernel(part_ref, three_ref, two_ref, out_ref):
@@ -382,7 +379,6 @@
         for x in (query, keys, values, cotangent)
     )
     extra = 2 * own if split_regs else 0
-    pad = 2 * extra
     two = [(i, i ^ 2) for i in range(count)]
     three = [(i, i ^ 3) for i in range(count)]
 
@@ -393,7 +389,7 @@
         (k, v, registers),
         (
             shape((2 * edge + extra, feature), BF),
-            shape((2 * edge + pad, feature), BF),
+            shape((2 * edge, feature), BF),
             shape(registers.shape, BF),
         ),
         0,
@@ -436,23 +432,27 @@
         )
     else:
         reg_shapes = (shape((2, reg_count, feature), F32),)
-    halo_exps, halo_dw, sums, kx, vx = call(
-        functools.partial(halo_kernel, tile_cols),
-        "halo",
-        (qbd, gbd, stats, got_a, got_b),
-        (
-            shape((tiles, edge, feature), F32),
-            shape((tiles, edge, feature), BF),
-            shape((tiles, 8, feature), F32),
-            shape((tile_rows, edge, feature), BF),
-            shape((tile_rows, edge, feature), BF),
-        ),
-        4 * tiles * edge * feature * feature,
-    )
+    halos = []
+    for group, got in enumerate((got_b, got_a)):
+        halos.append(
+            call(
+                functools.partial(halo_kernel, tile_cols, group),
+                "halo",
+                (qbd, gbd, stats, got),
+                (
+                    shape((tile_cols, edge, feature), F32),
+                    shape((tile_cols, edge, feature), BF),
+                    shape((tile_cols, 8, feature), F32),
+                    shape((edge, feature), BF),
+                    shape((edge, feature), BF),
+                ),
+                32 * tile_cols * edge * feature * feature,
+            )
+        )
     final, px, dsx, kr, vr, back_a, back_b, *back_regs = call(
         functools.partial(far_kernel, tile_cols, split_regs),
         "far",
-        (qbd, gbd, halo_exps, halo_dw, sums, got_a) + regs,
+        (qbd, gbd) + tuple(halos[0][:3]) + tuple(halos[1][:3]) + (got_a,) + regs,
         (
             shape((tiles, 8, feature), F32),
             shape((tiles, window, feature), BF),
@@ -460,7 +460,7 @@
             shape((reg_count, feature), BF),
             shape((reg_count, feature), BF),
             shape((2 * edge + extra, feature), BF),
-            shape((2 * edge + pad, feature), BF),
+            shape((2 * edge, feature), BF),
         )
         + reg_shapes,
         8 * tiles * window * feature * feature,
@@ -470,7 +470,7 @@
     attended, grad_query, dk, dv = call(
         functools.partial(rest_kernel, tile_cols),
         "rest",
-        (qbd, gbd, kt, vt, exps, dw, final, px, dsx, kx, vx, kr, vr),
+        (qbd, gbd, kt, vt, exps, dw, final, px, dsx) + tuple(halos[0][3:]) + tuple(halos[1][3:]) + (kr, vr),
         (
             shape((total, feature), BF),
             shape((total, feature), BF),

time: 24.6 us -> 24.3 us (0.988)
  waiting for transfers between devices: 4.12 us -> 2.5 us
  starting transfers between devices: 10 us -> 11 us
  Pallas kernels: 9.63 us -> 9.89 us
    ppermute x6, waiting for transfers between devices: 4.11 us -> 2.49 us  [swap(): return lax.ppermute(array, 'rows', pairs)]
    ppermute x6, starting transfers between devices: 9.45 us -> 10.5 us  [swap(): return lax.ppermute(array, 'rows', pairs)]
    pallas_call x7 -> x8, Pallas kernels: 9.63 us -> 9.89 us  [call(): pl.pallas_call(kernel, out_shape=tuple(outs), in_specs=in_specs or [VMEM]...]
  transfers between devices with their start and end apart: 8 -> 8, of which waited for: 3 -> 3; matrix products, arithmetic and copies ran while one was open for 0% -> 0% of each run, Pallas kernels for 26% -> 27%
where the time goes in v6:
time: 24.3 us; the launch traced here: 24.1 us
  starting transfers between devices  11 us (45%)
  Pallas kernels  9.89 us (41%)
  waiting for transfers between devices  2.5 us (10%)
  between operations  0.68 us (3%)
    ppermute x6, starting transfers between devices, swap(): return lax.ppermute(array, 'rows', pairs)  10.5 us
    pallas_call x8, Pallas kernels, call(): pl.pallas_call(kernel, out_shape=tuple(outs), in_specs=in_specs or [VMEM]...  9.89 us
    ppermute x6, waiting for transfers between devices, swap(): return lax.ppermute(array, 'rows', pairs)  2.49 us
    ppermute x2, starting transfers between devices, swap_b(): return lax.ppermute(array, ('rows', 'cols'), pairs)  0.52 us
  transfers between devices with their start and end apart: 8, of which 3 were waited for; matrix products, arithmetic and copies ran while one was open for 0% of the time, Pallas kernels for 27%

profile of v6, /device:TPU:0, one launch (start us, length us, event | category | flops | bytes accessed | tf_op | source)
XLA Modules:
  0.0 24.1 jit_solution(5433178665603828776)
XLA Ops:
  0.6 1.1 %prepare.1 = (bf16[416,256]{1,0:T(8,128)(2,1)S(1)}, bf16[384,256]{1,0:T(8,128)(2,1)S(1)}, bf16[2,16,256]{2,1,0:T(8,128)(2,1)S(1)}) custom-call(bf16[384,256]{1,0:T(8,128)(2,1)} %bitcast.8, bf16[384,256]{1,0:T(8,128)(2,1)} %bitcast.10, bf16[2,16,256]{2,1,0:T(8,128)(2,1)} %reg_ref.1), custom_call_target="tpu_custom_call" | custom-call | bytes 835584 | tf_op jit(solution)/shard_map/prepare/pallas_call | solution.py:354
  1.8 0.5 %collective-permute-start = (bf16[384,256]{1,0:T(8,128)(2,1)S(1)}, bf16[384,256]{1,0:T(8,128)(2,1)S(1)}, u32[]{:S(2)}, u32[]{:S(2)}) collective-permute-start(bf16[384,256]{1,0:T(8,128)(2,1)S(1)} %get-tuple-element.49), channel_id=1, source_target_pairs={{0,1},{1,0},{2,3},{3,2},{4,8},{5,9},{6,10},{7,11},{8,4},{9,5},{10,... | collective-permute-start | bytes 589832 | tf_op jit(solution)/shard_map/ppermute | solution.py:36
  2.3 4.1 %collective-permute-start.1 = (bf16[416,256]{1,0:T(8,128)(2,1)S(1)}, bf16[416,256]{1,0:T(8,128)(2,1)S(1)}, u32[]{:S(2)}, u32[]{:S(2)}) collective-permute-start(bf16[416,256]{1,0:T(8,128)(2,1)S(1)} %get-tuple-element.53), channel_id=1, source_target_pairs={{0,4},{4,0},{8,12},{12,8},{1,5},{5,1},{9,13},{13,9},{2,6},{6,2},{1... | collective-permute-start | bytes 638984 | tf_op jit(solution)/shard_map/ppermute | solution.py:21
  6.4 1.3 %collective-permute-start.3 = (bf16[2,16,256]{2,1,0:T(8,128)(2,1)S(1)}, bf16[2,16,256]{2,1,0:T(8,128)(2,1)S(1)}, u32[]{:S(2)}, u32[]{:S(2)}) collective-permute-start(bf16[2,16,256]{2,1,0:T(8,128)(2,1)S(1)} %get-tuple-element.57.refs_9_), channel_id=1, source_target_pairs={{0,12},{4,8},{8,4},{12,0},{1,13},{5,9},{9,5},{13,1},{2,14},{6,10},... | collective-permute-start | bytes 49160 | tf_op jit(solution)/shard_map/ppermute | solution.py:21
  7.8 0.1 collective-permute-start.2
  7.9 2.3 %own.1 = (bf16[6,256,256]{2,1,0:T(8,128)(2,1)S(1)}, bf16[6,256,256]{2,1,0:T(8,128)(2,1)S(1)}, bf16[256,384]{1,0:T(8,128)(2,1)S(1)}, bf16[256,384]{1,0:T(8,128)(2...) custom-call(bf16[384,256]{1,0:T(8,128)(2,1)} %bitcast.12, ...), custom_call_target="tpu_custom_call" | custom-call | flops 600000000 | bytes 6340608 | tf_op jit(solution)/shard_map/own/pallas_call | solution.py:354
  10.2 0.0 collective-permute-done.halo_ref
  10.3 0.5 %halo.2 = (f32[3,192,256]{2,1,0:T(8,128)S(1)}, bf16[3,192,256]{2,1,0:T(8,128)(2,1)S(1)}, f32[3,8,256]{2,1,0:T(8,128)S(1)}, bf16[192,256]{1,0:T(8,128)(2,1)S(1)}, bf16[192,256]{1,0:T(8,128)(2,1)S(1)}) custom-call(bf16[6,256,256]{2,1,0:T(8,128)(2,1)S(1)} %get-tuple-element.42.qbd_ref.refs_0_, bf16[6,256,256]{2,1,0:T(8,128)(2,1)S(1)} %get-tuple-element.43.gbd_ref.refs_1_, ...), custom_call_target="tpu_custom_call" | custom-call | flops 1207959552 | bytes 2924544 | tf_op jit(solution)/shard_map/halo/pallas_call | solution.py:354
  10.7 0.8 %collective-permute-done.1.halo_ref.refs_8_ = bf16[416,256]{1,0:T(8,128)(2,1)S(1)} collective-permute-done((bf16[416,256]{1,0:T(8,128)(2,1)S(1)}, bf16[416,256]{1,0:T(8,128)(2,1)S(1)}, u32[]{:S(2)}, u32[]{:S(2)}) %collective-permute-start.1) | collective-permute-done | bytes 213024 | tf_op jit(solution)/shard_map/ppermute | solution.py:21
  11.6 0.5 %halo.3 = (f32[3,192,256]{2,1,0:T(8,128)S(1)}, bf16[3,192,256]{2,1,0:T(8,128)(2,1)S(1)}, f32[3,8,256]{2,1,0:T(8,128)S(1)}, bf16[192,256]{1,0:T(8,128)(2,1)S(1)}, bf16[192,256]{1,0:T(8,128)(2,1)S(1)}) custom-call(bf16[6,256,256]{2,1,0:T(8,128)(2,1)S(1)} %get-tuple-element.42.qbd_ref.refs_0_, bf16[6,256,256]{2,1,0:T(8,128)(2,1)S(1)} %get-tuple-element.43.gbd_ref.refs_1_, ...), custom_call_target="tpu_custom_call" | custom-call | flops 1207959552 | bytes 2940928 | tf_op jit(solution)/shard_map/halo/pallas_call | solution.py:354
  12.0 1.3 %collective-permute-done.3.refs_11_ = bf16[2,16,256]{2,1,0:T(8,128)(2,1)S(1)} collective-permute-done((bf16[2,16,256]{2,1,0:T(8,128)(2,1)S(1)}, bf16[2,16,256]{2,1,0:T(8,128)(2,1)S(1)}, u32[]{:S(2)}, u32[]{:S(2)}) %collective-permute-start.3) | collective-permute-done | bytes 16416 | tf_op jit(solution)/shard_map/ppermute | solution.py:21
  13.3 0.0 collective-permute-done.2.refs_10_
  13.3 1.6 %far.1 = (f32[6,8,256]{2,1,0:T(8,128)S(1)}, bf16[6,256,256]{2,1,0:T(8,128)(2,1)S(1)}, bf16[6,256,256]{2,1,0:T(8,128)(2,1)S(1)}, bf16[64,256]{1,0:T(8,128)(2,1)S(...) custom-call(bf16[6,256,256]{2,1,0:T(8,128)(2,1)S(1)} %get-tuple-elem, ...), custom_call_target="tpu_custom_call" | custom-call | flops 805306368 | bytes 5816320 | tf_op jit(solution)/shard_map/far/pallas_call | solution.py:354
  14.9 0.9 %collective-permute-start.4 = (bf16[416,256]{1,0:T(8,128)(2,1)S(1)}, bf16[416,256]{1,0:T(8,128)(2,1)S(1)}, u32[]{:S(2)}, u32[]{:S(2)}) collective-permute-start(bf16[416,256]{1,0:T(8,128)(2,1)S(1)} %get-tuple-element.71), channel_id=1, source_target_pairs={{0,4},{4,0},{8,12},{12,8},{1,5},{5,1},{9,13},{13,9},{2,6},{6,2},{1... | collective-permute-start | bytes 638984 | tf_op jit(solution)/shard_map/ppermute | solution.py:21
  15.9 0.0 collective-permute-start.5
  15.9 2.0 %collective-permute-start.6 = (bf16[2,16,256]{2,1,0:T(8,128)(2,1)S(1)}, bf16[2,16,256]{2,1,0:T(8,128)(2,1)S(1)}, u32[]{:S(2)}, u32[]{:S(2)}) collective-permute-start(bf16[2,16,256]{2,1,0:T(8,128)(2,1)S(1)} %get-tuple-element.77), channel_id=1, source_target_pairs={{0,12},{4,8},{8,4},{12,0},{1,13},{5,9},{9,5},{13,1},{2,14},{6,10},... | collective-permute-start | bytes 49160 | tf_op jit(solution)/shard_map/ppermute | solution.py:21
  17.9 2.0 %collective-permute-start.7 = (bf16[2,16,256]{2,1,0:T(8,128)(2,1)S(1)}, bf16[2,16,256]{2,1,0:T(8,128)(2,1)S(1)}, u32[]{:S(2)}, u32[]{:S(2)}) collective-permute-start(bf16[2,16,256]{2,1,0:T(8,128)(2,1)S(1)} %get-tuple-element.78), channel_id=1, source_target_pairs={{0,8},{4,12},{8,0},{12,4},{1,9},{5,13},{9,1},{13,5},{2,10},{6,14},... | collective-permute-start | bytes 49160 | tf_op jit(solution)/shard_map/ppermute | solution.py:21
  19.8 2.4 %rest.1 = (bf16[384,256]{1,0:T(8,128)(2,1)}, bf16[384,256]{1,0:T(8,128)(2,1)}, f32[3,128,256]{2,1,0:T(8,128)S(1)}, f32[3,128,256]{2,1,0:T(8,128)S(1)}) custom-call(bf16[6,256,256]{2,1,0:T(8,128)(2,1)S(1)} %get-tuple-element.42.qbd_ref.refs_0_, bf16[6,256,256]{2,1,0:T(8,128)(2,1)S(1)} %get-tuple-element.43.gbd_ref.refs_1_, ...), custom_call_target="tpu_custom_call" | custom-call | flops 600000000 | bytes 8765440 | tf_op jit(solution)/shard_map/rest/pallas_call | solution.py:354
  22.3 0.0 collective-permute-done.5.b_ref
  22.3 0.0 collective-permute-done.4.a_ref
  22.3 0.8 %finish.1 = (bf16[384,256]{1,0:T(8,128)(2,1)}, bf16[384,256]{1,0:T(8,128)(2,1)}, f32[2,16,256]{2,1,0:T(8,128)S(1)}) custom-call(f32[3,128,256]{2,1,0:T(8,128)S(1)} %get-tuple-element.69.dk_ref, f32[3,128,256]{2,1,0:T(8,128)S(1)} %get-tuple-element.70.dv_ref, bf16[416,256]{1,0:T(8,128)(2,1)S(1)} %collective-permute-done.4.a_ref, ...), custom_call_target="tpu_custom_call" | custom-call | bytes 1654784 | tf_op jit(solution)/shard_map/finish/pallas_call | solution.py:354
  23.1 0.0 collective-permute-done.6.three_ref
  23.1 0.4 %collective-permute-done.7.two_ref = bf16[2,16,256]{2,1,0:T(8,128)(2,1)S(1)} collective-permute-done((bf16[2,16,256]{2,1,0:T(8,128)(2,1)S(1)}, bf16[2,16,256]{2,1,0:T(8,128)(2,1)S(1)}, u32[]{:S(2)}, u32[]{:S(2)}) %collective-permute-start.7) | collective-permute-done | bytes 16416 | tf_op jit(solution)/shard_map/ppermute | solution.py:21
  23.5 0.6 %registers.1 = f32[2,16,256]{2,1,0:T(8,128)} custom-call(f32[2,16,256]{2,1,0:T(8,128)S(1)} %get-tuple-element.76.part_ref, bf16[2,16,256]{2,1,0:T(8,128)(2,1)S(1)} %collective-permute-done.6.three_ref, bf16[2,16,256]{2,1,0:T(8,128)(2,1)S(1)} %collective-permute-done.7.two_ref), custom_call_target="tpu_custom_call" | custom-call | bytes 98304 | tf_op jit(solution)/shard_map/registers/pallas_call | solution.py:354
Async XLA Ops:
  1.8 8.5 %collective-permute-start = (bf16[384,256]{1,0:T(8,128)(2,1)S(1)}, bf16[384,256]{1,0:T(8,128)(2,1)S(1)}, u32[]{:S(2)}, u32[]{:S(2)}) collective-permute-start(bf16[384,256]{1,0:T(8,128)(2,1)S(1)} %get-tuple-element.49), channel_id=1, source_target_pairs={{0,1},{1,0},{2,3},{3,2},{4,8},{5,9},{6,10},{7,11},{8,4},{9,5},{10,... | collective-permute-start | bytes 589832 | tf_op jit(solution)/shard_map/ppermute | solution.py:36
  2.3 9.3 %collective-permute-start.1 = (bf16[416,256]{1,0:T(8,128)(2,1)S(1)}, bf16[416,256]{1,0:T(8,128)(2,1)S(1)}, u32[]{:S(2)}, u32[]{:S(2)}) collective-permute-start(bf16[416,256]{1,0:T(8,128)(2,1)S(1)} %get-tuple-element.53), channel_id=1, source_target_pairs={{0,4},{4,0},{8,12},{12,8},{1,5},{5,1},{9,13},{13,9},{2,6},{6,2},{1... | collective-permute-start | bytes 638984 | tf_op jit(solution)/shard_map/ppermute | solution.py:21
  6.4 6.9 %collective-permute-start.3 = (bf16[2,16,256]{2,1,0:T(8,128)(2,1)S(1)}, bf16[2,16,256]{2,1,0:T(8,128)(2,1)S(1)}, u32[]{:S(2)}, u32[]{:S(2)}) collective-permute-start(bf16[2,16,256]{2,1,0:T(8,128)(2,1)S(1)} %get-tuple-element.57.refs_9_), channel_id=1, source_target_pairs={{0,12},{4,8},{8,4},{12,0},{1,13},{5,9},{9,5},{13,1},{2,14},{6,10},... | collective-permute-start | bytes 49160 | tf_op jit(solution)/shard_map/ppermute | solution.py:21
  7.8 5.6 %collective-permute-start.2 = (bf16[2,16,256]{2,1,0:T(8,128)(2,1)S(1)}, bf16[2,16,256]{2,1,0:T(8,128)(2,1)S(1)}, u32[]{:S(2)}, u32[]{:S(2)}) collective-permute-start(bf16[2,16,256]{2,1,0:T(8,128)(2,1)S(1)} %get-tuple-element.57.refs_9_), channel_id=1, source_target_pairs={{0,8},{4,12},{8,0},{12,4},{1,9},{5,13},{9,1},{13,5},{2,10},{6,14},... | collective-permute-start | bytes 49160 | tf_op jit(solution)/shard_map/ppermute | solution.py:21
  14.9 7.4 %collective-permute-start.4 = (bf16[416,256]{1,0:T(8,128)(2,1)S(1)}, bf16[416,256]{1,0:T(8,128)(2,1)S(1)}, u32[]{:S(2)}, u32[]{:S(2)}) collective-permute-start(bf16[416,256]{1,0:T(8,128)(2,1)S(1)} %get-tuple-element.71), channel_id=1, source_target_pairs={{0,4},{4,0},{8,12},{12,8},{1,5},{5,1},{9,13},{13,9},{2,6},{6,2},{1... | collective-permute-start | bytes 638984 | tf_op jit(solution)/shard_map/ppermute | solution.py:21
  15.9 6.4 %collective-permute-start.5 = (bf16[384,256]{1,0:T(8,128)(2,1)S(1)}, bf16[384,256]{1,0:T(8,128)(2,1)S(1)}, u32[]{:S(2)}, u32[]{:S(2)}) collective-permute-start(bf16[384,256]{1,0:T(8,128)(2,1)S(1)} %get-tuple-element.72), channel_id=1, source_target_pairs={{0,1},{1,0},{2,3},{3,2},{4,8},{5,9},{6,10},{7,11},{8,4},{9,5},{10,... | collective-permute-start | bytes 589832 | tf_op jit(solution)/shard_map/ppermute | solution.py:36
  15.9 7.2 %collective-permute-start.6 = (bf16[2,16,256]{2,1,0:T(8,128)(2,1)S(1)}, bf16[2,16,256]{2,1,0:T(8,128)(2,1)S(1)}, u32[]{:S(2)}, u32[]{:S(2)}) collective-permute-start(bf16[2,16,256]{2,1,0:T(8,128)(2,1)S(1)} %get-tuple-element.77), channel_id=1, source_target_pairs={{0,12},{4,8},{8,4},{12,0},{1,13},{5,9},{9,5},{13,1},{2,14},{6,10},... | collective-permute-start | bytes 49160 | tf_op jit(solution)/shard_map/ppermute | solution.py:21
  17.9 5.6 %collective-permute-start.7 = (bf16[2,16,256]{2,1,0:T(8,128)(2,1)S(1)}, bf16[2,16,256]{2,1,0:T(8,128)(2,1)S(1)}, u32[]{:S(2)}, u32[]{:S(2)}) collective-permute-start(bf16[2,16,256]{2,1,0:T(8,128)(2,1)S(1)} %get-tuple-element.78), channel_id=1, source_target_pairs={{0,8},{4,12},{8,0},{12,4},{1,9},{5,13},{9,1},{13,5},{2,10},{6,14},... | collective-permute-start | bytes 49160 | tf_op jit(solution)/shard_map/ppermute | solution.py:21

commit v7 on v6

--- a/solution.py
+++ b/solution.py
@@ -200,43 +200,47 @@
     reg_outs = refs[7:]
     kr_ref[...], vr_ref[...] = regs
     feature = a_ref.shape[1]
+    places = [(group, c) for group in range(2) for c in range(tile_cols)]
+    tiles = [tile_row_of(group) * tile_cols + c for group, c in places]
+    scores = [dot_nt(kr_ref[...], qbd_ref[tile]) for tile in tiles]
+    grads = [dot_nt(vr_ref[...], gbd_ref[tile]).astype(BF).astype(F32) for tile in tiles]
+    parts = []
+    for n, (group, c) in enumerate(places):
+        sum_ref = halos[group][2]
+        s, d = scores[n], grads[n]
+        old_top = sum_ref[c, 0:1]
+        top = jnp.maximum(old_top, jnp.max(s, axis=0, keepdims=True))
+        e = jnp.exp(s - top)
+        ratio = jnp.exp(old_top - top)
+        inverse = 1.0 / (sum_ref[c, 1:2] * ratio + jnp.sum(e, axis=0, keepdims=True))
+        row_dot = (sum_ref[c, 2:3] * ratio + jnp.sum(e * d, axis=0, keepdims=True)) * inverse
+        scale = ratio * inverse
+        final_ref[n, 0:1] = sum_ref[c, 3:4] * scale
+        final_ref[n, 1:2] = row_dot
+        p = e * inverse
+        parts.append((scale, row_dot, p.astype(BF), (p * (d - row_dot)).astype(BF)))
+    for n, (group, c) in enumerate(places):
+        exp_ref, dw_ref, _ = halos[group]
+        scale, row_dot, p_reg, ds_reg = parts[n]
+        low, high = columns_near(c, tile_cols)
+        near = slice(low * PATCH, high * PATCH)
+        p = exp_ref[c, near] * scale
+        px_ref[n, near] = p.astype(BF)
+        dsx_ref[n, near] = (p * (dw_ref[c, near].astype(F32) - row_dot)).astype(BF)
+        px_ref[n, edge:] = p_reg
+        dsx_ref[n, edge:] = ds_reg
+        for ref in (px_ref, dsx_ref):
+            if low > 0:
+                ref[n, : low * PATCH] = jnp.zeros((low * PATCH, feature), BF)
+            if high < tile_cols:
+                ref[n, high * PATCH : edge] = jnp.zeros(((tile_cols - high) * PATCH, feature), BF)
     dk_reg = dv_reg = None
-    for group, (exp_ref, dw_ref, sum_ref) in enumerate(halos):
+    for group in range(2):
         dk_t = dv_t = None
         for c in range(tile_cols):
-            tile = tile_row_of(group) * tile_cols + c
-            q_bd = qbd_ref[tile]
-            g_bd = gbd_ref[tile]
-            low, high = columns_near(c, tile_cols)
-            near = slice(low * PATCH, high * PATCH)
-            s = dot_nt(kr_ref[...], q_bd)
-            d = dot_nt(vr_ref[...], g_bd).astype(BF).astype(F32)
-            old_top = sum_ref[c, 0:1]
-            top = jnp.maximum(old_top, jnp.max(s, axis=0, keepdims=True))
-            e = jnp.exp(s - top)
-            ratio = jnp.exp(old_top - top)
-            inverse = 1.0 / (sum_ref[c, 1:2] * ratio + jnp.sum(e, axis=0, keepdims=True))
-            row_dot = (sum_ref[c, 2:3] * ratio + jnp.sum(e * d, axis=0, keepdims=True)) * inverse
-            scale = ratio * inverse
-            final_ref[tile, 0:1] = sum_ref[c, 3:4] * scale
-            final_ref[tile, 1:2] = row_dot
-            p_near = exp_ref[c, near] * scale
-            p_reg = e * inverse
-            ds_near = p_near * (dw_ref[c, near].astype(F32) - row_dot)
-            ds_reg = p_reg * (d - row_dot)
-            parts = []
-            for x_near, x_reg in ((p_near, p_reg), (ds_near, ds_reg)):
-                pieces = [x_near.astype(BF), x_reg.astype(BF)]
-                if high < tile_cols:
-                    pieces.insert(1, jnp.zeros(((tile_cols - high) * PATCH, feature), BF))
-                if low > 0:
-                    pieces.insert(0, jnp.zeros((low * PATCH, feature), BF))
-                parts.append(jnp.concatenate(pieces, axis=0))
-            weights, d_scores = parts
-            px_ref[tile] = weights
-            dsx_ref[tile] = d_scores
-            dk = dot_nn(d_scores, q_bd)
-            dv = dot_nn(weights, g_bd)
+            n = group * tile_cols + c
+            dk = dot_nn(dsx_ref[n], qbd_ref[tiles[n]])
+            dv = dot_nn(px_ref[n], gbd_ref[tiles[n]])
             dk_t = dk if dk_t is None else dk_t + dk
             dv_t = dv if dv_t is None else dv_t + dv
         back_ref = (back_b_ref, back_a_ref)[group]
@@ -287,11 +291,12 @@
         o_cols, dq_cols = [], []
         for c in range(tile_cols):
             tile = t * tile_cols + c
+            n = group * tile_cols + c
             low, high = columns_near(c, tile_cols)
             near = slice(low * rows, high * rows)
             size = (high - low) * rows
-            p = exp_ref[tile, :size] * final_ref[tile, 0:1]
-            d_scores = (p * (dw_ref[tile, :size].astype(F32) - final_ref[tile, 1:2])).astype(BF)
+            p = exp_ref[tile, :size] * final_ref[n, 0:1]
+            d_scores = (p * (dw_ref[tile, :size].astype(F32) - final_ref[n, 1:2])).astype(BF)
             weights = p.astype(BF)
             dk = dot_nn(d_scores, qbd_ref[tile])
             dv = dot_nn(weights, gbd_ref[tile])
@@ -303,8 +308,8 @@
                         ref[x] = part
                     else:
                         ref[x] += part
-            o_t = dot_nn(vt_ref[:, near], weights) + dot_nn(vxt, px_ref[tile])
-            dq_t = dot_nn(kt_ref[:, near], d_scores) + dot_nn(kxt, dsx_ref[tile])
+            o_t = dot_nn(vt_ref[:, near], weights) + dot_nn(vxt, px_ref[n])
+            dq_t = dot_nn(kt_ref[:, near], d_scores) + dot_nn(kxt, dsx_ref[n])
             o_cols.append(from_transposed(o_t, heads))
             dq_cols.append(from_transposed(dq_t, heads) * FACTOR)
         lines = pl.ds(pl.multiple_of(t * line, line), line)

time: 24.3 us -> 23.9 us (0.984)
  Pallas kernels: 9.89 us -> 9.47 us
    pallas_call x8, Pallas kernels: 9.89 us -> 9.47 us  [call(): pl.pallas_call(kernel, out_shape=tuple(outs), in_specs=in_specs or [VMEM]...]
  transfers between devices with their start and end apart: 8 -> 8, of which waited for: 3 -> 3; matrix products, arithmetic and copies ran while one was open for 0% -> 0% of each run, Pallas kernels for 27% -> 28%
where the time goes in v7:
time: 23.9 us; the launch traced here: 23.7 us
  starting transfers between devices  11 us (46%)
  Pallas kernels  9.47 us (40%)
  waiting for transfers between devices  2.48 us (10%)
  between operations  0.68 us (3%)
    ppermute x6, starting transfers between devices, swap(): return lax.ppermute(array, 'rows', pairs)  10.5 us
    pallas_call x8, Pallas kernels, call(): pl.pallas_call(kernel, out_shape=tuple(outs), in_specs=in_specs or [VMEM]...  9.47 us
    ppermute x6, waiting for transfers between devices, swap(): return lax.ppermute(array, 'rows', pairs)  2.48 us
    ppermute x2, starting transfers between devices, swap_b(): return lax.ppermute(array, ('rows', 'cols'), pairs)  0.52 us
  transfers between devices with their start and end apart: 8, of which 3 were waited for; matrix products, arithmetic and copies ran while one was open for 0% of the time, Pallas kernels for 28%

profile of v7, /device:TPU:0, one launch (start us, length us, event | category | flops | bytes accessed | tf_op | source)
XLA Modules:
  0.0 23.7 jit_solution(10798012455175277693)
XLA Ops:
  0.6 1.1 %prepare.1 = (bf16[416,256]{1,0:T(8,128)(2,1)S(1)}, bf16[384,256]{1,0:T(8,128)(2,1)S(1)}, bf16[2,16,256]{2,1,0:T(8,128)(2,1)S(1)}) custom-call(bf16[384,256]{1,0:T(8,128)(2,1)} %bitcast.8, bf16[384,256]{1,0:T(8,128)(2,1)} %bitcast.10, bf16[2,16,256]{2,1,0:T(8,128)(2,1)} %reg_ref.1), custom_call_target="tpu_custom_call" | custom-call | bytes 835584 | tf_op jit(solution)/shard_map/prepare/pallas_call | solution.py:359
  1.8 0.5 %collective-permute-start = (bf16[384,256]{1,0:T(8,128)(2,1)S(1)}, bf16[384,256]{1,0:T(8,128)(2,1)S(1)}, u32[]{:S(2)}, u32[]{:S(2)}) collective-permute-start(bf16[384,256]{1,0:T(8,128)(2,1)S(1)} %get-tuple-element.49), channel_id=1, source_target_pairs={{0,1},{1,0},{2,3},{3,2},{4,8},{5,9},{6,10},{7,11},{8,4},{9,5},{10,... | collective-permute-start | bytes 589832 | tf_op jit(solution)/shard_map/ppermute | solution.py:36
  2.3 4.1 %collective-permute-start.1 = (bf16[416,256]{1,0:T(8,128)(2,1)S(1)}, bf16[416,256]{1,0:T(8,128)(2,1)S(1)}, u32[]{:S(2)}, u32[]{:S(2)}) collective-permute-start(bf16[416,256]{1,0:T(8,128)(2,1)S(1)} %get-tuple-element.53), channel_id=1, source_target_pairs={{0,4},{4,0},{8,12},{12,8},{1,5},{5,1},{9,13},{13,9},{2,6},{6,2},{1... | collective-permute-start | bytes 638984 | tf_op jit(solution)/shard_map/ppermute | solution.py:21
  6.4 1.3 %collective-permute-start.3 = (bf16[2,16,256]{2,1,0:T(8,128)(2,1)S(1)}, bf16[2,16,256]{2,1,0:T(8,128)(2,1)S(1)}, u32[]{:S(2)}, u32[]{:S(2)}) collective-permute-start(bf16[2,16,256]{2,1,0:T(8,128)(2,1)S(1)} %get-tuple-element.57.refs_9_), channel_id=1, source_target_pairs={{0,12},{4,8},{8,4},{12,0},{1,13},{5,9},{9,5},{13,1},{2,14},{6,10},... | collective-permute-start | bytes 49160 | tf_op jit(solution)/shard_map/ppermute | solution.py:21
  7.8 0.1 collective-permute-start.2
  7.9 2.3 %own.1 = (bf16[6,256,256]{2,1,0:T(8,128)(2,1)S(1)}, bf16[6,256,256]{2,1,0:T(8,128)(2,1)S(1)}, bf16[256,384]{1,0:T(8,128)(2,1)S(1)}, bf16[256,384]{1,0:T(8,128)(2...) custom-call(bf16[384,256]{1,0:T(8,128)(2,1)} %bitcast.12, ...), custom_call_target="tpu_custom_call" | custom-call | flops 600000000 | bytes 6340608 | tf_op jit(solution)/shard_map/own/pallas_call | solution.py:359
  10.2 0.0 collective-permute-done.halo_ref
  10.3 0.5 %halo.2 = (f32[3,192,256]{2,1,0:T(8,128)S(1)}, bf16[3,192,256]{2,1,0:T(8,128)(2,1)S(1)}, f32[3,8,256]{2,1,0:T(8,128)S(1)}, bf16[192,256]{1,0:T(8,128)(2,1)S(1)}, bf16[192,256]{1,0:T(8,128)(2,1)S(1)}) custom-call(bf16[6,256,256]{2,1,0:T(8,128)(2,1)S(1)} %get-tuple-element.42.qbd_ref.refs_0_, bf16[6,256,256]{2,1,0:T(8,128)(2,1)S(1)} %get-tuple-element.43.gbd_ref.refs_1_, ...), custom_call_target="tpu_custom_call" | custom-call | flops 1207959552 | bytes 2924544 | tf_op jit(solution)/shard_map/halo/pallas_call | solution.py:359
  10.7 0.8 %collective-permute-done.1.halo_ref.refs_8_ = bf16[416,256]{1,0:T(8,128)(2,1)S(1)} collective-permute-done((bf16[416,256]{1,0:T(8,128)(2,1)S(1)}, bf16[416,256]{1,0:T(8,128)(2,1)S(1)}, u32[]{:S(2)}, u32[]{:S(2)}) %collective-permute-start.1) | collective-permute-done | bytes 213024 | tf_op jit(solution)/shard_map/ppermute | solution.py:21
  11.6 0.5 %halo.3 = (f32[3,192,256]{2,1,0:T(8,128)S(1)}, bf16[3,192,256]{2,1,0:T(8,128)(2,1)S(1)}, f32[3,8,256]{2,1,0:T(8,128)S(1)}, bf16[192,256]{1,0:T(8,128)(2,1)S(1)}, bf16[192,256]{1,0:T(8,128)(2,1)S(1)}) custom-call(bf16[6,256,256]{2,1,0:T(8,128)(2,1)S(1)} %get-tuple-element.42.qbd_ref.refs_0_, bf16[6,256,256]{2,1,0:T(8,128)(2,1)S(1)} %get-tuple-element.43.gbd_ref.refs_1_, ...), custom_call_target="tpu_custom_call" | custom-call | flops 1207959552 | bytes 2940928 | tf_op jit(solution)/shard_map/halo/pallas_call | solution.py:359
  12.0 1.3 %collective-permute-done.3.refs_11_ = bf16[2,16,256]{2,1,0:T(8,128)(2,1)S(1)} collective-permute-done((bf16[2,16,256]{2,1,0:T(8,128)(2,1)S(1)}, bf16[2,16,256]{2,1,0:T(8,128)(2,1)S(1)}, u32[]{:S(2)}, u32[]{:S(2)}) %collective-permute-start.3) | collective-permute-done | bytes 16416 | tf_op jit(solution)/shard_map/ppermute | solution.py:21
  13.3 0.0 collective-permute-done.2.refs_10_
  13.3 1.2 %far.1 = (f32[6,8,256]{2,1,0:T(8,128)S(1)}, bf16[6,256,256]{2,1,0:T(8,128)(2,1)S(1)}, bf16[6,256,256]{2,1,0:T(8,128)(2,1)S(1)}, bf16[64,256]{1,0:T(8,128)(2,1)S(...) custom-call(bf16[6,256,256]{2,1,0:T(8,128)(2,1)S(1)} %get-tuple-elem, ...), custom_call_target="tpu_custom_call" | custom-call | flops 805306368 | bytes 5816320 | tf_op jit(solution)/shard_map/far/pallas_call | solution.py:359
  14.5 0.9 %collective-permute-start.4 = (bf16[416,256]{1,0:T(8,128)(2,1)S(1)}, bf16[416,256]{1,0:T(8,128)(2,1)S(1)}, u32[]{:S(2)}, u32[]{:S(2)}) collective-permute-start(bf16[416,256]{1,0:T(8,128)(2,1)S(1)} %get-tuple-element.71), channel_id=1, source_target_pairs={{0,4},{4,0},{8,12},{12,8},{1,5},{5,1},{9,13},{13,9},{2,6},{6,2},{1... | collective-permute-start | bytes 638984 | tf_op jit(solution)/shard_map/ppermute | solution.py:21
  15.4 0.0 collective-permute-start.5
  15.4 2.0 %collective-permute-start.6 = (bf16[2,16,256]{2,1,0:T(8,128)(2,1)S(1)}, bf16[2,16,256]{2,1,0:T(8,128)(2,1)S(1)}, u32[]{:S(2)}, u32[]{:S(2)}) collective-permute-start(bf16[2,16,256]{2,1,0:T(8,128)(2,1)S(1)} %get-tuple-element.77), channel_id=1, source_target_pairs={{0,12},{4,8},{8,4},{12,0},{1,13},{5,9},{9,5},{13,1},{2,14},{6,10},... | collective-permute-start | bytes 49160 | tf_op jit(solution)/shard_map/ppermute | solution.py:21
  17.4 2.0 %collective-permute-start.7 = (bf16[2,16,256]{2,1,0:T(8,128)(2,1)S(1)}, bf16[2,16,256]{2,1,0:T(8,128)(2,1)S(1)}, u32[]{:S(2)}, u32[]{:S(2)}) collective-permute-start(bf16[2,16,256]{2,1,0:T(8,128)(2,1)S(1)} %get-tuple-element.78), channel_id=1, source_target_pairs={{0,8},{4,12},{8,0},{12,4},{1,9},{5,13},{9,1},{13,5},{2,10},{6,14},... | collective-permute-start | bytes 49160 | tf_op jit(solution)/shard_map/ppermute | solution.py:21
  19.4 2.5 %rest.1 = (bf16[384,256]{1,0:T(8,128)(2,1)}, bf16[384,256]{1,0:T(8,128)(2,1)}, f32[3,128,256]{2,1,0:T(8,128)S(1)}, f32[3,128,256]{2,1,0:T(8,128)S(1)}) custom-call(bf16[6,256,256]{2,1,0:T(8,128)(2,1)S(1)} %get-tuple-element.42.qbd_ref.refs_0_, bf16[6,256,256]{2,1,0:T(8,128)(2,1)S(1)} %get-tuple-element.43.gbd_ref.refs_1_, ...), custom_call_target="tpu_custom_call" | custom-call | flops 600000000 | bytes 8765440 | tf_op jit(solution)/shard_map/rest/pallas_call | solution.py:359
  21.9 0.0 collective-permute-done.5.b_ref
  21.9 0.0 collective-permute-done.4.a_ref
  21.9 0.8 %finish.1 = (bf16[384,256]{1,0:T(8,128)(2,1)}, bf16[384,256]{1,0:T(8,128)(2,1)}, f32[2,16,256]{2,1,0:T(8,128)S(1)}) custom-call(f32[3,128,256]{2,1,0:T(8,128)S(1)} %get-tuple-element.69.dk_ref, f32[3,128,256]{2,1,0:T(8,128)S(1)} %get-tuple-element.70.dv_ref, bf16[416,256]{1,0:T(8,128)(2,1)S(1)} %collective-permute-done.4.a_ref, ...), custom_call_target="tpu_custom_call" | custom-call | bytes 1654784 | tf_op jit(solution)/shard_map/finish/pallas_call | solution.py:359
  22.7 0.0 collective-permute-done.6.three_ref
  22.7 0.4 %collective-permute-done.7.two_ref = bf16[2,16,256]{2,1,0:T(8,128)(2,1)S(1)} collective-permute-done((bf16[2,16,256]{2,1,0:T(8,128)(2,1)S(1)}, bf16[2,16,256]{2,1,0:T(8,128)(2,1)S(1)}, u32[]{:S(2)}, u32[]{:S(2)}) %collective-permute-start.7) | collective-permute-done | bytes 16416 | tf_op jit(solution)/shard_map/ppermute | solution.py:21
  23.0 0.6 %registers.1 = f32[2,16,256]{2,1,0:T(8,128)} custom-call(f32[2,16,256]{2,1,0:T(8,128)S(1)} %get-tuple-element.76.part_ref, bf16[2,16,256]{2,1,0:T(8,128)(2,1)S(1)} %collective-permute-done.6.three_ref, bf16[2,16,256]{2,1,0:T(8,128)(2,1)S(1)} %collective-permute-done.7.two_ref), custom_call_target="tpu_custom_call" | custom-call | bytes 98304 | tf_op jit(solution)/shard_map/registers/pallas_call | solution.py:359
Async XLA Ops:
  1.8 8.5 %collective-permute-start = (bf16[384,256]{1,0:T(8,128)(2,1)S(1)}, bf16[384,256]{1,0:T(8,128)(2,1)S(1)}, u32[]{:S(2)}, u32[]{:S(2)}) collective-permute-start(bf16[384,256]{1,0:T(8,128)(2,1)S(1)} %get-tuple-element.49), channel_id=1, source_target_pairs={{0,1},{1,0},{2,3},{3,2},{4,8},{5,9},{6,10},{7,11},{8,4},{9,5},{10,... | collective-permute-start | bytes 589832 | tf_op jit(solution)/shard_map/ppermute | solution.py:36
  2.3 9.3 %collective-permute-start.1 = (bf16[416,256]{1,0:T(8,128)(2,1)S(1)}, bf16[416,256]{1,0:T(8,128)(2,1)S(1)}, u32[]{:S(2)}, u32[]{:S(2)}) collective-permute-start(bf16[416,256]{1,0:T(8,128)(2,1)S(1)} %get-tuple-element.53), channel_id=1, source_target_pairs={{0,4},{4,0},{8,12},{12,8},{1,5},{5,1},{9,13},{13,9},{2,6},{6,2},{1... | collective-permute-start | bytes 638984 | tf_op jit(solution)/shard_map/ppermute | solution.py:21
  6.4 6.9 %collective-permute-start.3 = (bf16[2,16,256]{2,1,0:T(8,128)(2,1)S(1)}, bf16[2,16,256]{2,1,0:T(8,128)(2,1)S(1)}, u32[]{:S(2)}, u32[]{:S(2)}) collective-permute-start(bf16[2,16,256]{2,1,0:T(8,128)(2,1)S(1)} %get-tuple-element.57.refs_9_), channel_id=1, source_target_pairs={{0,12},{4,8},{8,4},{12,0},{1,13},{5,9},{9,5},{13,1},{2,14},{6,10},... | collective-permute-start | bytes 49160 | tf_op jit(solution)/shard_map/ppermute | solution.py:21
  7.8 5.6 %collective-permute-start.2 = (bf16[2,16,256]{2,1,0:T(8,128)(2,1)S(1)}, bf16[2,16,256]{2,1,0:T(8,128)(2,1)S(1)}, u32[]{:S(2)}, u32[]{:S(2)}) collective-permute-start(bf16[2,16,256]{2,1,0:T(8,128)(2,1)S(1)} %get-tuple-element.57.refs_9_), channel_id=1, source_target_pairs={{0,8},{4,12},{8,0},{12,4},{1,9},{5,13},{9,1},{13,5},{2,10},{6,14},... | collective-permute-start | bytes 49160 | tf_op jit(solution)/shard_map/ppermute | solution.py:21
  14.5 7.4 %collective-permute-start.4 = (bf16[416,256]{1,0:T(8,128)(2,1)S(1)}, bf16[416,256]{1,0:T(8,128)(2,1)S(1)}, u32[]{:S(2)}, u32[]{:S(2)}) collective-permute-start(bf16[416,256]{1,0:T(8,128)(2,1)S(1)} %get-tuple-element.71), channel_id=1, source_target_pairs={{0,4},{4,0},{8,12},{12,8},{1,5},{5,1},{9,13},{13,9},{2,6},{6,2},{1... | collective-permute-start | bytes 638984 | tf_op jit(solution)/shard_map/ppermute | solution.py:21
  15.4 6.4 %collective-permute-start.5 = (bf16[384,256]{1,0:T(8,128)(2,1)S(1)}, bf16[384,256]{1,0:T(8,128)(2,1)S(1)}, u32[]{:S(2)}, u32[]{:S(2)}) collective-permute-start(bf16[384,256]{1,0:T(8,128)(2,1)S(1)} %get-tuple-element.72), channel_id=1, source_target_pairs={{0,1},{1,0},{2,3},{3,2},{4,8},{5,9},{6,10},{7,11},{8,4},{9,5},{10,... | collective-permute-start | bytes 589832 | tf_op jit(solution)/shard_map/ppermute | solution.py:36
  15.4 7.3 %collective-permute-start.6 = (bf16[2,16,256]{2,1,0:T(8,128)(2,1)S(1)}, bf16[2,16,256]{2,1,0:T(8,128)(2,1)S(1)}, u32[]{:S(2)}, u32[]{:S(2)}) collective-permute-start(bf16[2,16,256]{2,1,0:T(8,128)(2,1)S(1)} %get-tuple-element.77), channel_id=1, source_target_pairs={{0,12},{4,8},{8,4},{12,0},{1,13},{5,9},{9,5},{13,1},{2,14},{6,10},... | collective-permute-start | bytes 49160 | tf_op jit(solution)/shard_map/ppermute | solution.py:21
  17.4 5.6 %collective-permute-start.7 = (bf16[2,16,256]{2,1,0:T(8,128)(2,1)S(1)}, bf16[2,16,256]{2,1,0:T(8,128)(2,1)S(1)}, u32[]{:S(2)}, u32[]{:S(2)}) collective-permute-start(bf16[2,16,256]{2,1,0:T(8,128)(2,1)S(1)} %get-tuple-element.78), channel_id=1, source_target_pairs={{0,8},{4,12},{8,0},{12,4},{1,9},{5,13},{9,1},{13,5},{2,10},{6,14},... | collective-permute-start | bytes 49160 | tf_op jit(solution)/shard_map/ppermute | solution.py:21

commit v8 on v7

--- a/solution.py
+++ b/solution.py
@@ -278,43 +278,54 @@
     vr_ref,
     *refs,
 ):
-    o_ref, dq_ref, dk_ref, dv_ref = refs[:4]
+    o_ref, dq_ref, dk_ref, dv_ref, weights_ref, ds_ref, held_o_ref, held_dq_ref, sems = refs
     feature = kt_ref.shape[0]
     heads = feature // HEAD
     line = tile_cols * PATCH
     tile_rows = qbd_ref.shape[0] // tile_cols
     rows = tile_rows * PATCH
+    places = [(group, c) for group in range(2) for c in range(tile_cols)]
+    tiles = [tile_row_of(group) * tile_cols + c for group, c in places]
+    for n, (_, c) in enumerate(places):
+        low, high = columns_near(c, tile_cols)
+        size = (high - low) * rows
+        p = exp_ref[tiles[n], :size] * final_ref[n, 0:1]
+        weights_ref[n, :size] = p.astype(BF)
+        ds_ref[n, :size] = (p * (dw_ref[tiles[n], :size].astype(F32) - final_ref[n, 1:2])).astype(BF)
+    copies = []
     for group, (kx_ref, vx_ref) in enumerate(((kb_ref, vb_ref), (ka_ref, va_ref))):
-        t = tile_row_of(group)
         kxt = jnp.concatenate([kx_ref[...], kr_ref[...]], axis=0).T
         vxt = jnp.concatenate([vx_ref[...], vr_ref[...]], axis=0).T
         o_cols, dq_cols = [], []
         for c in range(tile_cols):
-            tile = t * tile_cols + c
             n = group * tile_cols + c
             low, high = columns_near(c, tile_cols)
             near = slice(low * rows, high * rows)
             size = (high - low) * rows
-            p = exp_ref[tile, :size] * final_ref[n, 0:1]
-            d_scores = (p * (dw_ref[tile, :size].astype(F32) - final_ref[n, 1:2])).astype(BF)
-            weights = p.astype(BF)
-            dk = dot_nn(d_scores, qbd_ref[tile])
-            dv = dot_nn(weights, gbd_ref[tile])
-            first = group == 0
-            for ref, value in ((dk_ref, dk), (dv_ref, dv)):
-                for x in range(low, high):
-                    part = value[(x - low) * rows : (x - low + 1) * rows]
-                    if first and (x == c + 1 or (c == 0)):
-                        ref[x] = part
-                    else:
-                        ref[x] += part
-            o_t = dot_nn(vt_ref[:, near], weights) + dot_nn(vxt, px_ref[n])
-            dq_t = dot_nn(kt_ref[:, near], d_scores) + dot_nn(kxt, dsx_ref[n])
+            o_t = dot_nn(vt_ref[:, near], weights_ref[n, :size]) + dot_nn(vxt, px_ref[n])
+            dq_t = dot_nn(kt_ref[:, near], ds_ref[n, :size]) + dot_nn(kxt, dsx_ref[n])
             o_cols.append(from_transposed(o_t, heads))
             dq_cols.append(from_transposed(dq_t, heads) * FACTOR)
-        lines = pl.ds(pl.multiple_of(t * line, line), line)
-        o_ref[lines] = patch_order(o_cols).astype(BF)
-        dq_ref[lines] = patch_order(dq_cols).astype(BF)
+        lines = pl.ds(pl.multiple_of(tile_row_of(group) * line, line), line)
+        for out_ref, columns, held_ref in ((o_ref, o_cols, held_o_ref), (dq_ref, dq_cols, held_dq_ref)):
+            held_ref[group] = patch_order(columns).astype(BF)
+            copies.append(pltpu.make_async_copy(held_ref.at[group], out_ref.at[lines], sems.at[len(copies)]))
+            copies[-1].start()
+    sums_k, sums_v = [None] * tile_cols, [None] * tile_cols
+    for n, (_, c) in enumerate(places):
+        low, high = columns_near(c, tile_cols)
+        size = (high - low) * rows
+        dk = dot_nn(ds_ref[n, :size], qbd_ref[tiles[n]])
+        dv = dot_nn(weights_ref[n, :size], gbd_ref[tiles[n]])
+        for sums, value in ((sums_k, dk), (sums_v, dv)):
+            for x in range(low, high):
+                part = value[(x - low) * rows : (x - low + 1) * rows]
+                sums[x] = part if sums[x] is None else sums[x] + part
+    for x in range(tile_cols):
+        dk_ref[x] = sums_k[x]
+        dv_ref[x] = sums_v[x]
+    for copy in copies:
+        copy.wait()
 
 
 def registers_kernel(part_ref, three_ref, two_ref, out_ref):
@@ -354,13 +365,13 @@
     return jax.ShapeDtypeStruct(dims, dtype)
 
 
-def call(kernel, name, ins, outs, flops, in_specs=None, scratch=()):
+def call(kernel, name, ins, outs, flops, in_specs=None, out_specs=None, scratch=()):
     size = sum(x.size * x.dtype.itemsize for x in ins) + sum(x.size * x.dtype.itemsize for x in outs)
     return pl.pallas_call(
         kernel,
         out_shape=tuple(outs),
         in_specs=in_specs or [VMEM] * len(ins),
-        out_specs=(VMEM,) * len(outs),
+        out_specs=out_specs or (VMEM,) * len(outs),
         scratch_shapes=list(scratch),
         compiler_params=pltpu.CompilerParams(vmem_limit_bytes=24 * 1024 * 1024),
         cost_estimate=pl.CostEstimate(flops=flops, bytes_accessed=size, transcendentals=0),
@@ -483,6 +494,10 @@
             shape((tile_cols, rows, feature), F32),
         ),
         600_000_000,
+        out_specs=(HBM, HBM, VMEM, VMEM),
+        scratch=[pltpu.VMEM((tiles, most, feature), BF)] * 2
+        + [pltpu.VMEM((tile_rows, edge, feature), BF)] * 2
+        + [pltpu.SemaphoreType.DMA((4,))],
     )
     mine = (back_regs[0],) if split_regs else ()
     grad_keys, grad_values, *part = call(

time: 23.9 us -> 23.9 us (level)
  transfers between devices with their start and end apart: 8 -> 8, of which waited for: 3 -> 3; matrix products, arithmetic and copies ran while one was open for 0% -> 0% of each run, Pallas kernels for 28% -> 27%
where the time goes in v8:
time: 23.9 us; the launch traced here: 23.7 us
  starting transfers between devices  11 us (46%)
  Pallas kernels  9.27 us (39%)
  waiting for transfers between devices  2.66 us (11%)
  between operations  0.7 us (3%)
    ppermute x6, starting transfers between devices, swap(): return lax.ppermute(array, 'rows', pairs)  10.5 us
    pallas_call x8, Pallas kernels, call(): pl.pallas_call(kernel, out_shape=tuple(outs), in_specs=in_specs or [VMEM]...  9.27 us
    ppermute x6, waiting for transfers between devices, swap(): return lax.ppermute(array, 'rows', pairs)  2.65 us
    ppermute x2, starting transfers between devices, swap_b(): return lax.ppermute(array, ('rows', 'cols'), pairs)  0.52 us
  transfers between devices with their start and end apart: 8, of which 3 were waited for; matrix products, arithmetic and copies ran while one was open for 0% of the time, Pallas kernels for 27%

profile of v8, /device:TPU:0, one launch (start us, length us, event | category | flops | bytes accessed | tf_op | source)
XLA Modules:
  0.0 23.7 jit_solution(9315866264006550413)
XLA Ops:
  0.6 1.1 %prepare.1 = (bf16[416,256]{1,0:T(8,128)(2,1)S(1)}, bf16[384,256]{1,0:T(8,128)(2,1)S(1)}, bf16[2,16,256]{2,1,0:T(8,128)(2,1)S(1)}) custom-call(bf16[384,256]{1,0:T(8,128)(2,1)} %bitcast.8, bf16[384,256]{1,0:T(8,128)(2,1)} %bitcast.10, bf16[2,16,256]{2,1,0:T(8,128)(2,1)} %reg_ref.1), custom_call_target="tpu_custom_call" | custom-call | bytes 835584 | tf_op jit(solution)/shard_map/prepare/pallas_call | solution.py:370
  1.8 0.5 %collective-permute-start = (bf16[384,256]{1,0:T(8,128)(2,1)S(1)}, bf16[384,256]{1,0:T(8,128)(2,1)S(1)}, u32[]{:S(2)}, u32[]{:S(2)}) collective-permute-start(bf16[384,256]{1,0:T(8,128)(2,1)S(1)} %get-tuple-element.49), channel_id=1, source_target_pairs={{0,1},{1,0},{2,3},{3,2},{4,8},{5,9},{6,10},{7,11},{8,4},{9,5},{10,... | collective-permute-start | bytes 589832 | tf_op jit(solution)/shard_map/ppermute | solution.py:36
  2.3 4.1 %collective-permute-start.1 = (bf16[416,256]{1,0:T(8,128)(2,1)S(1)}, bf16[416,256]{1,0:T(8,128)(2,1)S(1)}, u32[]{:S(2)}, u32[]{:S(2)}) collective-permute-start(bf16[416,256]{1,0:T(8,128)(2,1)S(1)} %get-tuple-element.53), channel_id=1, source_target_pairs={{0,4},{4,0},{8,12},{12,8},{1,5},{5,1},{9,13},{13,9},{2,6},{6,2},{1... | collective-permute-start | bytes 638984 | tf_op jit(solution)/shard_map/ppermute | solution.py:21
  6.4 1.3 %collective-permute-start.3 = (bf16[2,16,256]{2,1,0:T(8,128)(2,1)S(1)}, bf16[2,16,256]{2,1,0:T(8,128)(2,1)S(1)}, u32[]{:S(2)}, u32[]{:S(2)}) collective-permute-start(bf16[2,16,256]{2,1,0:T(8,128)(2,1)S(1)} %get-tuple-element.57.refs_9_), channel_id=1, source_target_pairs={{0,12},{4,8},{8,4},{12,0},{1,13},{5,9},{9,5},{13,1},{2,14},{6,10},... | collective-permute-start | bytes 49160 | tf_op jit(solution)/shard_map/ppermute | solution.py:21
  7.8 0.1 collective-permute-start.2
  7.9 2.3 %own.1 = (bf16[6,256,256]{2,1,0:T(8,128)(2,1)S(1)}, bf16[6,256,256]{2,1,0:T(8,128)(2,1)S(1)}, bf16[256,384]{1,0:T(8,128)(2,1)S(1)}, bf16[256,384]{1,0:T(8,128)(2...) custom-call(bf16[384,256]{1,0:T(8,128)(2,1)} %bitcast.12, ...), custom_call_target="tpu_custom_call" | custom-call | flops 600000000 | bytes 6340608 | tf_op jit(solution)/shard_map/own/pallas_call | solution.py:370
  10.2 0.0 collective-permute-done.halo_ref
  10.3 0.5 %halo.2 = (f32[3,192,256]{2,1,0:T(8,128)S(1)}, bf16[3,192,256]{2,1,0:T(8,128)(2,1)S(1)}, f32[3,8,256]{2,1,0:T(8,128)S(1)}, bf16[192,256]{1,0:T(8,128)(2,1)S(1)}, bf16[192,256]{1,0:T(8,128)(2,1)S(1)}) custom-call(bf16[6,256,256]{2,1,0:T(8,128)(2,1)S(1)} %get-tuple-element.42.qbd_ref.refs_0_, bf16[6,256,256]{2,1,0:T(8,128)(2,1)S(1)} %get-tuple-element.43.gbd_ref.refs_1_, ...), custom_call_target="tpu_custom_call" | custom-call | flops 1207959552 | bytes 2924544 | tf_op jit(solution)/shard_map/halo/pallas_call | solution.py:370
  10.7 0.8 %collective-permute-done.1.halo_ref.refs_8_ = bf16[416,256]{1,0:T(8,128)(2,1)S(1)} collective-permute-done((bf16[416,256]{1,0:T(8,128)(2,1)S(1)}, bf16[416,256]{1,0:T(8,128)(2,1)S(1)}, u32[]{:S(2)}, u32[]{:S(2)}) %collective-permute-start.1) | collective-permute-done | bytes 213024 | tf_op jit(solution)/shard_map/ppermute | solution.py:21
  11.6 0.5 %halo.3 = (f32[3,192,256]{2,1,0:T(8,128)S(1)}, bf16[3,192,256]{2,1,0:T(8,128)(2,1)S(1)}, f32[3,8,256]{2,1,0:T(8,128)S(1)}, bf16[192,256]{1,0:T(8,128)(2,1)S(1)}, bf16[192,256]{1,0:T(8,128)(2,1)S(1)}) custom-call(bf16[6,256,256]{2,1,0:T(8,128)(2,1)S(1)} %get-tuple-element.42.qbd_ref.refs_0_, bf16[6,256,256]{2,1,0:T(8,128)(2,1)S(1)} %get-tuple-element.43.gbd_ref.refs_1_, ...), custom_call_target="tpu_custom_call" | custom-call | flops 1207959552 | bytes 2940928 | tf_op jit(solution)/shard_map/halo/pallas_call | solution.py:370
  12.0 1.3 %collective-permute-done.3.refs_11_ = bf16[2,16,256]{2,1,0:T(8,128)(2,1)S(1)} collective-permute-done((bf16[2,16,256]{2,1,0:T(8,128)(2,1)S(1)}, bf16[2,16,256]{2,1,0:T(8,128)(2,1)S(1)}, u32[]{:S(2)}, u32[]{:S(2)}) %collective-permute-start.3) | collective-permute-done | bytes 16416 | tf_op jit(solution)/shard_map/ppermute | solution.py:21
  13.3 0.0 collective-permute-done.2.refs_10_
  13.3 1.2 %far.1 = (f32[6,8,256]{2,1,0:T(8,128)S(1)}, bf16[6,256,256]{2,1,0:T(8,128)(2,1)S(1)}, bf16[6,256,256]{2,1,0:T(8,128)(2,1)S(1)}, bf16[64,256]{1,0:T(8,128)(2,1)S(...) custom-call(bf16[6,256,256]{2,1,0:T(8,128)(2,1)S(1)} %get-tuple-elem, ...), custom_call_target="tpu_custom_call" | custom-call | flops 805306368 | bytes 5816320 | tf_op jit(solution)/shard_map/far/pallas_call | solution.py:370
  14.5 0.9 %collective-permute-start.4 = (bf16[416,256]{1,0:T(8,128)(2,1)S(1)}, bf16[416,256]{1,0:T(8,128)(2,1)S(1)}, u32[]{:S(2)}, u32[]{:S(2)}) collective-permute-start(bf16[416,256]{1,0:T(8,128)(2,1)S(1)} %get-tuple-element.71), channel_id=1, source_target_pairs={{0,4},{4,0},{8,12},{12,8},{1,5},{5,1},{9,13},{13,9},{2,6},{6,2},{1... | collective-permute-start | bytes 638984 | tf_op jit(solution)/shard_map/ppermute | solution.py:21
  15.4 0.0 collective-permute-start.5
  15.4 2.0 %collective-permute-start.6 = (bf16[2,16,256]{2,1,0:T(8,128)(2,1)S(1)}, bf16[2,16,256]{2,1,0:T(8,128)(2,1)S(1)}, u32[]{:S(2)}, u32[]{:S(2)}) collective-permute-start(bf16[2,16,256]{2,1,0:T(8,128)(2,1)S(1)} %get-tuple-element.77), channel_id=1, source_target_pairs={{0,12},{4,8},{8,4},{12,0},{1,13},{5,9},{9,5},{13,1},{2,14},{6,10},... | collective-permute-start | bytes 49160 | tf_op jit(solution)/shard_map/ppermute | solution.py:21
  17.4 2.0 %collective-permute-start.7 = (bf16[2,16,256]{2,1,0:T(8,128)(2,1)S(1)}, bf16[2,16,256]{2,1,0:T(8,128)(2,1)S(1)}, u32[]{:S(2)}, u32[]{:S(2)}) collective-permute-start(bf16[2,16,256]{2,1,0:T(8,128)(2,1)S(1)} %get-tuple-element.78), channel_id=1, source_target_pairs={{0,8},{4,12},{8,0},{12,4},{1,9},{5,13},{9,1},{13,5},{2,10},{6,14},... | collective-permute-start | bytes 49160 | tf_op jit(solution)/shard_map/ppermute | solution.py:21
  19.4 2.3 %rest.1 = (bf16[384,256]{1,0:T(8,128)(2,1)}, bf16[384,256]{1,0:T(8,128)(2,1)}, f32[3,128,256]{2,1,0:T(8,128)S(1)}, f32[3,128,256]{2,1,0:T(8,128)S(1)}) custom-call(bf16[6,256,256]{2,1,0:T(8,128)(2,1)S(1)} %get-tuple-element.42.qbd_ref.refs_0_, bf16[6,256,256]{2,1,0:T(8,128)(2,1)S(1)} %get-tuple-element.43.gbd_ref.refs_1_, ...), custom_call_target="tpu_custom_call" | custom-call | flops 600000000 | bytes 8765440 | tf_op jit(solution)/shard_map/rest/pallas_call | solution.py:370
  21.7 0.0 collective-permute-done.5.b_ref
  21.7 0.0 collective-permute-done.4.a_ref
  21.7 0.8 %finish.1 = (bf16[384,256]{1,0:T(8,128)(2,1)}, bf16[384,256]{1,0:T(8,128)(2,1)}, f32[2,16,256]{2,1,0:T(8,128)S(1)}) custom-call(f32[3,128,256]{2,1,0:T(8,128)S(1)} %get-tuple-element.69.dk_ref, f32[3,128,256]{2,1,0:T(8,128)S(1)} %get-tuple-element.70.dv_ref, bf16[416,256]{1,0:T(8,128)(2,1)S(1)} %collective-permute-done.4.a_ref, ...), custom_call_target="tpu_custom_call" | custom-call | bytes 1654784 | tf_op jit(solution)/shard_map/finish/pallas_call | solution.py:370
  22.5 0.0 collective-permute-done.6.three_ref
  22.5 0.5 %collective-permute-done.7.two_ref = bf16[2,16,256]{2,1,0:T(8,128)(2,1)S(1)} collective-permute-done((bf16[2,16,256]{2,1,0:T(8,128)(2,1)S(1)}, bf16[2,16,256]{2,1,0:T(8,128)(2,1)S(1)}, u32[]{:S(2)}, u32[]{:S(2)}) %collective-permute-start.7) | collective-permute-done | bytes 16416 | tf_op jit(solution)/shard_map/ppermute | solution.py:21
  23.0 0.6 %registers.1 = f32[2,16,256]{2,1,0:T(8,128)} custom-call(f32[2,16,256]{2,1,0:T(8,128)S(1)} %get-tuple-element.76.part_ref, bf16[2,16,256]{2,1,0:T(8,128)(2,1)S(1)} %collective-permute-done.6.three_ref, bf16[2,16,256]{2,1,0:T(8,128)(2,1)S(1)} %collective-permute-done.7.two_ref), custom_call_target="tpu_custom_call" | custom-call | bytes 98304 | tf_op jit(solution)/shard_map/registers/pallas_call | solution.py:370
Async XLA Ops:
  1.8 8.5 %collective-permute-start = (bf16[384,256]{1,0:T(8,128)(2,1)S(1)}, bf16[384,256]{1,0:T(8,128)(2,1)S(1)}, u32[]{:S(2)}, u32[]{:S(2)}) collective-permute-start(bf16[384,256]{1,0:T(8,128)(2,1)S(1)} %get-tuple-element.49), channel_id=1, source_target_pairs={{0,1},{1,0},{2,3},{3,2},{4,8},{5,9},{6,10},{7,11},{8,4},{9,5},{10,... | collective-permute-start | bytes 589832 | tf_op jit(solution)/shard_map/ppermute | solution.py:36
  2.3 9.3 %collective-permute-start.1 = (bf16[416,256]{1,0:T(8,128)(2,1)S(1)}, bf16[416,256]{1,0:T(8,128)(2,1)S(1)}, u32[]{:S(2)}, u32[]{:S(2)}) collective-permute-start(bf16[416,256]{1,0:T(8,128)(2,1)S(1)} %get-tuple-element.53), channel_id=1, source_target_pairs={{0,4},{4,0},{8,12},{12,8},{1,5},{5,1},{9,13},{13,9},{2,6},{6,2},{1... | collective-permute-start | bytes 638984 | tf_op jit(solution)/shard_map/ppermute | solution.py:21
  6.4 6.9 %collective-permute-start.3 = (bf16[2,16,256]{2,1,0:T(8,128)(2,1)S(1)}, bf16[2,16,256]{2,1,0:T(8,128)(2,1)S(1)}, u32[]{:S(2)}, u32[]{:S(2)}) collective-permute-start(bf16[2,16,256]{2,1,0:T(8,128)(2,1)S(1)} %get-tuple-element.57.refs_9_), channel_id=1, source_target_pairs={{0,12},{4,8},{8,4},{12,0},{1,13},{5,9},{9,5},{13,1},{2,14},{6,10},... | collective-permute-start | bytes 49160 | tf_op jit(solution)/shard_map/ppermute | solution.py:21
  7.8 5.6 %collective-permute-start.2 = (bf16[2,16,256]{2,1,0:T(8,128)(2,1)S(1)}, bf16[2,16,256]{2,1,0:T(8,128)(2,1)S(1)}, u32[]{:S(2)}, u32[]{:S(2)}) collective-permute-start(bf16[2,16,256]{2,1,0:T(8,128)(2,1)S(1)} %get-tuple-element.57.refs_9_), channel_id=1, source_target_pairs={{0,8},{4,12},{8,0},{12,4},{1,9},{5,13},{9,1},{13,5},{2,10},{6,14},... | collective-permute-start | bytes 49160 | tf_op jit(solution)/shard_map/ppermute | solution.py:21
  14.5 7.2 %collective-permute-start.4 = (bf16[416,256]{1,0:T(8,128)(2,1)S(1)}, bf16[416,256]{1,0:T(8,128)(2,1)S(1)}, u32[]{:S(2)}, u32[]{:S(2)}) collective-permute-start(bf16[416,256]{1,0:T(8,128)(2,1)S(1)} %get-tuple-element.71), channel_id=1, source_target_pairs={{0,4},{4,0},{8,12},{12,8},{1,5},{5,1},{9,13},{13,9},{2,6},{6,2},{1... | collective-permute-start | bytes 638984 | tf_op jit(solution)/shard_map/ppermute | solution.py:21
  15.4 6.2 %collective-permute-start.5 = (bf16[384,256]{1,0:T(8,128)(2,1)S(1)}, bf16[384,256]{1,0:T(8,128)(2,1)S(1)}, u32[]{:S(2)}, u32[]{:S(2)}) collective-permute-start(bf16[384,256]{1,0:T(8,128)(2,1)S(1)} %get-tuple-element.72), channel_id=1, source_target_pairs={{0,1},{1,0},{2,3},{3,2},{4,8},{5,9},{6,10},{7,11},{8,4},{9,5},{10,... | collective-permute-start | bytes 589832 | tf_op jit(solution)/shard_map/ppermute | solution.py:36
  15.4 7.1 %collective-permute-start.6 = (bf16[2,16,256]{2,1,0:T(8,128)(2,1)S(1)}, bf16[2,16,256]{2,1,0:T(8,128)(2,1)S(1)}, u32[]{:S(2)}, u32[]{:S(2)}) collective-permute-start(bf16[2,16,256]{2,1,0:T(8,128)(2,1)S(1)} %get-tuple-element.77), channel_id=1, source_target_pairs={{0,12},{4,8},{8,4},{12,0},{1,13},{5,9},{9,5},{13,1},{2,14},{6,10},... | collective-permute-start | bytes 49160 | tf_op jit(solution)/shard_map/ppermute | solution.py:21
  17.4 5.6 %collective-permute-start.7 = (bf16[2,16,256]{2,1,0:T(8,128)(2,1)S(1)}, bf16[2,16,256]{2,1,0:T(8,128)(2,1)S(1)}, u32[]{:S(2)}, u32[]{:S(2)}) collective-permute-start(bf16[2,16,256]{2,1,0:T(8,128)(2,1)S(1)} %get-tuple-element.78), channel_id=1, source_target_pairs={{0,8},{4,12},{8,0},{12,4},{1,9},{5,13},{9,1},{13,5},{2,10},{6,14},... | collective-permute-start | bytes 49160 | tf_op jit(solution)/shard_map/ppermute | solution.py:21

commit v9 on v7

--- a/solution.py
+++ b/solution.py
@@ -225,29 +225,31 @@
         low, high = columns_near(c, tile_cols)
         near = slice(low * PATCH, high * PATCH)
         p = exp_ref[c, near] * scale
-        px_ref[n, near] = p.astype(BF)
-        dsx_ref[n, near] = (p * (dw_ref[c, near].astype(F32) - row_dot)).astype(BF)
-        px_ref[n, edge:] = p_reg
-        dsx_ref[n, edge:] = ds_reg
-        for ref in (px_ref, dsx_ref):
-            if low > 0:
-                ref[n, : low * PATCH] = jnp.zeros((low * PATCH, feature), BF)
-            if high < tile_cols:
-                ref[n, high * PATCH : edge] = jnp.zeros(((tile_cols - high) * PATCH, feature), BF)
+        size = (high - low) * PATCH
+        whole = size + p_reg.shape[0]
+        px_ref[n, :size] = p.astype(BF)
+        dsx_ref[n, :size] = (p * (dw_ref[c, near].astype(F32) - row_dot)).astype(BF)
+        px_ref[n, size:whole] = p_reg
+        dsx_ref[n, size:whole] = ds_reg
     dk_reg = dv_reg = None
     for group in range(2):
-        dk_t = dv_t = None
+        parts_k, parts_v = [None] * tile_cols, [None] * tile_cols
         for c in range(tile_cols):
             n = group * tile_cols + c
-            dk = dot_nn(dsx_ref[n], qbd_ref[tiles[n]])
-            dv = dot_nn(px_ref[n], gbd_ref[tiles[n]])
-            dk_t = dk if dk_t is None else dk_t + dk
-            dv_t = dv if dv_t is None else dv_t + dv
+            low, high = columns_near(c, tile_cols)
+            size = (high - low) * PATCH
+            whole = size + kr_ref.shape[0]
+            dk = dot_nn(dsx_ref[n, :whole], qbd_ref[tiles[n]])
+            dv = dot_nn(px_ref[n, :whole], gbd_ref[tiles[n]])
+            for sums, value in ((parts_k, dk), (parts_v, dv)):
+                for x in range(low, high):
+                    part = value[(x - low) * PATCH : (x - low + 1) * PATCH]
+                    sums[x] = part if sums[x] is None else sums[x] + part
+            dk_reg = dk[size:] if dk_reg is None else dk_reg + dk[size:]
+            dv_reg = dv[size:] if dv_reg is None else dv_reg + dv[size:]
         back_ref = (back_b_ref, back_a_ref)[group]
-        back_ref[:edge] = dk_t[:edge].astype(BF)
-        back_ref[edge : 2 * edge] = dv_t[:edge].astype(BF)
-        dk_reg = dk_t[edge:] if dk_reg is None else dk_reg + dk_t[edge:]
-        dv_reg = dv_t[edge:] if dv_reg is None else dv_reg + dv_t[edge:]
+        back_ref[:edge] = jnp.concatenate(parts_k, axis=0).astype(BF)
+        back_ref[edge : 2 * edge] = jnp.concatenate(parts_v, axis=0).astype(BF)
     for n, reg in enumerate((dk_reg, dv_reg)):
         if split_regs:
             base = 2 * edge + n * cut
@@ -308,8 +310,17 @@
                         ref[x] = part
                     else:
                         ref[x] += part
-            o_t = dot_nn(vt_ref[:, near], weights) + dot_nn(vxt, px_ref[n])
-            dq_t = dot_nn(kt_ref[:, near], d_scores) + dot_nn(kxt, dsx_ref[n])
+            far = []
+            for ref in (px_ref, dsx_ref):
+                halo = (high - low) * PATCH
+                pieces = [ref[n, :halo], ref[n, halo : halo + kr_ref.shape[0]]]
+                if high < tile_cols:
+                    pieces.insert(1, jnp.zeros(((tile_cols - high) * PATCH, feature), BF))
+                if low > 0:
+                    pieces.insert(0, jnp.zeros((low * PATCH, feature), BF))
+                far.append(jnp.concatenate(pieces, axis=0))
+            o_t = dot_nn(vt_ref[:, near], weights) + dot_nn(vxt, far[0])
+            dq_t = dot_nn(kt_ref[:, near], d_scores) + dot_nn(kxt, far[1])
             o_cols.append(from_transposed(o_t, heads))
             dq_cols.append(from_transposed(dq_t, heads) * FACTOR)
         lines = pl.ds(pl.multiple_of(t * line, line), line)

time: 23.9 us -> 23.8 us (level)
  no operation moved by 1% of the time
where the time goes in v9:
time: 23.8 us; the launch traced here: 23.6 us
  starting transfers between devices  11 us (46%)
  Pallas kernels  9.38 us (39%)
  waiting for transfers between devices  2.48 us (10%)
  between operations  0.68 us (3%)
    ppermute x6, starting transfers between devices, swap(): return lax.ppermute(array, 'rows', pairs)  10.5 us
    pallas_call x8, Pallas kernels, call(): pl.pallas_call(kernel, out_shape=tuple(outs), in_specs=in_specs or [VMEM]...  9.38 us
    ppermute x6, waiting for transfers between devices, swap(): return lax.ppermute(array, 'rows', pairs)  2.48 us
    ppermute x2, starting transfers between devices, swap_b(): return lax.ppermute(array, ('rows', 'cols'), pairs)  0.52 us
  transfers between devices with their start and end apart: 8, of which 3 were waited for; matrix products, arithmetic and copies ran while one was open for 0% of the time, Pallas kernels for 28%

profile of v9, /device:TPU:0, one launch (start us, length us, event | category | flops | bytes accessed | tf_op | source)
XLA Modules:
  0.0 23.6 jit_solution(8199122043970713759)
XLA Ops:
  0.6 1.1 %prepare.1 = (bf16[416,256]{1,0:T(8,128)(2,1)S(1)}, bf16[384,256]{1,0:T(8,128)(2,1)S(1)}, bf16[2,16,256]{2,1,0:T(8,128)(2,1)S(1)}) custom-call(bf16[384,256]{1,0:T(8,128)(2,1)} %bitcast.8, bf16[384,256]{1,0:T(8,128)(2,1)} %bitcast.10, bf16[2,16,256]{2,1,0:T(8,128)(2,1)} %reg_ref.1), custom_call_target="tpu_custom_call" | custom-call | bytes 835584 | tf_op jit(solution)/shard_map/prepare/pallas_call | solution.py:370
  1.8 0.5 %collective-permute-start = (bf16[384,256]{1,0:T(8,128)(2,1)S(1)}, bf16[384,256]{1,0:T(8,128)(2,1)S(1)}, u32[]{:S(2)}, u32[]{:S(2)}) collective-permute-start(bf16[384,256]{1,0:T(8,128)(2,1)S(1)} %get-tuple-element.49), channel_id=1, source_target_pairs={{0,1},{1,0},{2,3},{3,2},{4,8},{5,9},{6,10},{7,11},{8,4},{9,5},{10,... | collective-permute-start | bytes 589832 | tf_op jit(solution)/shard_map/ppermute | solution.py:36
  2.3 4.1 %collective-permute-start.1 = (bf16[416,256]{1,0:T(8,128)(2,1)S(1)}, bf16[416,256]{1,0:T(8,128)(2,1)S(1)}, u32[]{:S(2)}, u32[]{:S(2)}) collective-permute-start(bf16[416,256]{1,0:T(8,128)(2,1)S(1)} %get-tuple-element.53), channel_id=1, source_target_pairs={{0,4},{4,0},{8,12},{12,8},{1,5},{5,1},{9,13},{13,9},{2,6},{6,2},{1... | collective-permute-start | bytes 638984 | tf_op jit(solution)/shard_map/ppermute | solution.py:21
  6.4 1.3 %collective-permute-start.3 = (bf16[2,16,256]{2,1,0:T(8,128)(2,1)S(1)}, bf16[2,16,256]{2,1,0:T(8,128)(2,1)S(1)}, u32[]{:S(2)}, u32[]{:S(2)}) collective-permute-start(bf16[2,16,256]{2,1,0:T(8,128)(2,1)S(1)} %get-tuple-element.57.refs_9_), channel_id=1, source_target_pairs={{0,12},{4,8},{8,4},{12,0},{1,13},{5,9},{9,5},{13,1},{2,14},{6,10},... | collective-permute-start | bytes 49160 | tf_op jit(solution)/shard_map/ppermute | solution.py:21
  7.8 0.1 collective-permute-start.2
  7.9 2.3 %own.1 = (bf16[6,256,256]{2,1,0:T(8,128)(2,1)S(1)}, bf16[6,256,256]{2,1,0:T(8,128)(2,1)S(1)}, bf16[256,384]{1,0:T(8,128)(2,1)S(1)}, bf16[256,384]{1,0:T(8,128)(2...) custom-call(bf16[384,256]{1,0:T(8,128)(2,1)} %bitcast.12, ...), custom_call_target="tpu_custom_call" | custom-call | flops 600000000 | bytes 6340608 | tf_op jit(solution)/shard_map/own/pallas_call | solution.py:370
  10.2 0.0 collective-permute-done.halo_ref
  10.3 0.5 %halo.2 = (f32[3,192,256]{2,1,0:T(8,128)S(1)}, bf16[3,192,256]{2,1,0:T(8,128)(2,1)S(1)}, f32[3,8,256]{2,1,0:T(8,128)S(1)}, bf16[192,256]{1,0:T(8,128)(2,1)S(1)}, bf16[192,256]{1,0:T(8,128)(2,1)S(1)}) custom-call(bf16[6,256,256]{2,1,0:T(8,128)(2,1)S(1)} %get-tuple-element.42.qbd_ref.refs_0_, bf16[6,256,256]{2,1,0:T(8,128)(2,1)S(1)} %get-tuple-element.43.gbd_ref.refs_1_, ...), custom_call_target="tpu_custom_call" | custom-call | flops 1207959552 | bytes 2924544 | tf_op jit(solution)/shard_map/halo/pallas_call | solution.py:370
  10.7 0.8 %collective-permute-done.1.halo_ref.refs_8_ = bf16[416,256]{1,0:T(8,128)(2,1)S(1)} collective-permute-done((bf16[416,256]{1,0:T(8,128)(2,1)S(1)}, bf16[416,256]{1,0:T(8,128)(2,1)S(1)}, u32[]{:S(2)}, u32[]{:S(2)}) %collective-permute-start.1) | collective-permute-done | bytes 213024 | tf_op jit(solution)/shard_map/ppermute | solution.py:21
  11.6 0.5 %halo.3 = (f32[3,192,256]{2,1,0:T(8,128)S(1)}, bf16[3,192,256]{2,1,0:T(8,128)(2,1)S(1)}, f32[3,8,256]{2,1,0:T(8,128)S(1)}, bf16[192,256]{1,0:T(8,128)(2,1)S(1)}, bf16[192,256]{1,0:T(8,128)(2,1)S(1)}) custom-call(bf16[6,256,256]{2,1,0:T(8,128)(2,1)S(1)} %get-tuple-element.42.qbd_ref.refs_0_, bf16[6,256,256]{2,1,0:T(8,128)(2,1)S(1)} %get-tuple-element.43.gbd_ref.refs_1_, ...), custom_call_target="tpu_custom_call" | custom-call | flops 1207959552 | bytes 2940928 | tf_op jit(solution)/shard_map/halo/pallas_call | solution.py:370
  12.0 1.3 %collective-permute-done.3.refs_11_ = bf16[2,16,256]{2,1,0:T(8,128)(2,1)S(1)} collective-permute-done((bf16[2,16,256]{2,1,0:T(8,128)(2,1)S(1)}, bf16[2,16,256]{2,1,0:T(8,128)(2,1)S(1)}, u32[]{:S(2)}, u32[]{:S(2)}) %collective-permute-start.3) | collective-permute-done | bytes 16416 | tf_op jit(solution)/shard_map/ppermute | solution.py:21
  13.3 0.0 collective-permute-done.2.refs_10_
  13.3 1.1 %far.1 = (f32[6,8,256]{2,1,0:T(8,128)S(1)}, bf16[6,256,256]{2,1,0:T(8,128)(2,1)S(1)}, bf16[6,256,256]{2,1,0:T(8,128)(2,1)S(1)}, bf16[64,256]{1,0:T(8,128)(2,1)S(...) custom-call(bf16[6,256,256]{2,1,0:T(8,128)(2,1)S(1)} %get-tuple-elem, ...), custom_call_target="tpu_custom_call" | custom-call | flops 805306368 | bytes 5816320 | tf_op jit(solution)/shard_map/far/pallas_call | solution.py:370
  14.4 0.9 %collective-permute-start.4 = (bf16[416,256]{1,0:T(8,128)(2,1)S(1)}, bf16[416,256]{1,0:T(8,128)(2,1)S(1)}, u32[]{:S(2)}, u32[]{:S(2)}) collective-permute-start(bf16[416,256]{1,0:T(8,128)(2,1)S(1)} %get-tuple-element.71), channel_id=1, source_target_pairs={{0,4},{4,0},{8,12},{12,8},{1,5},{5,1},{9,13},{13,9},{2,6},{6,2},{1... | collective-permute-start | bytes 638984 | tf_op jit(solution)/shard_map/ppermute | solution.py:21
  15.3 0.0 collective-permute-start.5
  15.3 2.0 %collective-permute-start.6 = (bf16[2,16,256]{2,1,0:T(8,128)(2,1)S(1)}, bf16[2,16,256]{2,1,0:T(8,128)(2,1)S(1)}, u32[]{:S(2)}, u32[]{:S(2)}) collective-permute-start(bf16[2,16,256]{2,1,0:T(8,128)(2,1)S(1)} %get-tuple-element.77), channel_id=1, source_target_pairs={{0,12},{4,8},{8,4},{12,0},{1,13},{5,9},{9,5},{13,1},{2,14},{6,10},... | collective-permute-start | bytes 49160 | tf_op jit(solution)/shard_map/ppermute | solution.py:21
  17.3 2.0 %collective-permute-start.7 = (bf16[2,16,256]{2,1,0:T(8,128)(2,1)S(1)}, bf16[2,16,256]{2,1,0:T(8,128)(2,1)S(1)}, u32[]{:S(2)}, u32[]{:S(2)}) collective-permute-start(bf16[2,16,256]{2,1,0:T(8,128)(2,1)S(1)} %get-tuple-element.78), channel_id=1, source_target_pairs={{0,8},{4,12},{8,0},{12,4},{1,9},{5,13},{9,1},{13,5},{2,10},{6,14},... | collective-permute-start | bytes 49160 | tf_op jit(solution)/shard_map/ppermute | solution.py:21
  19.3 2.5 %rest.1 = (bf16[384,256]{1,0:T(8,128)(2,1)}, bf16[384,256]{1,0:T(8,128)(2,1)}, f32[3,128,256]{2,1,0:T(8,128)S(1)}, f32[3,128,256]{2,1,0:T(8,128)S(1)}) custom-call(bf16[6,256,256]{2,1,0:T(8,128)(2,1)S(1)} %get-tuple-element.42.qbd_ref.refs_0_, bf16[6,256,256]{2,1,0:T(8,128)(2,1)S(1)} %get-tuple-element.43.gbd_ref.refs_1_, ...), custom_call_target="tpu_custom_call" | custom-call | flops 600000000 | bytes 8765440 | tf_op jit(solution)/shard_map/rest/pallas_call | solution.py:370
  21.8 0.0 collective-permute-done.5.b_ref
  21.8 0.0 collective-permute-done.4.a_ref
  21.8 0.8 %finish.1 = (bf16[384,256]{1,0:T(8,128)(2,1)}, bf16[384,256]{1,0:T(8,128)(2,1)}, f32[2,16,256]{2,1,0:T(8,128)S(1)}) custom-call(f32[3,128,256]{2,1,0:T(8,128)S(1)} %get-tuple-element.69.dk_ref, f32[3,128,256]{2,1,0:T(8,128)S(1)} %get-tuple-element.70.dv_ref, bf16[416,256]{1,0:T(8,128)(2,1)S(1)} %collective-permute-done.4.a_ref, ...), custom_call_target="tpu_custom_call" | custom-call | bytes 1654784 | tf_op jit(solution)/shard_map/finish/pallas_call | solution.py:370
  22.6 0.0 collective-permute-done.6.three_ref
  22.6 0.4 %collective-permute-done.7.two_ref = bf16[2,16,256]{2,1,0:T(8,128)(2,1)S(1)} collective-permute-done((bf16[2,16,256]{2,1,0:T(8,128)(2,1)S(1)}, bf16[2,16,256]{2,1,0:T(8,128)(2,1)S(1)}, u32[]{:S(2)}, u32[]{:S(2)}) %collective-permute-start.7) | collective-permute-done | bytes 16416 | tf_op jit(solution)/shard_map/ppermute | solution.py:21
  23.0 0.6 %registers.1 = f32[2,16,256]{2,1,0:T(8,128)} custom-call(f32[2,16,256]{2,1,0:T(8,128)S(1)} %get-tuple-element.76.part_ref, bf16[2,16,256]{2,1,0:T(8,128)(2,1)S(1)} %collective-permute-done.6.three_ref, bf16[2,16,256]{2,1,0:T(8,128)(2,1)S(1)} %collective-permute-done.7.two_ref), custom_call_target="tpu_custom_call" | custom-call | bytes 98304 | tf_op jit(solution)/shard_map/registers/pallas_call | solution.py:370
Async XLA Ops:
  1.8 8.5 %collective-permute-start = (bf16[384,256]{1,0:T(8,128)(2,1)S(1)}, bf16[384,256]{1,0:T(8,128)(2,1)S(1)}, u32[]{:S(2)}, u32[]{:S(2)}) collective-permute-start(bf16[384,256]{1,0:T(8,128)(2,1)S(1)} %get-tuple-element.49), channel_id=1, source_target_pairs={{0,1},{1,0},{2,3},{3,2},{4,8},{5,9},{6,10},{7,11},{8,4},{9,5},{10,... | collective-permute-start | bytes 589832 | tf_op jit(solution)/shard_map/ppermute | solution.py:36
  2.3 9.3 %collective-permute-start.1 = (bf16[416,256]{1,0:T(8,128)(2,1)S(1)}, bf16[416,256]{1,0:T(8,128)(2,1)S(1)}, u32[]{:S(2)}, u32[]{:S(2)}) collective-permute-start(bf16[416,256]{1,0:T(8,128)(2,1)S(1)} %get-tuple-element.53), channel_id=1, source_target_pairs={{0,4},{4,0},{8,12},{12,8},{1,5},{5,1},{9,13},{13,9},{2,6},{6,2},{1... | collective-permute-start | bytes 638984 | tf_op jit(solution)/shard_map/ppermute | solution.py:21
  6.4 6.9 %collective-permute-start.3 = (bf16[2,16,256]{2,1,0:T(8,128)(2,1)S(1)}, bf16[2,16,256]{2,1,0:T(8,128)(2,1)S(1)}, u32[]{:S(2)}, u32[]{:S(2)}) collective-permute-start(bf16[2,16,256]{2,1,0:T(8,128)(2,1)S(1)} %get-tuple-element.57.refs_9_), channel_id=1, source_target_pairs={{0,12},{4,8},{8,4},{12,0},{1,13},{5,9},{9,5},{13,1},{2,14},{6,10},... | collective-permute-start | bytes 49160 | tf_op jit(solution)/shard_map/ppermute | solution.py:21
  7.8 5.6 %collective-permute-start.2 = (bf16[2,16,256]{2,1,0:T(8,128)(2,1)S(1)}, bf16[2,16,256]{2,1,0:T(8,128)(2,1)S(1)}, u32[]{:S(2)}, u32[]{:S(2)}) collective-permute-start(bf16[2,16,256]{2,1,0:T(8,128)(2,1)S(1)} %get-tuple-element.57.refs_9_), channel_id=1, source_target_pairs={{0,8},{4,12},{8,0},{12,4},{1,9},{5,13},{9,1},{13,5},{2,10},{6,14},... | collective-permute-start | bytes 49160 | tf_op jit(solution)/shard_map/ppermute | solution.py:21
  14.4 7.4 %collective-permute-start.4 = (bf16[416,256]{1,0:T(8,128)(2,1)S(1)}, bf16[416,256]{1,0:T(8,128)(2,1)S(1)}, u32[]{:S(2)}, u32[]{:S(2)}) collective-permute-start(bf16[416,256]{1,0:T(8,128)(2,1)S(1)} %get-tuple-element.71), channel_id=1, source_target_pairs={{0,4},{4,0},{8,12},{12,8},{1,5},{5,1},{9,13},{13,9},{2,6},{6,2},{1... | collective-permute-start | bytes 638984 | tf_op jit(solution)/shard_map/ppermute | solution.py:21
  15.3 6.4 %collective-permute-start.5 = (bf16[384,256]{1,0:T(8,128)(2,1)S(1)}, bf16[384,256]{1,0:T(8,128)(2,1)S(1)}, u32[]{:S(2)}, u32[]{:S(2)}) collective-permute-start(bf16[384,256]{1,0:T(8,128)(2,1)S(1)} %get-tuple-element.72), channel_id=1, source_target_pairs={{0,1},{1,0},{2,3},{3,2},{4,8},{5,9},{6,10},{7,11},{8,4},{9,5},{10,... | collective-permute-start | bytes 589832 | tf_op jit(solution)/shard_map/ppermute | solution.py:36
  15.3 7.3 %collective-permute-start.6 = (bf16[2,16,256]{2,1,0:T(8,128)(2,1)S(1)}, bf16[2,16,256]{2,1,0:T(8,128)(2,1)S(1)}, u32[]{:S(2)}, u32[]{:S(2)}) collective-permute-start(bf16[2,16,256]{2,1,0:T(8,128)(2,1)S(1)} %get-tuple-element.77), channel_id=1, source_target_pairs={{0,12},{4,8},{8,4},{12,0},{1,13},{5,9},{9,5},{13,1},{2,14},{6,10},... | collective-permute-start | bytes 49160 | tf_op jit(solution)/shard_map/ppermute | solution.py:21
  17.3 5.6 %collective-permute-start.7 = (bf16[2,16,256]{2,1,0:T(8,128)(2,1)S(1)}, bf16[2,16,256]{2,1,0:T(8,128)(2,1)S(1)}, u32[]{:S(2)}, u32[]{:S(2)}) collective-permute-start(bf16[2,16,256]{2,1,0:T(8,128)(2,1)S(1)} %get-tuple-element.78), channel_id=1, source_target_pairs={{0,8},{4,12},{8,0},{12,4},{1,9},{5,13},{9,1},{13,5},{2,10},{6,14},... | collective-permute-start | bytes 49160 | tf_op jit(solution)/shard_map/ppermute | solution.py:21

commit v10 on v7

--- a/solution.py
+++ b/solution.py
@@ -45,6 +45,26 @@
 def patch_order(columns):
     feature = columns[0].shape[1]
     parts = [x.reshape(-1, 1, TILE, feature) for x in columns]
+    return jnp.concatenate(parts, axis=1).reshape(-1, feature)
+
+
+def pick(block, low, high, tile_cols):
+    if high - low == tile_cols:
+        return block
+    feature = block.shape[1]
+    return block.reshape(-1, tile_cols, TILE, feature)[:, low:high].reshape(-1, feature)
+
+
+def spread(block, low, high, tile_cols):
+    if high - low == tile_cols:
+        return block
+    feature = block.shape[1]
+    parts = [block.reshape(-1, high - low, TILE, feature)]
+    count = parts[0].shape[0]
+    if low > 0:
+        parts.insert(0, jnp.zeros((count, low, TILE, feature), block.dtype))
+    if high < tile_cols:
+        parts.append(jnp.zeros((count, tile_cols - high, TILE, feature), block.dtype))
     return jnp.concatenate(parts, axis=1).reshape(-1, feature)
 
 
@@ -154,29 +174,30 @@
     return odd if group == 0 else 1 - odd
 
 
-def halo_kernel(tile_cols, group, qbd_ref, gbd_ref, stat_ref, halo_ref, exp_ref, dw_ref, sum_ref, kx_ref, vx_ref):
+def halo_kernel(tile_cols, group, qbd_ref, gbd_ref, stat_ref, halo_ref, exp_ref, dw_ref, sum_ref):
     edge = tile_cols * PATCH
     me = lax.axis_index("rows")
     inner = (me > 0) & (me < lax.axis_size("rows") - 1)
-    for n, ref in enumerate((kx_ref, vx_ref)):
-        ref[...] = jnp.concatenate(column_tiles(halo_ref[n * edge : (n + 1) * edge], tile_cols), axis=0).astype(BF)
+    tiles = [tile_row_of(group) * tile_cols + c for c in range(tile_cols)]
+    scores = [dot_nt(halo_ref[:edge], qbd_ref[tile]) for tile in tiles]
+    grads = [dot_nt(halo_ref[edge : 2 * edge], gbd_ref[tile]) for tile in tiles]
+    olds = [[stat_ref[tile, n : n + 1] for n in range(3)] for tile in tiles]
     for c in range(tile_cols):
-        tile = tile_row_of(group) * tile_cols + c
         low, high = columns_near(c, tile_cols)
-        near = slice(low * PATCH, high * PATCH)
-        s = dot_nt(kx_ref[near], qbd_ref[tile])
+        size = (high - low) * PATCH
+        s = pick(scores[c], low, high, tile_cols)
         if group == 0:
             s = jnp.where(inner, s, -1e30)
-        d = dot_nt(vx_ref[near], gbd_ref[tile]).astype(BF)
-        own_top = stat_ref[tile, 0:1]
+        d = pick(grads[c], low, high, tile_cols).astype(BF)
+        own_top, own_sum, own_dot = olds[c]
         top = jnp.maximum(own_top, jnp.max(s, axis=0, keepdims=True))
         e = jnp.exp(s - top)
         ratio = jnp.exp(own_top - top)
-        exp_ref[c, near] = e
-        dw_ref[c, near] = d
+        exp_ref[c, :size] = e
+        dw_ref[c, :size] = d
         sum_ref[c, 0:1] = top
-        sum_ref[c, 1:2] = stat_ref[tile, 1:2] * ratio + jnp.sum(e, axis=0, keepdims=True)
-        sum_ref[c, 2:3] = stat_ref[tile, 2:3] * ratio + jnp.sum(e * d.astype(F32), axis=0, keepdims=True)
+        sum_ref[c, 1:2] = own_sum * ratio + jnp.sum(e, axis=0, keepdims=True)
+        sum_ref[c, 2:3] = own_dot * ratio + jnp.sum(e * d.astype(F32), axis=0, keepdims=True)
         sum_ref[c, 3:4] = ratio
 
 
@@ -223,17 +244,13 @@
         exp_ref, dw_ref, _ = halos[group]
         scale, row_dot, p_reg, ds_reg = parts[n]
         low, high = columns_near(c, tile_cols)
-        near = slice(low * PATCH, high * PATCH)
-        p = exp_ref[c, near] * scale
-        px_ref[n, near] = p.astype(BF)
-        dsx_ref[n, near] = (p * (dw_ref[c, near].astype(F32) - row_dot)).astype(BF)
+        size = (high - low) * PATCH
+        p = exp_ref[c, :size] * scale
+        ds = p * (dw_ref[c, :size].astype(F32) - row_dot)
+        px_ref[n, :edge] = spread(p, low, high, tile_cols).astype(BF)
+        dsx_ref[n, :edge] = spread(ds, low, high, tile_cols).astype(BF)
         px_ref[n, edge:] = p_reg
         dsx_ref[n, edge:] = ds_reg
-        for ref in (px_ref, dsx_ref):
-            if low > 0:
-                ref[n, : low * PATCH] = jnp.zeros((low * PATCH, feature), BF)
-            if high < tile_cols:
-                ref[n, high * PATCH : edge] = jnp.zeros(((tile_cols - high) * PATCH, feature), BF)
     dk_reg = dv_reg = None
     for group in range(2):
         dk_t = dv_t = None
@@ -270,10 +287,8 @@
     final_ref,
     px_ref,
     dsx_ref,
-    kb_ref,
-    vb_ref,
-    ka_ref,
-    va_ref,
+    from_b_ref,
+    from_a_ref,
     kr_ref,
     vr_ref,
     *refs,
@@ -284,10 +299,11 @@
     line = tile_cols * PATCH
     tile_rows = qbd_ref.shape[0] // tile_cols
     rows = tile_rows * PATCH
-    for group, (kx_ref, vx_ref) in enumerate(((kb_ref, vb_ref), (ka_ref, va_ref))):
+    edge = tile_cols * PATCH
+    for group, halo_ref in enumerate((from_b_ref, from_a_ref)):
         t = tile_row_of(group)
-        kxt = jnp.concatenate([kx_ref[...], kr_ref[...]], axis=0).T
-        vxt = jnp.concatenate([vx_ref[...], vr_ref[...]], axis=0).T
+        kxt = jnp.concatenate([halo_ref[:edge], kr_ref[...]], axis=0).T
+        vxt = jnp.concatenate([halo_ref[edge : 2 * edge], vr_ref[...]], axis=0).T
         o_cols, dq_cols = [], []
         for c in range(tile_cols):
             tile = t * tile_cols + c
@@ -341,13 +357,9 @@
         from_b = b_ref[n * edge : (n + 1) * edge]
         top = jnp.where(has_top, jnp.where(even, from_b, from_a).astype(F32), 0.0)
         bottom = jnp.where(has_bottom, jnp.where(even, from_a, from_b).astype(F32), 0.0)
-        rows = acc_ref.shape[1]
-        columns = []
-        for c in range(tile_cols):
-            high = acc_ref[c, :PATCH] + top[c * PATCH : (c + 1) * PATCH]
-            low = acc_ref[c, rows - PATCH :] + bottom[c * PATCH : (c + 1) * PATCH]
-            columns.append(jnp.concatenate([high, low], axis=0))
-        out_ref[...] = patch_order(columns).astype(BF)
+        total = patch_order([acc_ref[c] for c in range(tile_cols)])
+        out_ref[:edge] = (total[:edge] + top).astype(BF)
+        out_ref[edge:] = (total[edge:] + bottom).astype(BF)
 
 
 def shape(dims, dtype):
@@ -448,8 +460,6 @@
                     shape((tile_cols, edge, feature), F32),
                     shape((tile_cols, edge, feature), BF),
                     shape((tile_cols, 8, feature), F32),
-                    shape((edge, feature), BF),
-                    shape((edge, feature), BF),
                 ),
                 32 * tile_cols * edge * feature * feature,
             )
@@ -457,7 +467,7 @@
     final, px, dsx, kr, vr, back_a, back_b, *back_regs = call(
         functools.partial(far_kernel, tile_cols, split_regs),
         "far",
-        (qbd, gbd) + tuple(halos[0][:3]) + tuple(halos[1][:3]) + (got_a,) + regs,
+        (qbd, gbd) + tuple(halos[0]) + tuple(halos[1]) + (got_a,) + regs,
         (
             shape((tiles, 8, feature), F32),
             shape((tiles, window, feature), BF),
@@ -475,7 +485,7 @@
     attended, grad_query, dk, dv = call(
         functools.partial(rest_kernel, tile_cols),
         "rest",
-        (qbd, gbd, kt, vt, exps, dw, final, px, dsx) + tuple(halos[0][3:]) + tuple(halos[1][3:]) + (kr, vr),
+        (qbd, gbd, kt, vt, exps, dw, final, px, dsx, got_b, got_a, kr, vr),
         (
             shape((total, feature), BF),
             shape((total, feature), BF),

time: 23.9 us -> 23.8 us (level)
  no operation moved by 1% of the time
where the time goes in v10:
time: 23.8 us; the launch traced here: 23.6 us
  starting transfers between devices  11 us (46%)
  Pallas kernels  9.42 us (40%)
  waiting for transfers between devices  2.52 us (11%)
  between operations  0.68 us (3%)
    ppermute x6, starting transfers between devices, swap(): return lax.ppermute(array, 'rows', pairs)  10.5 us
    pallas_call x8, Pallas kernels, call(): pl.pallas_call(kernel, out_shape=tuple(outs), in_specs=in_specs or [VMEM]...  9.42 us
    ppermute x6, waiting for transfers between devices, swap(): return lax.ppermute(array, 'rows', pairs)  2.51 us
    ppermute x2, starting transfers between devices, swap_b(): return lax.ppermute(array, ('rows', 'cols'), pairs)  0.52 us
  transfers between devices with their start and end apart: 8, of which 3 were waited for; matrix products, arithmetic and copies ran while one was open for 0% of the time, Pallas kernels for 28%

profile of v10, /device:TPU:0, one launch (start us, length us, event | category | flops | bytes accessed | tf_op | source)
XLA Modules:
  0.0 23.6 jit_solution(1523042664840879854)
XLA Ops:
  0.6 1.1 %prepare.1 = (bf16[416,256]{1,0:T(8,128)(2,1)S(1)}, bf16[384,256]{1,0:T(8,128)(2,1)S(1)}, bf16[2,16,256]{2,1,0:T(8,128)(2,1)S(1)}) custom-call(bf16[384,256]{1,0:T(8,128)(2,1)} %bitcast.8, bf16[384,256]{1,0:T(8,128)(2,1)} %bitcast.10, bf16[2,16,256]{2,1,0:T(8,128)(2,1)} %reg_ref.1), custom_call_target="tpu_custom_call" | custom-call | bytes 835584 | tf_op jit(solution)/shard_map/prepare/pallas_call | solution.py:371
  1.8 0.5 %collective-permute-start = (bf16[384,256]{1,0:T(8,128)(2,1)S(1)}, bf16[384,256]{1,0:T(8,128)(2,1)S(1)}, u32[]{:S(2)}, u32[]{:S(2)}) collective-permute-start(bf16[384,256]{1,0:T(8,128)(2,1)S(1)} %get-tuple-element.45), channel_id=1, source_target_pairs={{0,1},{1,0},{2,3},{3,2},{4,8},{5,9},{6,10},{7,11},{8,4},{9,5},{10,... | collective-permute-start | bytes 589832 | tf_op jit(solution)/shard_map/ppermute | solution.py:36
  2.3 4.1 %collective-permute-start.1 = (bf16[416,256]{1,0:T(8,128)(2,1)S(1)}, bf16[416,256]{1,0:T(8,128)(2,1)S(1)}, u32[]{:S(2)}, u32[]{:S(2)}) collective-permute-start(bf16[416,256]{1,0:T(8,128)(2,1)S(1)} %get-tuple-element.49), channel_id=1, source_target_pairs={{0,4},{4,0},{8,12},{12,8},{1,5},{5,1},{9,13},{13,9},{2,6},{6,2},{1... | collective-permute-start | bytes 638984 | tf_op jit(solution)/shard_map/ppermute | solution.py:21
  6.4 1.3 %collective-permute-start.3 = (bf16[2,16,256]{2,1,0:T(8,128)(2,1)S(1)}, bf16[2,16,256]{2,1,0:T(8,128)(2,1)S(1)}, u32[]{:S(2)}, u32[]{:S(2)}) collective-permute-start(bf16[2,16,256]{2,1,0:T(8,128)(2,1)S(1)} %get-tuple-element.53.refs_9_), channel_id=1, source_target_pairs={{0,12},{4,8},{8,4},{12,0},{1,13},{5,9},{9,5},{13,1},{2,14},{6,10},... | collective-permute-start | bytes 49160 | tf_op jit(solution)/shard_map/ppermute | solution.py:21
  7.8 0.1 collective-permute-start.2
  7.9 2.3 %own.1 = (bf16[6,256,256]{2,1,0:T(8,128)(2,1)S(1)}, bf16[6,256,256]{2,1,0:T(8,128)(2,1)S(1)}, bf16[256,384]{1,0:T(8,128)(2,1)S(1)}, bf16[256,384]{1,0:T(8,128)(2...) custom-call(bf16[384,256]{1,0:T(8,128)(2,1)} %bitcast.12, ...), custom_call_target="tpu_custom_call" | custom-call | flops 600000000 | bytes 6340608 | tf_op jit(solution)/shard_map/own/pallas_call | solution.py:371
  10.2 0.0 collective-permute-done.halo_ref.from_b_ref
  10.3 0.5 %halo.2 = (f32[3,192,256]{2,1,0:T(8,128)S(1)}, bf16[3,192,256]{2,1,0:T(8,128)(2,1)S(1)}, f32[3,8,256]{2,1,0:T(8,128)S(1)}) custom-call(bf16[6,256,256]{2,1,0:T(8,128)(2,1)S(1)} %get-tuple-element.38.qbd_ref.refs_0_, bf16[6,256,256]{2,1,0:T(8,128)(2,1)S(1)} %get-tuple-element.39.gbd_ref.refs_1_, f32[6,8,256]{2,1,0:T(8,128)S(1)} %get-tuple-element.44.stat_ref, ...), custom_call_target="tpu_custom_call" | custom-call | flops 1207959552 | bytes 2727936 | tf_op jit(solution)/shard_map/halo/pallas_call | solution.py:371
  10.7 0.8 %collective-permute-done.1.halo_ref.refs_8_.from_a_ref = bf16[416,256]{1,0:T(8,128)(2,1)S(1)} collective-permute-done((bf16[416,256]{1,0:T(8,128)(2,1)S(1)}, bf16[416,256]{1,0:T(8,128)(2,1)S(1)}, u32[]{:S(2)}, u32[]{:S(2)}) %collective-permute-start.1) | collective-permute-done | bytes 213024 | tf_op jit(solution)/shard_map/ppermute | solution.py:21
  11.6 0.4 %halo.3 = (f32[3,192,256]{2,1,0:T(8,128)S(1)}, bf16[3,192,256]{2,1,0:T(8,128)(2,1)S(1)}, f32[3,8,256]{2,1,0:T(8,128)S(1)}) custom-call(bf16[6,256,256]{2,1,0:T(8,128)(2,1)S(1)} %get-tuple-element.38.qbd_ref.refs_0_, bf16[6,256,256]{2,1,0:T(8,128)(2,1)S(1)} %get-tuple-element.39.gbd_ref.refs_1_, f32[6,8,256]{2,1,0:T(8,128)S(1)} %get-tuple-element.44.stat_ref, ...), custom_call_target="tpu_custom_call" | custom-call | flops 1207959552 | bytes 2744320 | tf_op jit(solution)/shard_map/halo/pallas_call | solution.py:371
  12.0 1.3 %collective-permute-done.3.refs_11_ = bf16[2,16,256]{2,1,0:T(8,128)(2,1)S(1)} collective-permute-done((bf16[2,16,256]{2,1,0:T(8,128)(2,1)S(1)}, bf16[2,16,256]{2,1,0:T(8,128)(2,1)S(1)}, u32[]{:S(2)}, u32[]{:S(2)}) %collective-permute-start.3) | collective-permute-done | bytes 16416 | tf_op jit(solution)/shard_map/ppermute | solution.py:21
  13.3 0.0 collective-permute-done.2.refs_10_
  13.3 1.1 %far.1 = (f32[6,8,256]{2,1,0:T(8,128)S(1)}, bf16[6,256,256]{2,1,0:T(8,128)(2,1)S(1)}, bf16[6,256,256]{2,1,0:T(8,128)(2,1)S(1)}, bf16[64,256]{1,0:T(8,128)(2,1)S(...) custom-call(bf16[6,256,256]{2,1,0:T(8,128)(2,1)S(1)} %get-tuple-elem, ...), custom_call_target="tpu_custom_call" | custom-call | flops 805306368 | bytes 5816320 | tf_op jit(solution)/shard_map/far/pallas_call | solution.py:371
  14.5 0.9 %collective-permute-start.4 = (bf16[416,256]{1,0:T(8,128)(2,1)S(1)}, bf16[416,256]{1,0:T(8,128)(2,1)S(1)}, u32[]{:S(2)}, u32[]{:S(2)}) collective-permute-start(bf16[416,256]{1,0:T(8,128)(2,1)S(1)} %get-tuple-element.63), channel_id=1, source_target_pairs={{0,4},{4,0},{8,12},{12,8},{1,5},{5,1},{9,13},{13,9},{2,6},{6,2},{1... | collective-permute-start | bytes 638984 | tf_op jit(solution)/shard_map/ppermute | solution.py:21
  15.4 0.0 collective-permute-start.5
  15.4 2.0 %collective-permute-start.6 = (bf16[2,16,256]{2,1,0:T(8,128)(2,1)S(1)}, bf16[2,16,256]{2,1,0:T(8,128)(2,1)S(1)}, u32[]{:S(2)}, u32[]{:S(2)}) collective-permute-start(bf16[2,16,256]{2,1,0:T(8,128)(2,1)S(1)} %get-tuple-element.69), channel_id=1, source_target_pairs={{0,12},{4,8},{8,4},{12,0},{1,13},{5,9},{9,5},{13,1},{2,14},{6,10},... | collective-permute-start | bytes 49160 | tf_op jit(solution)/shard_map/ppermute | solution.py:21
  17.4 1.9 %collective-permute-start.7 = (bf16[2,16,256]{2,1,0:T(8,128)(2,1)S(1)}, bf16[2,16,256]{2,1,0:T(8,128)(2,1)S(1)}, u32[]{:S(2)}, u32[]{:S(2)}) collective-permute-start(bf16[2,16,256]{2,1,0:T(8,128)(2,1)S(1)} %get-tuple-element.70), channel_id=1, source_target_pairs={{0,8},{4,12},{8,0},{12,4},{1,9},{5,13},{9,1},{13,5},{2,10},{6,14},... | collective-permute-start | bytes 49160 | tf_op jit(solution)/shard_map/ppermute | solution.py:21
  19.4 2.5 %rest.1 = (bf16[384,256]{1,0:T(8,128)(2,1)}, bf16[384,256]{1,0:T(8,128)(2,1)}, f32[3,128,256]{2,1,0:T(8,128)S(1)}, f32[3,128,256]{2,1,0:T(8,128)S(1)}) custom-call(bf16[6,256,256]{2,1,0:T(8,128)(2,1)S(1)} %get-tuple-element.38.qbd_ref.refs_0_, bf16[6,256,256]{2,1,0:T(8,128)(2,1)S(1)} %get-tuple-element.39.gbd_ref.refs_1_, ...), custom_call_target="tpu_custom_call" | custom-call | flops 600000000 | bytes 8781824 | tf_op jit(solution)/shard_map/rest/pallas_call | solution.py:371
  21.9 0.0 collective-permute-done.5.b_ref
  21.9 0.0 collective-permute-done.4.a_ref
  21.9 0.8 %finish.1 = (bf16[384,256]{1,0:T(8,128)(2,1)}, bf16[384,256]{1,0:T(8,128)(2,1)}, f32[2,16,256]{2,1,0:T(8,128)S(1)}) custom-call(f32[3,128,256]{2,1,0:T(8,128)S(1)} %get-tuple-element.61.dk_ref, f32[3,128,256]{2,1,0:T(8,128)S(1)} %get-tuple-element.62.dv_ref, bf16[416,256]{1,0:T(8,128)(2,1)S(1)} %collective-permute-done.4.a_ref, ...), custom_call_target="tpu_custom_call" | custom-call | bytes 1654784 | tf_op jit(solution)/shard_map/finish/pallas_call | solution.py:371
  22.7 0.0 collective-permute-done.6.three_ref
  22.7 0.3 %collective-permute-done.7.two_ref = bf16[2,16,256]{2,1,0:T(8,128)(2,1)S(1)} collective-permute-done((bf16[2,16,256]{2,1,0:T(8,128)(2,1)S(1)}, bf16[2,16,256]{2,1,0:T(8,128)(2,1)S(1)}, u32[]{:S(2)}, u32[]{:S(2)}) %collective-permute-start.7) | collective-permute-done | bytes 16416 | tf_op jit(solution)/shard_map/ppermute | solution.py:21
  23.0 0.6 %registers.1 = f32[2,16,256]{2,1,0:T(8,128)} custom-call(f32[2,16,256]{2,1,0:T(8,128)S(1)} %get-tuple-element.68.part_ref, bf16[2,16,256]{2,1,0:T(8,128)(2,1)S(1)} %collective-permute-done.6.three_ref, bf16[2,16,256]{2,1,0:T(8,128)(2,1)S(1)} %collective-permute-done.7.two_ref), custom_call_target="tpu_custom_call" | custom-call | bytes 98304 | tf_op jit(solution)/shard_map/registers/pallas_call | solution.py:371
Async XLA Ops:
  1.8 8.5 %collective-permute-start = (bf16[384,256]{1,0:T(8,128)(2,1)S(1)}, bf16[384,256]{1,0:T(8,128)(2,1)S(1)}, u32[]{:S(2)}, u32[]{:S(2)}) collective-permute-start(bf16[384,256]{1,0:T(8,128)(2,1)S(1)} %get-tuple-element.45), channel_id=1, source_target_pairs={{0,1},{1,0},{2,3},{3,2},{4,8},{5,9},{6,10},{7,11},{8,4},{9,5},{10,... | collective-permute-start | bytes 589832 | tf_op jit(solution)/shard_map/ppermute | solution.py:36
  2.3 9.3 %collective-permute-start.1 = (bf16[416,256]{1,0:T(8,128)(2,1)S(1)}, bf16[416,256]{1,0:T(8,128)(2,1)S(1)}, u32[]{:S(2)}, u32[]{:S(2)}) collective-permute-start(bf16[416,256]{1,0:T(8,128)(2,1)S(1)} %get-tuple-element.49), channel_id=1, source_target_pairs={{0,4},{4,0},{8,12},{12,8},{1,5},{5,1},{9,13},{13,9},{2,6},{6,2},{1... | collective-permute-start | bytes 638984 | tf_op jit(solution)/shard_map/ppermute | solution.py:21
  6.4 6.9 %collective-permute-start.3 = (bf16[2,16,256]{2,1,0:T(8,128)(2,1)S(1)}, bf16[2,16,256]{2,1,0:T(8,128)(2,1)S(1)}, u32[]{:S(2)}, u32[]{:S(2)}) collective-permute-start(bf16[2,16,256]{2,1,0:T(8,128)(2,1)S(1)} %get-tuple-element.53.refs_9_), channel_id=1, source_target_pairs={{0,12},{4,8},{8,4},{12,0},{1,13},{5,9},{9,5},{13,1},{2,14},{6,10},... | collective-permute-start | bytes 49160 | tf_op jit(solution)/shard_map/ppermute | solution.py:21
  7.8 5.6 %collective-permute-start.2 = (bf16[2,16,256]{2,1,0:T(8,128)(2,1)S(1)}, bf16[2,16,256]{2,1,0:T(8,128)(2,1)S(1)}, u32[]{:S(2)}, u32[]{:S(2)}) collective-permute-start(bf16[2,16,256]{2,1,0:T(8,128)(2,1)S(1)} %get-tuple-element.53.refs_9_), channel_id=1, source_target_pairs={{0,8},{4,12},{8,0},{12,4},{1,9},{5,13},{9,1},{13,5},{2,10},{6,14},... | collective-permute-start | bytes 49160 | tf_op jit(solution)/shard_map/ppermute | solution.py:21
  14.5 7.4 %collective-permute-start.4 = (bf16[416,256]{1,0:T(8,128)(2,1)S(1)}, bf16[416,256]{1,0:T(8,128)(2,1)S(1)}, u32[]{:S(2)}, u32[]{:S(2)}) collective-permute-start(bf16[416,256]{1,0:T(8,128)(2,1)S(1)} %get-tuple-element.63), channel_id=1, source_target_pairs={{0,4},{4,0},{8,12},{12,8},{1,5},{5,1},{9,13},{13,9},{2,6},{6,2},{1... | collective-permute-start | bytes 638984 | tf_op jit(solution)/shard_map/ppermute | solution.py:21
  15.4 6.5 %collective-permute-start.5 = (bf16[384,256]{1,0:T(8,128)(2,1)S(1)}, bf16[384,256]{1,0:T(8,128)(2,1)S(1)}, u32[]{:S(2)}, u32[]{:S(2)}) collective-permute-start(bf16[384,256]{1,0:T(8,128)(2,1)S(1)} %get-tuple-element.64), channel_id=1, source_target_pairs={{0,1},{1,0},{2,3},{3,2},{4,8},{5,9},{6,10},{7,11},{8,4},{9,5},{10,... | collective-permute-start | bytes 589832 | tf_op jit(solution)/shard_map/ppermute | solution.py:36
  15.4 7.3 %collective-permute-start.6 = (bf16[2,16,256]{2,1,0:T(8,128)(2,1)S(1)}, bf16[2,16,256]{2,1,0:T(8,128)(2,1)S(1)}, u32[]{:S(2)}, u32[]{:S(2)}) collective-permute-start(bf16[2,16,256]{2,1,0:T(8,128)(2,1)S(1)} %get-tuple-element.69), channel_id=1, source_target_pairs={{0,12},{4,8},{8,4},{12,0},{1,13},{5,9},{9,5},{13,1},{2,14},{6,10},... | collective-permute-start | bytes 49160 | tf_op jit(solution)/shard_map/ppermute | solution.py:21
  17.4 5.6 %collective-permute-start.7 = (bf16[2,16,256]{2,1,0:T(8,128)(2,1)S(1)}, bf16[2,16,256]{2,1,0:T(8,128)(2,1)S(1)}, u32[]{:S(2)}, u32[]{:S(2)}) collective-permute-start(bf16[2,16,256]{2,1,0:T(8,128)(2,1)S(1)} %get-tuple-element.70), channel_id=1, source_target_pairs={{0,8},{4,12},{8,0},{12,4},{1,9},{5,13},{9,1},{13,5},{2,10},{6,14},... | collective-permute-start | bytes 49160 | tf_op jit(solution)/shard_map/ppermute | solution.py:21

commit v11 on v10

--- a/solution.py
+++ b/solution.py
@@ -333,10 +333,6 @@
         dq_ref[lines] = patch_order(dq_cols).astype(BF)
 
 
-def registers_kernel(part_ref, three_ref, two_ref, out_ref):
-    out_ref[...] = part_ref[...] + two_ref[...].astype(F32) + three_ref[...].astype(F32)
-
-
 def finish_kernel(split_regs, dk_ref, dv_ref, a_ref, b_ref, *refs):
     if split_regs:
         own_ref, gk_ref, gv_ref, part_ref = refs
@@ -503,12 +499,8 @@
         0,
     )
     if split_regs:
-        (grad_registers,) = call(
-            registers_kernel,
-            "registers",
-            (part[0], swap(back_regs[2], three), swap(back_regs[1], two)),
-            (shape((2, own, feature), F32),),
-            0,
+        grad_registers = (
+            part[0] + swap(back_regs[2], three).astype(F32) + swap(back_regs[1], two).astype(F32)
         )
     else:
         grad_registers = lax.psum_scatter(back_regs[0], "rows", scatter_dimension=1, tiled=True)

time: 23.8 us -> 23.8 us (level)
  other arithmetic: 0 us -> 0.62 us
  Pallas kernels: 9.42 us -> 8.8 us
    pallas_call x8 -> x7, Pallas kernels: 9.42 us -> 8.8 us  [call(): pl.pallas_call(kernel, out_shape=tuple(outs), in_specs=in_specs or [VMEM]...]
    add x0 -> x1, other arithmetic: none -> 0.62 us  [shards(): part[0] + swap(back_regs[2], three).astype(F32)]
where the time goes in v11:
time: 23.8 us; the launch traced here: 23.6 us
  starting transfers between devices  11 us (46%)
  Pallas kernels  8.8 us (37%)
  waiting for transfers between devices  2.52 us (11%)
  between operations  0.68 us (3%)
  other arithmetic  0.62 us (3%)
    ppermute x6, starting transfers between devices, swap(): return lax.ppermute(array, 'rows', pairs)  10.5 us
    pallas_call x7, Pallas kernels, call(): pl.pallas_call(kernel, out_shape=tuple(outs), in_specs=in_specs or [VMEM]...  8.8 us
    ppermute x6, waiting for transfers between devices, swap(): return lax.ppermute(array, 'rows', pairs)  2.51 us
    add x1, other arithmetic, shards(): part[0] + swap(back_regs[2], three).astype(F32)  0.62 us
    ppermute x2, starting transfers between devices, swap_b(): return lax.ppermute(array, ('rows', 'cols'), pairs)  0.52 us
  transfers between devices with their start and end apart: 8, of which 3 were waited for; matrix products, arithmetic and copies ran while one was open for 0% of the time, Pallas kernels for 28%

profile of v11, /device:TPU:0, one launch (start us, length us, event | category | flops | bytes accessed | tf_op | source)
XLA Modules:
  0.0 23.6 jit_solution(5345023962160350946)
XLA Ops:
  0.6 1.1 %prepare.1 = (bf16[416,256]{1,0:T(8,128)(2,1)S(1)}, bf16[384,256]{1,0:T(8,128)(2,1)S(1)}, bf16[2,16,256]{2,1,0:T(8,128)(2,1)S(1)}) custom-call(bf16[384,256]{1,0:T(8,128)(2,1)} %bitcast.8, bf16[384,256]{1,0:T(8,128)(2,1)} %bitcast.10, bf16[2,16,256]{2,1,0:T(8,128)(2,1)} %reg_ref.1), custom_call_target="tpu_custom_call" | custom-call | bytes 835584 | tf_op jit(solution)/shard_map/prepare/pallas_call | solution.py:367
  1.8 0.5 %collective-permute-start = (bf16[384,256]{1,0:T(8,128)(2,1)S(1)}, bf16[384,256]{1,0:T(8,128)(2,1)S(1)}, u32[]{:S(2)}, u32[]{:S(2)}) collective-permute-start(bf16[384,256]{1,0:T(8,128)(2,1)S(1)} %get-tuple-element.45), channel_id=1, source_target_pairs={{0,1},{1,0},{2,3},{3,2},{4,8},{5,9},{6,10},{7,11},{8,4},{9,5},{10,... | collective-permute-start | bytes 589832 | tf_op jit(solution)/shard_map/ppermute | solution.py:36
  2.3 4.1 %collective-permute-start.1 = (bf16[416,256]{1,0:T(8,128)(2,1)S(1)}, bf16[416,256]{1,0:T(8,128)(2,1)S(1)}, u32[]{:S(2)}, u32[]{:S(2)}) collective-permute-start(bf16[416,256]{1,0:T(8,128)(2,1)S(1)} %get-tuple-element.49), channel_id=1, source_target_pairs={{0,4},{4,0},{8,12},{12,8},{1,5},{5,1},{9,13},{13,9},{2,6},{6,2},{1... | collective-permute-start | bytes 638984 | tf_op jit(solution)/shard_map/ppermute | solution.py:21
  6.4 1.3 %collective-permute-start.3 = (bf16[2,16,256]{2,1,0:T(8,128)(2,1)S(1)}, bf16[2,16,256]{2,1,0:T(8,128)(2,1)S(1)}, u32[]{:S(2)}, u32[]{:S(2)}) collective-permute-start(bf16[2,16,256]{2,1,0:T(8,128)(2,1)S(1)} %get-tuple-element.53.refs_9_), channel_id=1, source_target_pairs={{0,12},{4,8},{8,4},{12,0},{1,13},{5,9},{9,5},{13,1},{2,14},{6,10},... | collective-permute-start | bytes 49160 | tf_op jit(solution)/shard_map/ppermute | solution.py:21
  7.8 0.1 collective-permute-start.2
  7.9 2.3 %own.1 = (bf16[6,256,256]{2,1,0:T(8,128)(2,1)S(1)}, bf16[6,256,256]{2,1,0:T(8,128)(2,1)S(1)}, bf16[256,384]{1,0:T(8,128)(2,1)S(1)}, bf16[256,384]{1,0:T(8,128)(2...) custom-call(bf16[384,256]{1,0:T(8,128)(2,1)} %bitcast.12, ...), custom_call_target="tpu_custom_call" | custom-call | flops 600000000 | bytes 6340608 | tf_op jit(solution)/shard_map/own/pallas_call | solution.py:367
  10.2 0.0 collective-permute-done.halo_ref.from_b_ref
  10.3 0.5 %halo.2 = (f32[3,192,256]{2,1,0:T(8,128)S(1)}, bf16[3,192,256]{2,1,0:T(8,128)(2,1)S(1)}, f32[3,8,256]{2,1,0:T(8,128)S(1)}) custom-call(bf16[6,256,256]{2,1,0:T(8,128)(2,1)S(1)} %get-tuple-element.38.qbd_ref.refs_0_, bf16[6,256,256]{2,1,0:T(8,128)(2,1)S(1)} %get-tuple-element.39.gbd_ref.refs_1_, f32[6,8,256]{2,1,0:T(8,128)S(1)} %get-tuple-element.44.stat_ref, ...), custom_call_target="tpu_custom_call" | custom-call | flops 1207959552 | bytes 2727936 | tf_op jit(solution)/shard_map/halo/pallas_call | solution.py:367
  10.7 0.8 %collective-permute-done.1.halo_ref.refs_8_.from_a_ref = bf16[416,256]{1,0:T(8,128)(2,1)S(1)} collective-permute-done((bf16[416,256]{1,0:T(8,128)(2,1)S(1)}, bf16[416,256]{1,0:T(8,128)(2,1)S(1)}, u32[]{:S(2)}, u32[]{:S(2)}) %collective-permute-start.1) | collective-permute-done | bytes 213024 | tf_op jit(solution)/shard_map/ppermute | solution.py:21
  11.6 0.4 %halo.3 = (f32[3,192,256]{2,1,0:T(8,128)S(1)}, bf16[3,192,256]{2,1,0:T(8,128)(2,1)S(1)}, f32[3,8,256]{2,1,0:T(8,128)S(1)}) custom-call(bf16[6,256,256]{2,1,0:T(8,128)(2,1)S(1)} %get-tuple-element.38.qbd_ref.refs_0_, bf16[6,256,256]{2,1,0:T(8,128)(2,1)S(1)} %get-tuple-element.39.gbd_ref.refs_1_, f32[6,8,256]{2,1,0:T(8,128)S(1)} %get-tuple-element.44.stat_ref, ...), custom_call_target="tpu_custom_call" | custom-call | flops 1207959552 | bytes 2744320 | tf_op jit(solution)/shard_map/halo/pallas_call | solution.py:367
  12.0 1.3 %collective-permute-done.3.refs_11_ = bf16[2,16,256]{2,1,0:T(8,128)(2,1)S(1)} collective-permute-done((bf16[2,16,256]{2,1,0:T(8,128)(2,1)S(1)}, bf16[2,16,256]{2,1,0:T(8,128)(2,1)S(1)}, u32[]{:S(2)}, u32[]{:S(2)}) %collective-permute-start.3) | collective-permute-done | bytes 16416 | tf_op jit(solution)/shard_map/ppermute | solution.py:21
  13.3 0.0 collective-permute-done.2.refs_10_
  13.3 1.1 %far.1 = (f32[6,8,256]{2,1,0:T(8,128)S(1)}, bf16[6,256,256]{2,1,0:T(8,128)(2,1)S(1)}, bf16[6,256,256]{2,1,0:T(8,128)(2,1)S(1)}, bf16[64,256]{1,0:T(8,128)(2,1)S(...) custom-call(bf16[6,256,256]{2,1,0:T(8,128)(2,1)S(1)} %get-tuple-elem, ...), custom_call_target="tpu_custom_call" | custom-call | flops 805306368 | bytes 5816320 | tf_op jit(solution)/shard_map/far/pallas_call | solution.py:367
  14.5 0.9 %collective-permute-start.4 = (bf16[416,256]{1,0:T(8,128)(2,1)S(1)}, bf16[416,256]{1,0:T(8,128)(2,1)S(1)}, u32[]{:S(2)}, u32[]{:S(2)}) collective-permute-start(bf16[416,256]{1,0:T(8,128)(2,1)S(1)} %get-tuple-element.63), channel_id=1, source_target_pairs={{0,4},{4,0},{8,12},{12,8},{1,5},{5,1},{9,13},{13,9},{2,6},{6,2},{1... | collective-permute-start | bytes 638984 | tf_op jit(solution)/shard_map/ppermute | solution.py:21
  15.4 0.0 collective-permute-start.5
  15.4 2.0 %collective-permute-start.6 = (bf16[2,16,256]{2,1,0:T(8,128)(2,1)S(1)}, bf16[2,16,256]{2,1,0:T(8,128)(2,1)S(1)}, u32[]{:S(2)}, u32[]{:S(2)}) collective-permute-start(bf16[2,16,256]{2,1,0:T(8,128)(2,1)S(1)} %get-tuple-element.69), channel_id=1, source_target_pairs={{0,12},{4,8},{8,4},{12,0},{1,13},{5,9},{9,5},{13,1},{2,14},{6,10},... | collective-permute-start | bytes 49160 | tf_op jit(solution)/shard_map/ppermute | solution.py:21
  17.4 1.9 %collective-permute-start.7 = (bf16[2,16,256]{2,1,0:T(8,128)(2,1)S(1)}, bf16[2,16,256]{2,1,0:T(8,128)(2,1)S(1)}, u32[]{:S(2)}, u32[]{:S(2)}) collective-permute-start(bf16[2,16,256]{2,1,0:T(8,128)(2,1)S(1)} %get-tuple-element.70), channel_id=1, source_target_pairs={{0,8},{4,12},{8,0},{12,4},{1,9},{5,13},{9,1},{13,5},{2,10},{6,14},... | collective-permute-start | bytes 49160 | tf_op jit(solution)/shard_map/ppermute | solution.py:21
  19.4 2.5 %rest.1 = (bf16[384,256]{1,0:T(8,128)(2,1)}, bf16[384,256]{1,0:T(8,128)(2,1)}, f32[3,128,256]{2,1,0:T(8,128)S(1)}, f32[3,128,256]{2,1,0:T(8,128)S(1)}) custom-call(bf16[6,256,256]{2,1,0:T(8,128)(2,1)S(1)} %get-tuple-element.38.qbd_ref.refs_0_, bf16[6,256,256]{2,1,0:T(8,128)(2,1)S(1)} %get-tuple-element.39.gbd_ref.refs_1_, ...), custom_call_target="tpu_custom_call" | custom-call | flops 600000000 | bytes 8781824 | tf_op jit(solution)/shard_map/rest/pallas_call | solution.py:367
  21.9 0.0 collective-permute-done.5.b_ref
  21.9 0.0 collective-permute-done.4.a_ref
  21.9 0.8 %finish.1 = (bf16[384,256]{1,0:T(8,128)(2,1)}, bf16[384,256]{1,0:T(8,128)(2,1)}, f32[2,16,256]{2,1,0:T(8,128)S(1)}) custom-call(f32[3,128,256]{2,1,0:T(8,128)S(1)} %get-tuple-element.61.dk_ref, f32[3,128,256]{2,1,0:T(8,128)S(1)} %get-tuple-element.62.dv_ref, bf16[416,256]{1,0:T(8,128)(2,1)S(1)} %collective-permute-done.4.a_ref, ...), custom_call_target="tpu_custom_call" | custom-call | bytes 1654784 | tf_op jit(solution)/shard_map/finish/pallas_call | solution.py:367
  22.7 0.0 collective-permute-done.6
  22.7 0.3 %collective-permute-done.7 = bf16[2,16,256]{2,1,0:T(8,128)(2,1)S(1)} collective-permute-done((bf16[2,16,256]{2,1,0:T(8,128)(2,1)S(1)}, bf16[2,16,256]{2,1,0:T(8,128)(2,1)S(1)}, u32[]{:S(2)}, u32[]{:S(2)}) %collective-permute-start.7) | collective-permute-done | bytes 16416 | tf_op jit(solution)/shard_map/ppermute | solution.py:21
  23.0 0.6 %convert_add_fusion = f32[2,16,256]{2,1,0:T(8,128)} fusion(bf16[2,16,256]{2,1,0:T(8,128)(2,1)S(1)} %collective-permute-done.7, f32[2,16,256]{2,1,0:T(8,128)S(1)} %get-tuple-element.68, bf16[2,16,256]{2,1,0:T(8,128)(2,1)S(1)} %collective-permute-done.6), kind=kLoop, calls=%fused_computation | loop fusion | flops 32768 | bytes 98304 | tf_op jit(solution)/shard_map/add | solution.py:503
Async XLA Ops:
  1.8 8.5 %collective-permute-start = (bf16[384,256]{1,0:T(8,128)(2,1)S(1)}, bf16[384,256]{1,0:T(8,128)(2,1)S(1)}, u32[]{:S(2)}, u32[]{:S(2)}) collective-permute-start(bf16[384,256]{1,0:T(8,128)(2,1)S(1)} %get-tuple-element.45), channel_id=1, source_target_pairs={{0,1},{1,0},{2,3},{3,2},{4,8},{5,9},{6,10},{7,11},{8,4},{9,5},{10,... | collective-permute-start | bytes 589832 | tf_op jit(solution)/shard_map/ppermute | solution.py:36
  2.3 9.3 %collective-permute-start.1 = (bf16[416,256]{1,0:T(8,128)(2,1)S(1)}, bf16[416,256]{1,0:T(8,128)(2,1)S(1)}, u32[]{:S(2)}, u32[]{:S(2)}) collective-permute-start(bf16[416,256]{1,0:T(8,128)(2,1)S(1)} %get-tuple-element.49), channel_id=1, source_target_pairs={{0,4},{4,0},{8,12},{12,8},{1,5},{5,1},{9,13},{13,9},{2,6},{6,2},{1... | collective-permute-start | bytes 638984 | tf_op jit(solution)/shard_map/ppermute | solution.py:21
  6.4 6.9 %collective-permute-start.3 = (bf16[2,16,256]{2,1,0:T(8,128)(2,1)S(1)}, bf16[2,16,256]{2,1,0:T(8,128)(2,1)S(1)}, u32[]{:S(2)}, u32[]{:S(2)}) collective-permute-start(bf16[2,16,256]{2,1,0:T(8,128)(2,1)S(1)} %get-tuple-element.53.refs_9_), channel_id=1, source_target_pairs={{0,12},{4,8},{8,4},{12,0},{1,13},{5,9},{9,5},{13,1},{2,14},{6,10},... | collective-permute-start | bytes 49160 | tf_op jit(solution)/shard_map/ppermute | solution.py:21
  7.8 5.6 %collective-permute-start.2 = (bf16[2,16,256]{2,1,0:T(8,128)(2,1)S(1)}, bf16[2,16,256]{2,1,0:T(8,128)(2,1)S(1)}, u32[]{:S(2)}, u32[]{:S(2)}) collective-permute-start(bf16[2,16,256]{2,1,0:T(8,128)(2,1)S(1)} %get-tuple-element.53.refs_9_), channel_id=1, source_target_pairs={{0,8},{4,12},{8,0},{12,4},{1,9},{5,13},{9,1},{13,5},{2,10},{6,14},... | collective-permute-start | bytes 49160 | tf_op jit(solution)/shard_map/ppermute | solution.py:21
  14.5 7.4 %collective-permute-start.4 = (bf16[416,256]{1,0:T(8,128)(2,1)S(1)}, bf16[416,256]{1,0:T(8,128)(2,1)S(1)}, u32[]{:S(2)}, u32[]{:S(2)}) collective-permute-start(bf16[416,256]{1,0:T(8,128)(2,1)S(1)} %get-tuple-element.63), channel_id=1, source_target_pairs={{0,4},{4,0},{8,12},{12,8},{1,5},{5,1},{9,13},{13,9},{2,6},{6,2},{1... | collective-permute-start | bytes 638984 | tf_op jit(solution)/shard_map/ppermute | solution.py:21
  15.4 6.5 %collective-permute-start.5 = (bf16[384,256]{1,0:T(8,128)(2,1)S(1)}, bf16[384,256]{1,0:T(8,128)(2,1)S(1)}, u32[]{:S(2)}, u32[]{:S(2)}) collective-permute-start(bf16[384,256]{1,0:T(8,128)(2,1)S(1)} %get-tuple-element.64), channel_id=1, source_target_pairs={{0,1},{1,0},{2,3},{3,2},{4,8},{5,9},{6,10},{7,11},{8,4},{9,5},{10,... | collective-permute-start | bytes 589832 | tf_op jit(solution)/shard_map/ppermute | solution.py:36
  15.4 7.3 %collective-permute-start.6 = (bf16[2,16,256]{2,1,0:T(8,128)(2,1)S(1)}, bf16[2,16,256]{2,1,0:T(8,128)(2,1)S(1)}, u32[]{:S(2)}, u32[]{:S(2)}) collective-permute-start(bf16[2,16,256]{2,1,0:T(8,128)(2,1)S(1)} %get-tuple-element.69), channel_id=1, source_target_pairs={{0,12},{4,8},{8,4},{12,0},{1,13},{5,9},{9,5},{13,1},{2,14},{6,10},... | collective-permute-start | bytes 49160 | tf_op jit(solution)/shard_map/ppermute | solution.py:21
  17.4 5.6 %collective-permute-start.7 = (bf16[2,16,256]{2,1,0:T(8,128)(2,1)S(1)}, bf16[2,16,256]{2,1,0:T(8,128)(2,1)S(1)}, u32[]{:S(2)}, u32[]{:S(2)}) collective-permute-start(bf16[2,16,256]{2,1,0:T(8,128)(2,1)S(1)} %get-tuple-element.70), channel_id=1, source_target_pairs={{0,8},{4,12},{8,0},{12,4},{1,9},{5,13},{9,1},{13,5},{2,10},{6,14},... | collective-permute-start | bytes 49160 | tf_op jit(solution)/shard_map/ppermute | solution.py:21
